TPU v7x, 32 devices: a whole 2x2x4 slice. The times are simulated.
32 devices in a mesh: expert: 8 (over y, x, core), dp: 4 (over z).
Axes of the slice: x: 2, y: 2, z: 4, core: 2. Of those that a mesh axis runs over, the one named last changes fastest.
Arguments:
- tokens: bfloat16 [4096, 2048], P(('expert', 'dp')), may hold values from -6 to 6
- cotangent: bfloat16 [4096, 2048], P(('expert', 'dp')), may hold values from -6 to 6
- gate_weights: float32 [4096, 8], P(('expert', 'dp')), may hold values from 0.02 to 0.5
- expert_ids: int32 [4096, 8], P(('expert', 'dp')), may hold values from 0 to 15, as said below
- copy_pick: int32 [4096, 8], P(('expert', 'dp')), may hold values from 0 to 1, as said below
- copy_expert: int32 [8], replicated, may hold values from 0 to 15, as said below
- up_weight: bfloat16 [16, 2048, 384], P('expert'), may hold values from -0.125 to 0.125
- down_weight: bfloat16 [16, 384, 2048], P('expert'), may hold values from -0.3125 to 0.3125
- copy_up: bfloat16 [8, 2048, 384], P('expert'), may hold values from -0.125 to 0.125
- copy_down: bfloat16 [8, 384, 2048], P('expert'), may hold values from -0.3125 to 0.3125
Outputs:
- layer_output: bfloat16 [4096, 2048], P(('expert', 'dp'))
- token_grad: bfloat16 [4096, 2048], P(('expert', 'dp'))
- gate_grad: float32 [4096, 8], P(('expert', 'dp'))
- up_grad: bfloat16 [16, 2048, 384], P('expert', 'dp')
- down_grad: bfloat16 [16, 384, 2048], P('expert', None, 'dp')
Inputs may be any that keep to these rules, and one draw needn't show every extreme that they name: `expert_ids`: each row names 8 different experts. In the 128 rows of one device, the 2 experts of any one device are named 8 * 128 // 8 times together; the one of them that copy_expert lists is named at most 64 + 32 times and the other at most 64 - 32 + 32 // 2 times, and both bounds are reached in every block of rows. `copy_pick`: A 1 stands only where the pair's expert is listed in copy_expert. From the rows of one device at most 24 pairs go to one copy and at most 152 pairs go to one device (its own experts and its copy together). In each group of devices that share an index along dp, some device receives exactly 152 pairs from every device of the group, and the copy before it exactly 24 from each. `copy_expert`: entry c is one of the experts of device c - 1 along the expert axis (of the last device for entry 0); device o holds the experts 2 * o to 2 * o + 1.
All inputs are finite; a program needn't handle non-finite values.
Results may differ from a plain program's by a relative error of at most 0.014.
Values may be sent and summed in bfloat16 or wider, within the bound.
No kernel may reach another device: no remote copies, remote signals or barrier semaphores. Data moves between devices by JAX's collectives and lax.ppermute only.
A program may use at most 128 MiB of HBM per device.

v0:
```python
import jax
import jax.numpy as jnp
from jax import lax
from jax.sharding import PartitionSpec as P


def from_behind(block, axis, distance):
    devices = range(lax.axis_size(axis))
    route = [((i - distance) % len(devices), i) for i in devices]
    return lax.ppermute(block, axis, route)


def silu_slope(values):
    sigma_values = jax.nn.sigmoid(values)
    return sigma_values * (1.0 + values * (1.0 - sigma_values))


def local(
    tokens,
    cotangent,
    gate_weights,
    expert_ids,
    copy_pick,
    copy_expert,
    up_weight,
    down_weight,
    copy_up,
    copy_down,
):
    device_count = lax.axis_size("expert")
    my_index = lax.axis_index("expert")
    token_rows, feature_width = tokens.shape
    chosen = expert_ids.shape[1]
    local_count = up_weight.shape[0]
    pair_count = token_rows * chosen
    mean_rows = pair_count // (local_count * device_count)
    extra_rows = mean_rows // 2
    moved_most = 3 * mean_rows // 8
    capacity = local_count * mean_rows + moved_most
    buffer_rows = device_count * capacity
    region_sizes = [
        device_count * (mean_rows + extra_rows),
        device_count * (mean_rows - extra_rows + extra_rows // 2),
        device_count * moved_most,
    ]
    region_starts = [0, region_sizes[0], region_sizes[0] + region_sizes[1]]
    region_total = region_starts[2] + region_sizes[2]
    flat_ids = expert_ids.reshape(pair_count)
    flat_picks = copy_pick.reshape(pair_count)
    flat_gates = gate_weights.reshape(pair_count)
    owner_device = flat_ids // local_count
    target_device = (owner_device + flat_picks) % device_count
    slot_index = jnp.where(flat_picks == 1, local_count, flat_ids % local_count)
    device_hit = (
        target_device[:, None] == jnp.arange(device_count, dtype=jnp.int32)[None, :]
    ).astype(jnp.int32)
    rank_index = jnp.sum((jnp.cumsum(device_hit, axis=0) - device_hit) * device_hit, axis=1)
    placement = target_device * capacity + rank_index
    source_pair = (
        jnp.full((buffer_rows,), pair_count, jnp.int32)
        .at[placement]
        .set(jnp.arange(pair_count, dtype=jnp.int32))
    )
    filled = source_pair < pair_count
    safe_pair = jnp.minimum(source_pair, pair_count - 1)
    safe_token = safe_pair // chosen
    send_rows = jnp.where(filled[:, None], tokens[safe_token], jnp.zeros((), jnp.bfloat16)).reshape(
        device_count, capacity, feature_width
    )
    send_slots = jnp.where(filled, slot_index[safe_pair], local_count + 1).reshape(
        device_count, capacity
    )
    scaled = (flat_gates[safe_pair][:, None] * cotangent[safe_token].astype(jnp.float32)).astype(
        jnp.bfloat16
    )
    send_scaled = jnp.where(filled[:, None], scaled, jnp.zeros((), jnp.bfloat16)).reshape(
        device_count, capacity, feature_width
    )
    hot_slot = copy_expert[(my_index + 1) % device_count] % local_count
    cold_slot = local_count - 1 - hot_slot
    region_up = [up_weight[hot_slot], up_weight[cold_slot], copy_up[0]]
    region_down = [down_weight[hot_slot], down_weight[cold_slot], copy_down[0]]

    def sorted_rows_of(arrived, source_row):
        present = source_row < buffer_rows
        flat = arrived.reshape(buffer_rows, feature_width)
        return jnp.where(
            present[:, None],
            flat[jnp.minimum(source_row, buffer_rows - 1)],
            jnp.zeros((), jnp.bfloat16),
        )

    def to_buffer(region_values, position, valid):
        picked = region_values[jnp.minimum(position, region_total - 1)]
        return jnp.where(valid[:, None], picked, jnp.zeros((), jnp.bfloat16)).reshape(
            device_count, capacity, feature_width
        )

    arrived_rows, arrived_slots = (
        lax.all_to_all(send_rows, "expert", split_axis=0, concat_axis=0, tiled=True),
        lax.all_to_all(send_slots, "expert", split_axis=0, concat_axis=0, tiled=True),
    )
    slots = arrived_slots.reshape(buffer_rows)
    kind = jnp.where(
        slots == hot_slot,
        0,
        jnp.where(slots < local_count, 1, jnp.where(slots == local_count, 2, 3)),
    )
    kind_hit = (kind[:, None] == jnp.arange(3, dtype=jnp.int32)[None, :]).astype(jnp.int32)
    rank_in = jnp.sum((jnp.cumsum(kind_hit, axis=0) - kind_hit) * kind_hit, axis=1)
    valid = kind < 3
    start_table = jnp.array(region_starts, jnp.int32)
    position = jnp.where(valid, start_table[jnp.minimum(kind, 2)] + rank_in, region_total)
    source_row = (
        jnp.full((region_total,), buffer_rows, jnp.int32)
        .at[position]
        .set(jnp.arange(buffer_rows, dtype=jnp.int32), mode="drop")
    )
    sorted_rows = sorted_rows_of(arrived_rows, source_row)
    saved = []
    pieces = []
    for region in range(3):
        rows = sorted_rows[region_starts[region] : region_starts[region] + region_sizes[region]]
        linear_part = jnp.dot(rows, region_up[region], preferred_element_type=jnp.float32)
        active = jax.nn.silu(linear_part).astype(jnp.bfloat16)
        pieces.append(
            jnp.dot(active, region_down[region], preferred_element_type=jnp.float32).astype(
                jnp.bfloat16
            )
        )
        saved.append((rows, linear_part, active))
    outputs = jnp.concatenate(pieces, axis=0)
    position, valid, source_row, saved, outputs = (position, valid, source_row, saved, outputs)
    returned = lax.all_to_all(
        to_buffer(outputs, position, valid), "expert", split_axis=0, concat_axis=0, tiled=True
    )
    arrived_scaled = lax.all_to_all(send_scaled, "expert", split_axis=0, concat_axis=0, tiled=True)
    sorted_scaled = sorted_rows_of(arrived_scaled, source_row)
    pieces = []
    up_parts = []
    down_parts = []
    for region in range(3):
        rows, linear_part, active = saved[region]
        region_scaled = sorted_scaled[
            region_starts[region] : region_starts[region] + region_sizes[region]
        ]
        active_grad = jnp.dot(
            region_scaled, region_down[region].T, preferred_element_type=jnp.float32
        )
        linear_grad = (active_grad * silu_slope(linear_part)).astype(jnp.bfloat16)
        pieces.append(
            jnp.dot(linear_grad, region_up[region].T, preferred_element_type=jnp.float32).astype(
                jnp.bfloat16
            )
        )
        up_parts.append(jnp.dot(rows.T, linear_grad, preferred_element_type=jnp.float32))
        down_parts.append(jnp.dot(active.T, region_scaled, preferred_element_type=jnp.float32))
    pair_grad, up_parts, down_parts = (jnp.concatenate(pieces, axis=0), up_parts, down_parts)
    grad_back = lax.all_to_all(
        to_buffer(pair_grad, position, valid), "expert", split_axis=0, concat_axis=0, tiled=True
    )
    pair_out = returned.reshape(buffer_rows, feature_width)[placement].reshape(
        token_rows, chosen, feature_width
    )
    mixed_rows = jnp.sum(gate_weights[:, :, None] * pair_out.astype(jnp.float32), axis=1).astype(
        jnp.bfloat16
    )
    gate_grad = jnp.einsum("tkw,tw->tk", pair_out, cotangent, preferred_element_type=jnp.float32)
    pair_back = grad_back.reshape(buffer_rows, feature_width)[placement].reshape(
        token_rows, chosen, feature_width
    )
    token_grad = jnp.sum(pair_back.astype(jnp.float32), axis=1).astype(jnp.bfloat16)
    first_hot = hot_slot == 0
    own_up = jnp.stack(
        [
            jnp.where(first_hot, up_parts[0], up_parts[1]),
            jnp.where(first_hot, up_parts[1], up_parts[0]),
        ]
    )
    own_down = jnp.stack(
        [
            jnp.where(first_hot, down_parts[0], down_parts[1]),
            jnp.where(first_hot, down_parts[1], down_parts[0]),
        ]
    )
    copy_slot = copy_expert[(my_index + 1) % device_count] % local_count
    slot_mask = (jnp.arange(local_count, dtype=jnp.int32) == copy_slot).astype(jnp.float32)
    up_sum, down_sum, copy_up_sum, copy_down_sum = (
        lax.psum_scatter(own_up.astype(jnp.bfloat16), "dp", scatter_dimension=1, tiled=True).astype(
            jnp.float32
        ),
        lax.psum_scatter(
            own_down.astype(jnp.bfloat16), "dp", scatter_dimension=2, tiled=True
        ).astype(jnp.float32),
        lax.psum_scatter(
            up_parts[2].astype(jnp.bfloat16), "dp", scatter_dimension=0, tiled=True
        ).astype(jnp.float32),
        lax.psum_scatter(
            down_parts[2].astype(jnp.bfloat16), "dp", scatter_dimension=1, tiled=True
        ).astype(jnp.float32),
    )
    extra_up, extra_down = (
        from_behind(copy_up_sum.astype(jnp.bfloat16), "expert", -1).astype(copy_up_sum.dtype),
        from_behind(copy_down_sum.astype(jnp.bfloat16), "expert", -1).astype(copy_down_sum.dtype),
    )
    up_grad = (up_sum + slot_mask[:, None, None] * extra_up[None]).astype(jnp.bfloat16)
    down_grad = (down_sum + slot_mask[:, None, None] * extra_down[None]).astype(jnp.bfloat16)
    return (mixed_rows, token_grad, gate_grad, up_grad, down_grad)


def solution(mesh):
    placed = (
        P(("expert", "dp"), None),
        P(("expert", "dp"), None),
        P(("expert", "dp"), None),
        P(("expert", "dp"), None),
        P(("expert", "dp"), None),
        P(),
        P("expert", None, None),
        P("expert", None, None),
        P("expert", None, None),
        P("expert", None, None),
    )
    return jax.shard_map(
        local,
        mesh=mesh,
        in_specs=placed,
        out_specs=(
            P(("expert", "dp"), None),
            P(("expert", "dp"), None),
            P(("expert", "dp"), None),
            P("expert", "dp", None),
            P("expert", None, "dp"),
        ),
        check_vma=False,
    )
```

profile of v0, /device:TPU:1, one launch (start us, length us, event | category | flops | bytes accessed | tf_op | source)
XLA Modules:
  0.0 497.3 jit_solution(3023715269262635039)
XLA Ops:
  22.8 5.2 %all-to-all-start = ((s32[8,1,152]{2,1,0:T(1,128)}), s32[8,1,152]{2,1,0:T(1,128)S(1)}, u32[]{:S(2)}, u32[]{:S(2)}) async-start(s32[8,1,152]{2,1,0:T(1,128)} %all_to_all.18), calls=%async_computation | async-start | bytes 16384 | tf_op jit(solution)/shard_map/all_to_all | solution.py:101
  33.3 11.9 %gather_fusion.6 = bf16[1216,2048]{1,0:T(8,128)(2,1)} fusion(bf16[128,2048]{1,0:T(8,128)(2,1)} %param.12, s32[2048]{0:T(1024)S(1)} %pad_clamp_fusion.2), kind=kCustom, calls=%fused_computation.6 | custom fusion | bytes 9966336 | tf_op jit(solution)/shard_map/gather | solution.py:73
  45.1 11.9 %gather_fusion.1 = bf16[1216,2048]{1,0:T(8,128)(2,1)} fusion(bf16[128,2048]{1,0:T(8,128)(2,1)} %param.11, s32[2048]{0:T(1024)S(1)} %pad_clamp_fusion.2), kind=kCustom, calls=%fused_computation.1 | custom fusion | bytes 9966336 | tf_op jit(solution)/shard_map/gather | solution.py:67
  57.0 8.3 %fusion.1 = (bf16[8,152,2048]{2,1,0:T(8,128)(2,1)}, bf16[8,152,2048]{2,1,0:T(8,128)(2,1)}) fusion(bf16[8,152,2048]{2,1,0:T(8,128)(2,1)} %bitcast.118, f32[8,152]{1,0:T(8,128)S(1)} %mul.112, pred[8,152]{1,0:T(8,128)(4,1)S(1)} %broadcast_in_dim.119, bf16[8,152,2048]{2,1,0:T(8,128)(2,1)} %bitcast.119), kind=kLoop, calls=%fused_computation.19 | loop fusion | flops 12451840 | bytes 19929024 | tf_op jit(solution)/shard_map/jit(_where)/select_n | solution.py:76
  65.3 60.7 %all_to_all.29 = bf16[8,152,2048]{2,1,0:T(8,128)(2,1)} all-to-all(bf16[8,152,2048]{2,1,0:T(8,128)(2,1)} %get-tuple-element.23), channel_id=1, replica_groups=mesh['expert'=8,'dp'=4] {'expert'}, dimensions={0} | all-to-all | bytes 9961472 | tf_op jit(solution)/shard_map/all_to_all | solution.py:100
  126.0 6.0 %all-to-all-start.3 = ((bf16[8,152,2048]{2,1,0:T(8,128)(2,1)}), bf16[8,152,2048]{2,1,0:T(8,128)(2,1)}, u32[]{:S(2)}, u32[]{:S(2)}) async-start(bf16[8,152,2048]{2,1,0:T(8,128)(2,1)} %get-tuple-element.22), calls=%async_computation.3 | async-start | bytes 9961472 | tf_op jit(solution)/shard_map/all_to_all | solution.py:137
  136.4 6.6 %scatter_custom_fusion.1 = s32[1344]{0:T(1024)S(1)} fusion(s32[1216]{0:T(1024)S(1)} %get-tuple-element.6, s32[1216]{0:T(1024)S(1)} %iota.25, s32[]{:T(128)} %constant.110.clone.1), kind=kCustom, calls=%fused_computation.173 | custom fusion | bytes 5380 | tf_op jit(solution)/shard_map/scatter | solution.py:117
  143.1 15.5 %gather_fusion.2 = bf16[1344,2048]{1,0:T(8,128)(2,1)} fusion(bf16[1216,2048]{1,0:T(8,128)(2,1)} %bitcast.115, s32[2048]{0:T(1024)S(1)} %pad_clamp_fusion.1), kind=kCustom, calls=%fused_computation.2 | custom fusion | bytes 11015424 | tf_op jit(solution)/shard_map/gather | solution.py:89
  158.6 27.5 %all-to-all-done.3 = bf16[8,152,2048]{2,1,0:T(8,128)(2,1)} async-done(((bf16[8,152,2048]{2,1,0:T(8,128)(2,1)}), bf16[8,152,2048]{2,1,0:T(8,128)(2,1)}, u32[]{:S(2)}, u32[]{:S(2)}) %all-to-all-start.3) | async-done | bytes 4980768 | tf_op jit(solution)/shard_map/all_to_all | solution.py:137
  186.0 15.5 %gather_fusion.7 = bf16[1344,2048]{1,0:T(8,128)(2,1)} fusion(bf16[1216,2048]{1,0:T(8,128)(2,1)} %bitcast.18, s32[2048]{0:T(1024)S(1)} %pad_clamp_fusion.1), kind=kCustom, calls=%fused_computation.7 | custom fusion | bytes 11015424 | tf_op jit(solution)/shard_map/gather | solution.py:89
  201.5 5.3 %broadcast_select_fusion = (bf16[1344,2048]{1,0:T(8,128)(2,1)S(1)}, bf16[1344,2048]{1,0:T(8,128)(2,1)S(1)}) fusion(bf16[1344,2048]{1,0:T(8,128)(2,1)} %gather_fusion.7, pred[1344]{0:T(1024)(128)(4,1)S(1)} %broadcast_compare_fusion, bf16[1344,2048]{1,0:T(8,128)(2,1)} %gather_fusion.2), kind=kLoop, calls=%fused_computation.17 | loop fusion | flops 5505024 | bytes 22021440 | tf_op jit(solution)/shard_map/jit(_where)/select_n | solution.py:87
  249.0 7.7 %pad_maximum_fusion = bf16[1344,2048]{1,0:T(8,128)(2,1)} fusion(bf16[192,2048]{1,0:T(8,128)(2,1)} %convolution_convert_fusion.7, bf16[384,2048]{1,0:T(8,128)(2,1)} %convolution_convert_fusion.3, bf16[768,2048]{1,0:T(8,128)(2,1)S(1)} %copy-done.6), kind=kLoop, calls=%fused_computation.15 | loop fusion | flops 16515072 | bytes 11010048 | tf_op jit(solution)/shard_map/concatenate | solution.py:132
  256.7 14.4 %gather_fusion.3 = bf16[1216,2048]{1,0:T(8,128)(2,1)} fusion(bf16[1344,2048]{1,0:T(8,128)(2,1)} %pad_maximum_fusion, s32[2048]{0:T(1024)S(1)} %pad_clamp_fusion), kind=kCustom, calls=%fused_computation.3 | custom fusion | bytes 9966336 | tf_op jit(solution)/shard_map/gather | solution.py:94
  276.3 9.6 %pad_maximum_fusion.1 = bf16[1344,2048]{1,0:T(8,128)(2,1)} fusion(bf16[192,2048]{1,0:T(8,128)(2,1)S(1)} %convolution_convert_fusion.6, bf16[384,2048]{1,0:T(8,128)(2,1)S(1)} %convolution_convert_fusion.2, bf16[768,2048]{1,0:T(8,128)(2,1)S(1)} %convolution_convert_fusion), kind=kLoop, calls=%fused_computation.16 | loop fusion | flops 16515072 | bytes 11010048 | tf_op jit(solution)/shard_map/concatenate | solution.py:158
  285.9 14.3 %gather_fusion.8 = bf16[1216,2048]{1,0:T(8,128)(2,1)} fusion(bf16[1344,2048]{1,0:T(8,128)(2,1)} %pad_maximum_fusion.1, s32[2048]{0:T(1024)S(1)} %pad_clamp_fusion), kind=kCustom, calls=%fused_computation.8 | custom fusion | bytes 9966336 | tf_op jit(solution)/shard_map/gather | solution.py:94
  300.2 8.6 %broadcast_select_fusion.3 = (bf16[8,152,2048]{2,1,0:T(8,128)(2,1)}, bf16[8,152,2048]{2,1,0:T(8,128)(2,1)}) fusion(bf16[8,152,2048]{2,1,0:T(8,128)(2,1)} %bitcast.117, pred[8,152]{1,0:T(8,128)(4,1)S(1)} %fusion.121, bf16[8,152,2048]{2,1,0:T(8,128)(2,1)} %bitcast.116), kind=kLoop, calls=%fused_computation.21 | loop fusion | flops 4980736 | bytes 19924160 | tf_op jit(solution)/shard_map/jit(_where)/select_n | solution.py:95
  308.8 7.9 %all-to-all-start.4 = ((bf16[8,152,2048]{2,1,0:T(8,128)(2,1)}), bf16[8,152,2048]{2,1,0:T(8,128)(2,1)}, u32[]{:S(2)}, u32[]{:S(2)}) async-start(bf16[8,152,2048]{2,1,0:T(8,128)(2,1)} %get-tuple-element.18), calls=%async_computation.4 | async-start | bytes 9961472 | tf_op jit(solution)/shard_map/all_to_all | solution.py:159
  324.6 46.1 %all-to-all-done.4 = bf16[8,152,2048]{2,1,0:T(8,128)(2,1)} async-done(((bf16[8,152,2048]{2,1,0:T(8,128)(2,1)}), bf16[8,152,2048]{2,1,0:T(8,128)(2,1)}, u32[]{:S(2)}, u32[]{:S(2)}) %all-to-all-start.4) | async-done | bytes 4980768 | tf_op jit(solution)/shard_map/all_to_all | solution.py:159
  370.8 8.3 %all-to-all-start.2 = ((bf16[8,152,2048]{2,1,0:T(8,128)(2,1)}), bf16[8,152,2048]{2,1,0:T(8,128)(2,1)}, u32[]{:S(2)}, u32[]{:S(2)}) async-start(bf16[8,152,2048]{2,1,0:T(8,128)(2,1)} %get-tuple-element.19), calls=%async_computation.2 | async-start | bytes 9961472 | tf_op jit(solution)/shard_map/all_to_all | solution.py:134
  381.8 57.4 %collective-permute-done.1 = bf16[384,512]{1,0:T(8,128)(2,1)S(1)} collective-permute-done((bf16[384,512]{1,0:T(8,128)(2,1)}, bf16[384,512]{1,0:T(8,128)(2,1)S(1)}, u32[]{:S(2)}, u32[]{:S(2)}) %collective-permute-start.1) | collective-permute-done | bytes 393248 | tf_op jit(solution)/shard_map/ppermute | solution.py:10
  444.3 11.9 %gather_fusion.9 = bf16[1024,2048]{1,0:T(8,128)(2,1)} fusion(bf16[1216,2048]{1,0:T(8,128)(2,1)} %bitcast.20, s32[1024]{0:T(1024)S(1)} %broadcast_clamp_fusion), kind=kCustom, calls=%fused_computation.9 | custom fusion | bytes 8392704 | tf_op jit(solution)/shard_map/gather | solution.py:169
  456.2 12.2 %gather_fusion.4 = bf16[1024,2048]{1,0:T(8,128)(2,1)} fusion(bf16[1216,2048]{1,0:T(8,128)(2,1)} %bitcast.15, s32[1024]{0:T(1024)S(1)} %broadcast_clamp_fusion), kind=kCustom, calls=%fused_computation.4 | custom fusion | bytes 8392704 | tf_op jit(solution)/shard_map/gather | solution.py:162
  474.1 6.0 %bitcast_reduce_fusion = bf16[128,2048]{1,0:T(8,128)(2,1)} fusion(bf16[1024,2048]{1,0:T(8,128)(2,1)} %gather_fusion.9), kind=kLoop, calls=%fused_computation.23 | loop fusion | flops 1835008 | bytes 4718592 | tf_op jit(solution)/shard_map/reduce_sum | solution.py:172
  480.1 5.2 %multiply_reduce_fusion = bf16[128,2048]{1,0:T(8,128)(2,1)} fusion(bf16[1024,2048]{1,0:T(8,128)(2,1)S(1)} %copy-done.3, f32[128,8]{1,0:T(8,128)S(1)} %copy-done.12), kind=kLoop, calls=%fused_computation.14 | loop fusion | flops 6029312 | bytes 4722688 | tf_op jit(solution)/shard_map/reduce_sum | solution.py:165
  (162 shorter events, 96.5 us)
Async XLA Ops:
  7.2 218.5 %copy-start = (bf16[2,384,2048]{2,1,0:T(8,128)(2,1)S(1)}, bf16[2,384,2048]{2,1,0:T(8,128)(2,1)}, u32[]{:S(2)}) copy-start(bf16[2,384,2048]{2,1,0:T(8,128)(2,1)} %param.18) | copy-start | bytes 9437188
  17.3 10.8 %copy-start.17 = (f32[128,8]{0,1:T(8,128)S(1)}, f32[128,8]{0,1:T(8,128)}, u32[]{:S(2)}) copy-start(f32[128,8]{0,1:T(8,128)} %param.13) | copy-start | bytes 12292
  22.8 42.5 %all-to-all-start = ((s32[8,1,152]{2,1,0:T(1,128)}), s32[8,1,152]{2,1,0:T(1,128)S(1)}, u32[]{:S(2)}, u32[]{:S(2)}) async-start(s32[8,1,152]{2,1,0:T(1,128)} %all_to_all.18), calls=%async_computation | async-start | bytes 16384 | tf_op jit(solution)/shard_map/all_to_all | solution.py:101
  126.0 6.0 %copy-start.19 = (s32[8]{0:T(128)S(1)}, s32[8]{0:T(128)}, u32[]{:S(2)}) copy-start(s32[8]{0:T(128)} %param.16) | copy-start | bytes 100
  126.0 60.0 %all-to-all-start.3 = ((bf16[8,152,2048]{2,1,0:T(8,128)(2,1)}), bf16[8,152,2048]{2,1,0:T(8,128)(2,1)}, u32[]{:S(2)}, u32[]{:S(2)}) async-start(bf16[8,152,2048]{2,1,0:T(8,128)(2,1)} %get-tuple-element.22), calls=%async_computation.3 | async-start | bytes 9961472 | tf_op jit(solution)/shard_map/all_to_all | solution.py:137
  132.0 247.0 %reduce-scatter.11.cloned.1.call-start = ((), (), s32[]{:S(2)}) async-start(), calls=%async_computation.12 | async-start | bytes 1966080 | tf_op jit(solution)/shard_map/reduce_scatter | solution.py:198
  201.5 7.8 %copy-start.7 = (bf16[1,2048,384]{2,1,0:T(8,128)(2,1)S(1)}, bf16[1,2048,384]{2,1,0:T(8,128)(2,1)}, u32[]{:S(2)}) copy-start(bf16[1,2048,384]{2,1,0:T(8,128)(2,1)} %param.19) | copy-start | bytes 4718596
  212.8 166.4 %reduce-scatter.7.cloned.1.call-start = ((), (), s32[]{:S(2)}) async-start(), calls=%async_computation.10 | async-start | bytes 1966080 | tf_op jit(solution)/shard_map/reduce_scatter | solution.py:195
  216.7 5.6 %copy-start.21 = (f32[192,384]{1,0:T(8,128)S(1)}, f32[192,384]{1,0:T(8,128)}, u32[]{:S(2)}) copy-start(f32[192,384]{1,0:T(8,128)} %copy-done.20) | copy-start | bytes 884740
  225.2 260.0 %reduce-scatter.5.cloned.1.call-start = ((), (), s32[]{:S(2)}) async-start(), calls=%async_computation.9 | async-start | bytes 3932160 | tf_op jit(solution)/shard_map/reduce_scatter | solution.py:189
  225.7 6.1 %slice-start.2 = ((s8[5505024]{0:T(1024)(128)(4,1)}), s8[4194304]{0:T(1024)(128)(4,1)S(1)}, s32[]{:S(2)}) async-start(s8[5505024]{0:T(1024)(128)(4,1)} %bitcast.122), calls=%async_computation.15 | async-start | bytes 8388608
  225.7 8.4 %slice-start = ((s8[5505024]{0:T(1024)(128)(4,1)}), s8[4194304]{0:T(1024)(128)(4,1)S(1)}, s32[]{:S(2)}) async-start(s8[5505024]{0:T(1024)(128)(4,1)} %bitcast.120), calls=%async_computation.13 | async-start | bytes 8388608
  256.7 17.0 %copy-start.14 = (bf16[192,384]{1,0:T(8,128)(2,1)S(1)}, bf16[192,384]{1,0:T(8,128)(2,1)}, u32[]{:S(2)}) copy-start(bf16[192,384]{1,0:T(8,128)(2,1)} %copy-done.13) | copy-start | bytes 442372
  308.8 7.9 %copy-start.26 = (f32[768,384]{1,0:T(8,128)S(1)}, f32[768,384]{1,0:T(8,128)}, u32[]{:S(2)}) copy-start(f32[768,384]{1,0:T(8,128)} %copy-done.25) | copy-start | bytes 3538948
  308.8 61.9 %all-to-all-start.4 = ((bf16[8,152,2048]{2,1,0:T(8,128)(2,1)}), bf16[8,152,2048]{2,1,0:T(8,128)(2,1)}, u32[]{:S(2)}, u32[]{:S(2)}) async-start(bf16[8,152,2048]{2,1,0:T(8,128)(2,1)} %get-tuple-element.18), calls=%async_computation.4 | async-start | bytes 9961472 | tf_op jit(solution)/shard_map/all_to_all | solution.py:159
  316.7 171.1 %reduce-scatter.9.cloned.1.call-start = ((), (), s32[]{:S(2)}) async-start(), calls=%async_computation.11 | async-start | bytes 3932160 | tf_op jit(solution)/shard_map/reduce_scatter | solution.py:192
  370.8 11.0 %copy-start.16 = (s32[1024,1]{0,1:T(1,128)S(1)}, s32[1024,1]{0,1:T(1,128)}, u32[]{:S(2)}) copy-start(s32[1024,1]{0,1:T(1,128)} %copy-done.15) | copy-start | bytes 12292
  370.8 85.5 %all-to-all-start.2 = ((bf16[8,152,2048]{2,1,0:T(8,128)(2,1)}), bf16[8,152,2048]{2,1,0:T(8,128)(2,1)}, u32[]{:S(2)}, u32[]{:S(2)}) async-start(bf16[8,152,2048]{2,1,0:T(8,128)(2,1)} %get-tuple-element.19), calls=%async_computation.2 | async-start | bytes 9961472 | tf_op jit(solution)/shard_map/all_to_all | solution.py:134
  379.0 60.2 %collective-permute-start.1 = (bf16[384,512]{1,0:T(8,128)(2,1)}, bf16[384,512]{1,0:T(8,128)(2,1)S(1)}, u32[]{:S(2)}, u32[]{:S(2)}) collective-permute-start(bf16[384,512]{1,0:T(8,128)(2,1)} %reduce-scatter.11.cloned.1.call-done), channel_id=1, source_target_pairs={{4,0},{8,4},{12,8},{16,12},{20,16},{24,20},{28,24},{0,28},{5,1},{9... | collective-permute-start | bytes 1179656 | tf_op jit(solution)/shard_map/ppermute | solution.py:10
  379.2 64.2 %collective-permute-start = (bf16[512,384]{1,0:T(8,128)(2,1)}, bf16[512,384]{1,0:T(8,128)(2,1)S(1)}, u32[]{:S(2)}, u32[]{:S(2)}) collective-permute-start(bf16[512,384]{1,0:T(8,128)(2,1)} %reduce-scatter.7.cloned.1.call-done), channel_id=1, source_target_pairs={{4,0},{8,4},{12,8},{16,12},{20,16},{24,20},{28,24},{0,28},{5,1},{9... | collective-permute-start | bytes 1179656 | tf_op jit(solution)/shard_map/ppermute | solution.py:10
  456.2 12.3 %copy-start.2 = (bf16[128,2048]{1,0:T(8,128)(2,1)S(1)}, bf16[128,2048]{1,0:T(8,128)(2,1)}, u32[]{:S(2)}) copy-start(bf16[128,2048]{1,0:T(8,128)(2,1)} %param.12) | copy-start | bytes 1572868
  473.4 6.7 %copy-start.12 = (f32[128,8]{1,0:T(8,128)S(1)}, f32[128,8]{1,0:T(8,128)}, u32[]{:S(2)}) copy-start(f32[128,8]{1,0:T(8,128)} %copy-done.11) | copy-start | bytes 12292
  474.1 6.0 %copy-start.3 = (bf16[1024,2048]{1,0:T(8,128)(2,1)S(1)}, bf16[1024,2048]{1,0:T(8,128)(2,1)}, u32[]{:S(2)}) copy-start(bf16[1024,2048]{1,0:T(8,128)(2,1)} %gather_fusion.4) | copy-start | bytes 12582916
  480.1 10.3 %copy-start.1 = (bf16[2,384,2048]{2,1,0:T(8,128)(2,1)S(1)}, bf16[2,384,2048]{2,1,0:T(8,128)(2,1)}, u32[]{:S(2)}) copy-start(bf16[2,384,2048]{2,1,0:T(8,128)(2,1)} %param.18) | copy-start | bytes 9437188
  (17 other events, 46.5 us)
Sparse Core Ops, SparseCore 0:
  212.9 37.4 reduce-scatter.10
  252.8 34.2 reduce-scatter.6
  289.4 59.2 reduce-scatter.4
  350.8 60.2 reduce-scatter.8
where the time goes:
time: 506 us; the launch traced here: 497 us
  local copies, waits for them, and re-layouts  142 us (28%)
  waiting for transfers between devices  134 us (26%)
  other arithmetic  65.6 us (13%)
  blocking collectives  60.7 us (12%)
  matrix products  47.8 us (9%)
  starting transfers between devices  30.6 us (6%)
  between operations  16.8 us (3%)
    all_to_all x1, blocking collectives, local(): lax.all_to_all(send_rows, 'expert', split_axis=0, concat_axis=0, tiled=True)  60.7 us
    ppermute x2, waiting for transfers between devices, from_behind(): return lax.ppermute(block, axis, route)  60.7 us
    all_to_all x1, waiting for transfers between devices, local(): lax.all_to_all(to_buffer(pair_grad, position, valid), 'expert', split_axi...  46.1 us
    gather x2, local copies, waits for them, and re-layouts, sorted_rows_of(): flat[jnp.minimum(source_row, buffer_rows - 1)]  31 us
    gather x2, local copies, waits for them, and re-layouts, to_buffer(): picked = region_values[jnp.minimum(position, region_total - 1)]  28.8 us
    all_to_all x1, waiting for transfers between devices, local(): lax.all_to_all(send_scaled, 'expert', split_axis=0, concat_axis=0, tiled=...  27.5 us
    gather x1, local copies, waits for them, and re-layouts, local(): returned.reshape(buffer_rows, feature_width)[placement]  12.2 us
    gather x1, local copies, waits for them, and re-layouts, local(): grad_back.reshape(buffer_rows, feature_width)[placement]  11.9 us
  transfers between devices with their start and end apart: 10, of which 4 were waited for; matrix products, arithmetic and copies ran while one was open for 41% of the time, Pallas kernels for 0%

commit v1 on v0

v1 whole, which is shorter than its diff:
```python
import jax
import jax.numpy as jnp
from jax import lax
from jax.sharding import PartitionSpec as P

BF16 = jnp.bfloat16
F32 = jnp.float32


def padded(count, multiple):
    return -(-count // multiple) * multiple


def dot(a, b, contract):
    return lax.dot_general(a, b, ((contract[:1], contract[1:]), ((), ())), preferred_element_type=F32)


def split_two(values):
    high = values.astype(BF16)
    return high, (values - high.astype(F32)).astype(BF16)


class CubeExchange:
    def __init__(self):
        self.first = [(i, i ^ (4 if i & 1 else 2)) for i in range(8)]
        self.second = [(i, i ^ (2 if i & 1 else 4)) for i in range(8)]
        self.mate = [(i, i ^ 1) for i in range(8)]

    def sources(self, me):
        core = me % 2
        first = jnp.where(core == 1, 4, 2)
        second = 6 - first
        zero = jnp.zeros_like(me)
        mine = [zero, first, second, zero + 6]
        mates = [zero + 1, second + 1, first + 1, zero + 7]
        return jnp.stack([me ^ m for m in mine + mates])

    def gather(self, block):
        a = lax.ppermute(block, "expert", self.first)
        b = lax.ppermute(block, "expert", self.second)
        own_mate = lax.ppermute(block, "expert", self.mate)
        d = lax.ppermute(a, "expert", self.second)
        a_mate = lax.ppermute(a, "expert", self.mate)
        b_mate = lax.ppermute(b, "expert", self.mate)
        d_mate = lax.ppermute(d, "expert", self.mate)
        return jnp.concatenate([block, a, b, d, own_mate, a_mate, b_mate, d_mate], axis=0)

    def reduce(self, partial):
        rows = partial.shape[0] // 8
        arrived = lax.ppermute(partial[4 * rows :].astype(BF16), "expert", self.mate)
        mine = partial[: 4 * rows].astype(F32) + arrived.astype(F32)
        own, a, b, d = (mine[i * rows : (i + 1) * rows] for i in range(4))
        d_arrived = lax.ppermute(d.astype(BF16), "expert", self.second)
        b_arrived = lax.ppermute(b.astype(BF16), "expert", self.second)
        a = a + d_arrived.astype(F32)
        a_arrived = lax.ppermute(a.astype(BF16), "expert", self.first)
        return own + a_arrived.astype(F32) + b_arrived.astype(F32)


class PlainExchange:
    def __init__(self, count):
        self.count = count

    def sources(self, me):
        return jnp.arange(self.count, dtype=jnp.int32)

    def gather(self, block):
        return lax.all_gather(block, "expert", tiled=True)

    def reduce(self, partial):
        return lax.psum_scatter(
            partial.astype(BF16), "expert", scatter_dimension=0, tiled=True
        ).astype(F32)


def local(
    tokens,
    cotangent,
    gate_weights,
    expert_ids,
    copy_pick,
    copy_expert,
    up_weight,
    down_weight,
    copy_up,
    copy_down,
):
    device_count = lax.axis_size("expert")
    me = lax.axis_index("expert")
    rows, width = tokens.shape
    chosen = expert_ids.shape[1]
    local_count = up_weight.shape[0]
    hidden = up_weight.shape[2]
    expert_count = local_count * device_count
    moved_most = 3 * (rows * chosen // expert_count) // 8
    moved_rows = padded(device_count * moved_most, 128)
    exchange = CubeExchange() if device_count == 8 else PlainExchange(device_count)

    column_count = expert_count + device_count
    owner = expert_ids // local_count
    column = jnp.where(copy_pick == 1, expert_count + owner, expert_ids)
    hit = column[:, :, None] == jnp.arange(column_count, dtype=jnp.int32)
    gates = jnp.sum(jnp.where(hit, gate_weights[:, :, None], 0.0), axis=1)
    moved = jnp.sum(hit[:, :, expert_count:].astype(F32), axis=1)
    lower = (
        jnp.arange(rows, dtype=jnp.int32)[:, None] >= jnp.arange(rows, dtype=jnp.int32)[None, :]
    )
    rank = dot(lower.astype(BF16), moved.astype(BF16), (1, 0)) * moved
    gate_high, gate_low = split_two(gates)
    table_width = padded(2 * column_count + device_count, 128)
    table = jnp.concatenate(
        [
            gate_high,
            gate_low,
            rank.astype(BF16),
            jnp.zeros((rows, table_width - 2 * column_count - device_count), BF16),
        ],
        axis=1,
    )
    behind = (me + device_count - 1) % device_count
    columns = [local_count * me + i for i in range(local_count)] + [expert_count + behind]
    slots = len(columns)
    table_rows = jnp.arange(table_width, dtype=jnp.int32)
    wanted = jnp.stack(columns)
    high_pick = (table_rows[:, None] == wanted[None, :]).astype(BF16)
    low_pick = (table_rows[:, None] == wanted[None, :] + column_count).astype(BF16)
    wanted_rank = 2 * column_count + jnp.stack([behind, me])
    rank_pick = (table_rows[:, None] == wanted_rank[None, :]).astype(BF16)
    up_all = jnp.concatenate([up_weight[i] for i in range(local_count)] + [copy_up[0]], axis=1)
    down_all = jnp.concatenate(
        [down_weight[i] for i in range(local_count)] + [copy_down[0]], axis=0
    )
    to_owner = [(i, (i - 1) % device_count) for i in range(device_count)]
    hot_slot = copy_expert[(me + 1) % device_count] % local_count
    own_width = local_count * hidden

    def some_rows(own_block):
        gathered = exchange.gather(own_block)
        all_tokens = gathered[:, :width]
        all_cotangent = gathered[:, width : 2 * width]
        all_table = gathered[:, 2 * width :]
        slot_gates = dot(all_table, high_pick + low_pick, (1, 0))
        ranks = dot(all_table, rank_pick, (1, 0)).astype(jnp.int32)
        base = jnp.repeat(exchange.sources(me) * moved_most, own_block.shape[0])
        place = jnp.where(ranks > 0, base[:, None] + ranks - 1, -1)
        moved_index = jnp.arange(moved_rows, dtype=jnp.int32)[None, :]
        served_place = (place[:, :1] == moved_index).astype(BF16)
        owned_place = (place[:, 1:] == moved_index).astype(BF16)
        linear = dot(all_tokens, up_all, (1, 0))
        raw_grad = dot(all_cotangent, down_all, (1, 1))
        spread = jnp.repeat(slot_gates, hidden, axis=1)
        sigma = jax.nn.sigmoid(linear)
        active = (linear * sigma).astype(BF16).astype(F32)
        gate_part = jnp.sum((active * raw_grad).reshape(-1, slots, hidden), axis=2)
        weighted = (spread * active).astype(BF16)
        slope = sigma * (1.0 + linear * (1.0 - sigma))
        linear_grad = (spread * raw_grad * slope).astype(BF16)
        both = jnp.concatenate([linear_grad[:, own_width:], weighted[:, own_width:]], axis=1)
        packed = dot(served_place, both, (0, 0)).astype(BF16)
        packed = lax.ppermute(packed, "expert", to_owner)
        unpacked = dot(owned_place, packed, (1, 0)).astype(BF16)
        up_parts = []
        down_parts = []
        for i in range(local_count):
            here = (hot_slot == i).astype(BF16)
            part = slice(i * hidden, (i + 1) * hidden)
            total_grad = linear_grad[:, part] + unpacked[:, :hidden] * here
            total_active = weighted[:, part] + unpacked[:, hidden:] * here
            up_parts.append(dot(all_tokens, total_grad, (0, 0)))
            down_parts.append(dot(total_active, all_cotangent, (0, 0)))
        mixed = dot(weighted, down_all, (1, 0)).astype(BF16)
        back = dot(linear_grad, up_all, (1, 1)).astype(BF16)
        part_high, part_low = split_two(gate_part)
        grad_table = dot(part_high, high_pick, (1, 1)) + dot(part_low, low_pick, (1, 1))
        summed = exchange.reduce(
            jnp.concatenate([mixed, back, grad_table.astype(BF16)], axis=1)
        )
        return summed, jnp.stack(up_parts), jnp.stack(down_parts)

    own = jnp.concatenate([tokens, cotangent, table], axis=1)
    pieces = max(1, device_count // 8)
    if pieces == 1:
        summed, up_sum, down_sum = some_rows(own)
    else:

        def step(totals, piece):
            summed, up_part, down_part = some_rows(piece)
            return (totals[0] + up_part, totals[1] + down_part), summed

        zeros = (jnp.zeros(up_weight.shape, F32), jnp.zeros(down_weight.shape, F32))
        (up_sum, down_sum), summed = lax.scan(
            step, zeros, own.reshape(pieces, rows // pieces, own.shape[1])
        )
        summed = summed.reshape(rows, own.shape[1])
    up_grad = lax.psum_scatter(up_sum.astype(BF16), "dp", scatter_dimension=1, tiled=True)
    down_grad = lax.psum_scatter(down_sum.astype(BF16), "dp", scatter_dimension=2, tiled=True)
    layer_output = summed[:, :width].astype(BF16)
    token_grad = summed[:, width : 2 * width].astype(BF16)
    grads = summed[:, 2 * width : 2 * width + column_count]
    grads = grads + summed[:, 2 * width + column_count : 2 * width + 2 * column_count]
    gate_grad = jnp.sum(jnp.where(hit, grads[:, None, :], 0.0), axis=2)
    return layer_output, token_grad, gate_grad, up_grad, down_grad


def solution(mesh):
    placed = (
        P(("expert", "dp"), None),
        P(("expert", "dp"), None),
        P(("expert", "dp"), None),
        P(("expert", "dp"), None),
        P(("expert", "dp"), None),
        P(),
        P("expert", None, None),
        P("expert", None, None),
        P("expert", None, None),
        P("expert", None, None),
    )
    return jax.shard_map(
        local,
        mesh=mesh,
        in_specs=placed,
        out_specs=(
            P(("expert", "dp"), None),
            P(("expert", "dp"), None),
            P(("expert", "dp"), None),
            P("expert", "dp", None),
            P("expert", None, "dp"),
        ),
        check_vma=False,
    )
```

time: 506 us -> 255 us (0.50)
  the two profiles are of different devices: /device:TPU:1 before, /device:TPU:8 now
where the time goes in v1:
time: 255 us; the launch traced here: 252 us
  waiting for transfers between devices  118 us (46%)
  matrix products  49.3 us (19%)
  local copies, waits for them, and re-layouts  41 us (16%)
  other arithmetic  19.5 us (8%)
  between operations  16.4 us (6%)
  starting transfers between devices  8.34 us (3%)
    reduce_scatter x1, waiting for transfers between devices, local(): lax.psum_scatter(up_sum.astype(BF16), 'dp', scatter_dimension=1, tiled=True)  57.4 us
    dot_general x15, matrix products, dot(): lax.dot_general(a, b, ((contract[:1], contract[1:]), ((), ())), preferred...  49.3 us
    ppermute x1, waiting for transfers between devices, reduce(): b_arrived = lax.ppermute(b.astype(BF16), 'expert', self.second)  20.2 us
    ppermute x1, waiting for transfers between devices, reduce(): d_arrived = lax.ppermute(d.astype(BF16), 'expert', self.second)  13.1 us
    ppermute x1, waiting for transfers between devices, gather(): a = lax.ppermute(block, 'expert', self.first)  12.6 us
    ppermute x1, waiting for transfers between devices, gather(): d = lax.ppermute(a, 'expert', self.second)  11.4 us
    unnamed x39, local copies, waits for them, and re-layouts  10.4 us
    reshape x1, local copies, waits for them, and re-layouts, some_rows(): spread = jnp.repeat(slot_gates, hidden, axis=1)  6.09 us
  transfers between devices with their start and end apart: 14, of which 8 were waited for; matrix products, arithmetic and copies ran while one was open for 19% of the time, Pallas kernels for 0%

profile of v1, /device:TPU:8, one launch (start us, length us, event | category | flops | bytes accessed | tf_op | source)
XLA Modules:
  0.0 252.5 jit_solution(12681747300224451754)
XLA Ops:
  17.8 3.4 %slice_bitcast_fusion.3 = (bf16[2048,384]{1,0:T(8,128)(2,1)S(1)}, bf16[2048,384]{1,0:T(8,128)(2,1)}) fusion(bf16[2,2048,384]{2,1,0:T(8,128)(2,1)} %param.16), kind=kLoop, calls=%fused_computation.46 | loop fusion | bytes 6291456 | tf_op jit(solution)/shard_map/squeeze | solution.py:129
  21.5 4.2 %slice_bitcast_fusion.1 = (bf16[384,2048]{1,0:T(8,128)(2,1)}, bf16[384,2048]{1,0:T(8,128)(2,1)}) fusion(bf16[2,384,2048]{2,1,0:T(8,128)(2,1)} %param.17), kind=kLoop, calls=%fused_computation.44 | loop fusion | bytes 6291456 | tf_op jit(solution)/shard_map/squeeze | solution.py:131
  25.8 12.6 %collective-permute-done = bf16[128,4224]{1,0:T(8,128)(2,1)} collective-permute-done((bf16[128,4224]{1,0:T(8,128)(2,1)S(1)}, bf16[128,4224]{1,0:T(8,128)(2,1)}, u32[]{:S(2)}, u32[]{:S(2)}) %collective-permute-start) | collective-permute-done | bytes 1081376 | tf_op jit(solution)/shard_map/ppermute | solution.py:39
  42.3 11.4 %collective-permute-done.2 = bf16[128,4224]{1,0:T(8,128)(2,1)S(1)} collective-permute-done((bf16[128,4224]{1,0:T(8,128)(2,1)}, bf16[128,4224]{1,0:T(8,128)(2,1)S(1)}, u32[]{:S(2)}, u32[]{:S(2)}) %collective-permute-start.2) | collective-permute-done | bytes 1081376 | tf_op jit(solution)/shard_map/ppermute | solution.py:42
  56.6 3.4 %copy-done.8 = bf16[1024,4224]{1,0:T(8,128)(2,1)} copy-done((bf16[1024,4224]{1,0:T(8,128)(2,1)}, bf16[1024,4224]{1,0:T(8,128)(2,1)S(1)}, u32[]{:S(2)}) %copy-start.8) | copy-done | bytes 8650776
  60.1 2.7 %broadcast_in_dim.29 = f32[1024,3,384]{0,2,1:T(8,128)} broadcast(f32[1024,3]{0,1:T(4,128)S(1)} %fusion.63), dimensions={0,1} | broadcast | bytes 4730880 | tf_op jit(solution)/shard_map/broadcast_in_dim | solution.py:151
  62.9 6.1 %copy.40 = f32[1024,1152]{1,0:T(8,128)} copy(f32[1024,1152]{0,1:T(8,128)} %bitcast.41) | data formatting | bytes 9437184 | tf_op jit(solution)/shard_map/reshape | solution.py:151
  69.0 8.9 %fusion.11 = f32[1024,1152]{1,0:T(8,128)S(1)} fusion(bf16[1024,4224]{1,0:T(8,128)(2,1)} %copy-done.8, bf16[2048,384]{1,0:T(8,128)(2,1)} %bitcast.50, bf16[2048,384]{1,0:T(8,128)(2,1)} %get-tuple-element.19, bf16[2048,384]{1,0:T(8,128)(2,1)S(1)} %get-tuple-element.18), kind=kOutput, calls=%fused_computation.22 | convolution fusion | flops 4845993984 | bytes 13631488 | tf_op jit(solution)/shard_map/dot_general | solution.py:15
  77.9 7.9 %fusion.5 = f32[1024,1152]{1,0:T(8,128)S(1)} fusion(bf16[1024,4224]{1,0:T(8,128)(2,1)} %copy-done.8, bf16[384,2048]{1,0:T(8,128)(2,1)S(1)} %bitcast.48, bf16[384,2048]{1,0:T(8,128)(2,1)S(1)} %copy-done.5, bf16[384,2048]{1,0:T(8,128)(2,1)S(1)} %copy-done.4), kind=kOutput, calls=%fused_computation.16 | convolution fusion | flops 4845993984 | bytes 13631488 | tf_op jit(solution)/shard_map/dot_general | solution.py:15
  85.9 4.7 %fusion = (bf16[1024,1152]{1,0:T(8,128)(2,1)S(1)}, bf16[1024,1152]{1,0:T(8,128)(2,1)S(1)}, f32[1024,1152]{1,0:T(8,128)}) fusion(f32[1024,1152]{1,0:T(8,128)S(1)} %bitcast.43, f32[1024,1152]{1,0:T(8,128)S(1)} %fusion.11, f32[1024,1152]{1,0:T(8,128)S(1)} %fusion.5), kind=kLoop, calls=%fused_computation.4 | loop fusion | flops 18874368 | bytes 23592960 | tf_op jit(solution)/shard_map/convert_element_type | solution.py:155
  90.7 7.2 %convolution_convert_fusion.1 = bf16[1024,2048]{1,0:T(8,128)(2,1)} fusion(bf16[1024,1152]{1,0:T(8,128)(2,1)S(1)} %get-tuple-element.13, bf16[384,2048]{1,0:T(8,128)(2,1)S(1)} %bitcast.49, bf16[384,2048]{1,0:T(8,128)(2,1)S(1)} %copy-done.5, bf16[384,2048]{1,0:T(8,128)(2,1)S(1)} %copy-done.4), kind=kOutput, calls=%fused_computation.11 | convolution fusion | flops 4848091136 | bytes 11272192 | tf_op jit(solution)/shard_map/dot_general | solution.py:15
  101.4 6.1 %copy.42 = f32[1024,1152]{0,1:T(8,128)} copy(f32[1024,1152]{1,0:T(8,128)} %get-tuple-element.15) | data formatting | bytes 9437184 | tf_op jit(solution)/shard_map/mul | solution.py:154
  107.5 2.6 %reduce_sum.38 = f32[1024,3]{0,1:T(4,128)S(1)} reduce(f32[1024,3,384]{0,2,1:T(8,128)} %bitcast.40, f32[]{:T(128)} %constant.65.clone.1), dimensions={2}, to_apply=%region_2.3 | reduce | flops 1176576 | bytes 4730884 | tf_op jit(solution)/shard_map/reduce_sum | solution.py:154
  111.4 4.9 %fusion.28 = bf16[1,384,2048]{2,1,0:T(8,128)(2,1)S(1)} fusion(bf16[1024,4224]{1,0:T(8,128)(2,1)} %copy-done.8, bf16[1024,1152]{1,0:T(8,128)(2,1)} %copy-done.1, bf16[1024,768]{1,0:T(8,128)(2,1)S(1)} %convolution_convert_fusion.2, bf16[]{:T(256)S(6)} %convert_element_type.124), kind=kOutput, calls=%fused_computation.31 | convolution fusion | flops 1612185600 | bytes 7340034 | tf_op jit(solution)/shard_map/dot_general | solution.py:15
  116.2 4.3 %fusion.25 = bf16[1,384,2048]{2,1,0:T(8,128)(2,1)S(1)} fusion(bf16[1024,4224]{1,0:T(8,128)(2,1)} %copy-done.8, bf16[1024,1152]{1,0:T(8,128)(2,1)} %copy-done.1, bf16[1024,768]{1,0:T(8,128)(2,1)S(1)} %convolution_convert_fusion.2, bf16[]{:T(256)S(6)} %convert_element_type.125), kind=kOutput, calls=%fused_computation.30 | convolution fusion | flops 1612185600 | bytes 7340034 | tf_op jit(solution)/shard_map/dot_general | solution.py:15
  122.6 7.8 %convolution_convert_fusion = bf16[1024,2048]{1,0:T(8,128)(2,1)S(1)} fusion(bf16[1024,1152]{1,0:T(8,128)(2,1)S(1)} %get-tuple-element.14, bf16[2048,384]{1,0:T(8,128)(2,1)} %bitcast.51, bf16[2048,384]{1,0:T(8,128)(2,1)} %get-tuple-element.19, bf16[2048,384]{1,0:T(8,128)(2,1)} %copy-done.3), kind=kOutput, calls=%fused_computation.10 | convolution fusion | flops 4848091136 | bytes 11272192 | tf_op jit(solution)/shard_map/dot_general | solution.py:15
  131.2 2.4 slice.123
  133.6 2.4 copy-done
  136.0 2.4 fusion.34
  138.4 2.4 fusion.31
  143.7 4.6 %convert_add_fusion = (f32[512,4224]{1,0:T(8,128)S(1)}, bf16[512,4224]{1,0:T(8,128)(2,1)S(1)}) fusion(bf16[512,4224]{1,0:T(8,128)(2,1)} %collective-permute-done.7, bf16[1024,4224]{1,0:T(8,128)(2,1)} %copy-done), kind=kLoop, calls=%fused_computation.1 | loop fusion | flops 8650752 | bytes 21626880 | tf_op jit(solution)/shard_map/add | solution.py:51
  150.5 13.1 %collective-permute-done.8 = bf16[128,4224]{1,0:T(8,128)(2,1)S(1)} collective-permute-done((bf16[128,4224]{1,0:T(8,128)(2,1)S(1)}, bf16[128,4224]{1,0:T(8,128)(2,1)S(1)}, u32[]{:S(2)}, u32[]{:S(2)}) %collective-permute-start.8) | collective-permute-done | bytes 1081376 | tf_op jit(solution)/shard_map/ppermute | solution.py:53
  164.3 20.2 %collective-permute-done.10 = bf16[128,4224]{1,0:T(8,128)(2,1)S(1)} collective-permute-done((bf16[128,4224]{1,0:T(8,128)(2,1)S(1)}, bf16[128,4224]{1,0:T(8,128)(2,1)S(1)}, u32[]{:S(2)}, u32[]{:S(2)}) %collective-permute-start.10) | collective-permute-done | bytes 1081376 | tf_op jit(solution)/shard_map/ppermute | solution.py:54
  188.2 57.4 %reduce-scatter.3.cloned.1.call-done = bf16[2,512,384]{2,1,0:T(8,128)(2,1)} async-done(((bf16[2,2048,384]{2,1,0:T(8,128)(2,1)}), bf16[2,512,384]{2,1,0:T(8,128)(2,1)}) %reduce-scatter.3.cloned.1.call-update) | async-done | bytes 786448 | tf_op jit(solution)/shard_map/reduce_scatter | solution.py:195
  (101 shorter events, 33.0 us)
Async XLA Ops:
  7.2 181.0 %reduce-scatter.5.cloned.1.call-start = ((), (), s32[]{:S(2)}) async-start(), calls=%async_computation.3 | async-start | bytes 3932160 | tf_op jit(solution)/shard_map/reduce_scatter | solution.py:196
  11.6 26.8 %collective-permute-start = (bf16[128,4224]{1,0:T(8,128)(2,1)S(1)}, bf16[128,4224]{1,0:T(8,128)(2,1)}, u32[]{:S(2)}, u32[]{:S(2)}) collective-permute-start(bf16[128,4224]{1,0:T(8,128)(2,1)S(1)} %concatenate.26), channel_id=1, source_target_pairs={{0,8},{4,20},{8,0},{12,28},{16,24},{20,4},{24,16},{28,12},{1,9},{5... | collective-permute-start | bytes 3244040 | tf_op jit(solution)/shard_map/ppermute | solution.py:39
  13.1 26.0 %collective-permute-start.1 = (bf16[128,4224]{1,0:T(8,128)(2,1)S(1)}, bf16[128,4224]{1,0:T(8,128)(2,1)}, u32[]{:S(2)}, u32[]{:S(2)}) collective-permute-start(bf16[128,4224]{1,0:T(8,128)(2,1)S(1)} %concatenate.26), channel_id=1, source_target_pairs={{0,16},{4,12},{8,24},{12,4},{16,0},{20,28},{24,8},{28,20},{1,17},{... | collective-permute-start | bytes 3244040 | tf_op jit(solution)/shard_map/ppermute | solution.py:40
  14.6 39.2 %collective-permute-start.3 = (bf16[128,4224]{1,0:T(8,128)(2,1)S(1)}, bf16[128,4224]{1,0:T(8,128)(2,1)}, u32[]{:S(2)}, u32[]{:S(2)}) collective-permute-start(bf16[128,4224]{1,0:T(8,128)(2,1)S(1)} %concatenate.26), channel_id=1, source_target_pairs={{0,4},{4,0},{8,12},{12,8},{16,20},{20,16},{24,28},{28,24},{1,5},{5... | collective-permute-start | bytes 3244040 | tf_op jit(solution)/shard_map/ppermute | solution.py:41
  21.2 47.7 %copy-start.3 = (bf16[2048,384]{1,0:T(8,128)(2,1)}, bf16[2048,384]{1,0:T(8,128)(2,1)S(1)}, u32[]{:S(2)}) copy-start(bf16[2048,384]{1,0:T(8,128)(2,1)S(1)} %get-tuple-element.18) | copy-start | bytes 4718596
  38.4 15.4 %collective-permute-start.2 = (bf16[128,4224]{1,0:T(8,128)(2,1)}, bf16[128,4224]{1,0:T(8,128)(2,1)S(1)}, u32[]{:S(2)}, u32[]{:S(2)}) collective-permute-start(bf16[128,4224]{1,0:T(8,128)(2,1)} %collective-permute-done), channel_id=1, source_target_pairs={{0,16},{4,12},{8,24},{12,4},{16,0},{20,28},{24,8},{28,20},{1,17},{... | collective-permute-start | bytes 3244040 | tf_op jit(solution)/shard_map/ppermute | solution.py:42
  39.1 16.2 %collective-permute-start.4 = (bf16[128,4224]{1,0:T(8,128)(2,1)}, bf16[128,4224]{1,0:T(8,128)(2,1)S(1)}, u32[]{:S(2)}, u32[]{:S(2)}) collective-permute-start(bf16[128,4224]{1,0:T(8,128)(2,1)} %collective-permute-done), channel_id=1, source_target_pairs={{0,4},{4,0},{8,12},{12,8},{16,20},{20,16},{24,28},{28,24},{1,5},{5... | collective-permute-start | bytes 3244040 | tf_op jit(solution)/shard_map/ppermute | solution.py:43
  39.1 16.3 %collective-permute-start.5 = (bf16[128,4224]{1,0:T(8,128)(2,1)}, bf16[128,4224]{1,0:T(8,128)(2,1)S(1)}, u32[]{:S(2)}, u32[]{:S(2)}) collective-permute-start(bf16[128,4224]{1,0:T(8,128)(2,1)} %collective-permute-done.1), channel_id=1, source_target_pairs={{0,4},{4,0},{8,12},{12,8},{16,20},{20,16},{24,28},{28,24},{1,5},{5... | collective-permute-start | bytes 3244040 | tf_op jit(solution)/shard_map/ppermute | solution.py:44
  53.7 2.7 %collective-permute-start.6 = (bf16[128,4224]{1,0:T(8,128)(2,1)S(1)}, bf16[128,4224]{1,0:T(8,128)(2,1)S(1)}, u32[]{:S(2)}, u32[]{:S(2)}) collective-permute-start(bf16[128,4224]{1,0:T(8,128)(2,1)S(1)} %collective-permute-done.2), channel_id=1, source_target_pairs={{0,4},{4,0},{8,12},{12,8},{16,20},{20,16},{24,28},{28,24},{1,5},{5... | collective-permute-start | bytes 3244040 | tf_op jit(solution)/shard_map/ppermute | solution.py:45
  69.0 8.9 %copy-start.4 = (bf16[384,2048]{1,0:T(8,128)(2,1)S(1)}, bf16[384,2048]{1,0:T(8,128)(2,1)}, u32[]{:S(2)}) copy-start(bf16[384,2048]{1,0:T(8,128)(2,1)} %get-tuple-element.20) | copy-start | bytes 4718596
  69.0 8.9 %copy-start.5 = (bf16[384,2048]{1,0:T(8,128)(2,1)S(1)}, bf16[384,2048]{1,0:T(8,128)(2,1)}, u32[]{:S(2)}) copy-start(bf16[384,2048]{1,0:T(8,128)(2,1)} %get-tuple-element.21) | copy-start | bytes 4718596
  69.0 8.9 %copy-start.9 = (bf16[1,384,2048]{2,1,0:T(8,128)(2,1)S(1)}, bf16[1,384,2048]{2,1,0:T(8,128)(2,1)}, u32[]{:S(2)}) copy-start(bf16[1,384,2048]{2,1,0:T(8,128)(2,1)} %param.19) | copy-start | bytes 4718596
  69.0 16.8 %slice-start = ((s8[4718592]{0:T(1024)(128)(4,1)}), s8[4194304]{0:T(1024)(128)(4,1)S(1)}, s32[]{:S(2)}) async-start(s8[4718592]{0:T(1024)(128)(4,1)} %bitcast.42), calls=%async_computation.4 | async-start | bytes 8388608
  77.8 8.0 %slice-start.1 = ((s8[4718592]{0:T(1024)(128)(4,1)}), s8[524288]{0:T(1024)(128)(4,1)S(1)}, s32[]{:S(2)}) async-start(s8[4718592]{0:T(1024)(128)(4,1)} %bitcast.42), calls=%async_computation.5 | async-start | bytes 1048576
  90.6 7.3 %copy-start.1 = (bf16[1024,1152]{1,0:T(8,128)(2,1)}, bf16[1024,1152]{1,0:T(8,128)(2,1)S(1)}, u32[]{:S(2)}) copy-start(bf16[1024,1152]{1,0:T(8,128)(2,1)S(1)} %get-tuple-element.13) | copy-start | bytes 7077892
  100.0 10.7 %collective-permute-start.11 = (bf16[256,768]{1,0:T(8,128)(2,1)S(1)}, bf16[256,768]{1,0:T(8,128)(2,1)S(1)}, u32[]{:S(2)}, u32[]{:S(2)}) collective-permute-start(bf16[256,768]{1,0:T(8,128)(2,1)S(1)} %fusion.43), channel_id=1, source_target_pairs={{0,28},{4,0},{8,4},{12,8},{16,12},{20,16},{24,20},{28,24},{1,29},{... | collective-permute-start | bytes 1179656 | tf_op jit(solution)/shard_map/ppermute | solution.py:160
  122.5 123.1 %reduce-scatter.3.cloned.1.call-start = ((), (), s32[]{:S(2)}) async-start(), calls=%async_computation.2 | async-start | bytes 3932160 | tf_op jit(solution)/shard_map/reduce_scatter | solution.py:195
  122.5 7.9 %copy-start.2 = (bf16[1024,2048]{1,0:T(8,128)(2,1)S(1)}, bf16[1024,2048]{1,0:T(8,128)(2,1)}, u32[]{:S(2)}) copy-start(bf16[1024,2048]{1,0:T(8,128)(2,1)} %convolution_convert_fusion.1) | copy-start | bytes 12582916
  122.6 13.4 %slice-start.2 = ((s8[8650752]{0:T(1024)(128)(4,1)}), s8[4194304]{0:T(1024)(128)(4,1)S(1)}, s32[]{:S(2)}) async-start(s8[8650752]{0:T(1024)(128)(4,1)} %bitcast.44), calls=%async_computation.6 | async-start | bytes 8388608
  122.6 13.4 %slice-start.3 = ((s8[8650752]{0:T(1024)(128)(4,1)}), s8[4194304]{0:T(1024)(128)(4,1)S(1)}, s32[]{:S(2)}) async-start(s8[8650752]{0:T(1024)(128)(4,1)} %bitcast.44), calls=%async_computation.7 | async-start | bytes 8388608
  136.0 7.7 %collective-permute-start.7 = (bf16[512,4224]{1,0:T(8,128)(2,1)}, bf16[512,4224]{1,0:T(8,128)(2,1)}, u32[]{:S(2)}, u32[]{:S(2)}) collective-permute-start(bf16[512,4224]{1,0:T(8,128)(2,1)} %slice.123), channel_id=1, source_target_pairs={{0,4},{4,0},{8,12},{12,8},{16,20},{20,16},{24,28},{28,24},{1,5},{5... | collective-permute-start | bytes 12976136 | tf_op jit(solution)/shard_map/ppermute | solution.py:50
  148.4 15.2 %collective-permute-start.8 = (bf16[128,4224]{1,0:T(8,128)(2,1)S(1)}, bf16[128,4224]{1,0:T(8,128)(2,1)S(1)}, u32[]{:S(2)}, u32[]{:S(2)}) collective-permute-start(bf16[128,4224]{1,0:T(8,128)(2,1)S(1)} %get-tuple-element.16), channel_id=1, source_target_pairs={{0,16},{4,12},{8,24},{12,4},{16,0},{20,28},{24,8},{28,20},{1,17},{... | collective-permute-start | bytes 3244040 | tf_op jit(solution)/shard_map/ppermute | solution.py:53
  149.8 34.7 %collective-permute-start.10 = (bf16[128,4224]{1,0:T(8,128)(2,1)S(1)}, bf16[128,4224]{1,0:T(8,128)(2,1)S(1)}, u32[]{:S(2)}, u32[]{:S(2)}) collective-permute-start(bf16[128,4224]{1,0:T(8,128)(2,1)S(1)} %get-tuple-element.17), channel_id=1, source_target_pairs={{0,16},{4,12},{8,24},{12,4},{16,0},{20,28},{24,8},{28,20},{1,17},{... | collective-permute-start | bytes 3244040 | tf_op jit(solution)/shard_map/ppermute | solution.py:54
  163.9 22.1 %collective-permute-start.9 = (bf16[128,4224]{1,0:T(8,128)(2,1)S(1)}, bf16[128,4224]{1,0:T(8,128)(2,1)S(1)}, u32[]{:S(2)}, u32[]{:S(2)}) collective-permute-start(bf16[128,4224]{1,0:T(8,128)(2,1)S(1)} %fusion.37), channel_id=1, source_target_pairs={{0,8},{4,20},{8,0},{12,28},{16,24},{20,4},{24,16},{28,12},{1,9},{5... | collective-permute-start | bytes 3244040 | tf_op jit(solution)/shard_map/ppermute | solution.py:56
  (6 other events, 28.2 us)
Sparse Core Ops, SparseCore 0:
  122.6 59.7 reduce-scatter.4
  185.3 60.2 reduce-scatter.2

commit v2 on v1

--- a/solution.py
+++ b/solution.py
@@ -1,6 +1,10 @@
+import functools
+
 import jax
 import jax.numpy as jnp
 from jax import lax
+from jax.experimental import pallas as pl
+from jax.experimental.pallas import tpu as pltpu
 from jax.sharding import PartitionSpec as P
 
 BF16 = jnp.bfloat16
@@ -18,6 +22,461 @@
 def split_two(values):
     high = values.astype(BF16)
     return high, (values - high.astype(F32)).astype(BF16)
+
+
+VMEM_LIMIT = 64 * 1024 * 1024
+ANYWHERE = pl.BlockSpec(memory_space=pl.ANY)
+
+
+def call_params():
+    return pltpu.CompilerParams(vmem_limit_bytes=VMEM_LIMIT)
+
+
+def small_cost():
+    return pl.CostEstimate(flops=1, bytes_accessed=1, transcendentals=0)
+
+
+class Fetches:
+    def __init__(self, sems):
+        self.sems = sems
+        self.copies = []
+
+    def add(self, source, target):
+        self.copies.append(
+            pltpu.make_async_copy(source, target, self.sems.at[len(self.copies)])
+        )
+        return len(self.copies) - 1
+
+    def start(self):
+        for copy in self.copies:
+            copy.start()
+
+    def wait(self, numbers):
+        for number in numbers:
+            self.copies[number].wait()
+
+
+COPY, COLD = "copy", "cold"
+SERVED_RANK, OWNED_RANK, COLD_GATE = 3, 4, 5
+
+
+def hidden_kernel(blocks, slots, packing, width, *refs):
+    hot_ref, refs = refs[0], refs[1:]
+    row_refs, refs = refs[:blocks], refs[blocks:]
+    up_ref, down_ref, copy_up_ref, copy_down_ref, pick_ref, base_ref, *refs = refs
+    before_ref = refs.pop(0) if packing == 2 else None
+    grad_ref, active_ref, *refs = refs
+    part_ref = refs.pop(0) if COLD not in slots else None
+    place_ref, packed_ref = (refs.pop(0), refs.pop(0)) if packing else (None, None)
+    together, ups, downs, gates, slot_sems, block_sems = refs
+    rows = row_refs[0].shape[0]
+    hidden = down_ref.shape[1]
+    group = 2 * rows
+
+    def slot_copies(number, slot):
+        index = 0 if slot == COPY else (1 - hot_ref[0] if slot == COLD else slot)
+        up, down = (copy_up_ref, copy_down_ref) if slot == COPY else (up_ref, down_ref)
+        return [
+            pltpu.make_async_copy(up.at[index], ups.at[number], slot_sems.at[number, 0]),
+            pltpu.make_async_copy(down.at[index], downs.at[number], slot_sems.at[number, 1]),
+        ]
+
+    block_copies = [
+        pltpu.make_async_copy(ref, together.at[pl.ds(i * rows, rows)], block_sems.at[i])
+        for i, ref in enumerate(row_refs)
+    ]
+    for copy in slot_copies(0, slots[0]) + block_copies:
+        copy.start()
+    for number in range(1, len(slots)):
+        for copy in slot_copies(number, slots[number]):
+            copy.start()
+    for copy in block_copies:
+        copy.wait()
+    gates[...] = dot(pick_ref[...], together[:, 2 * width :], (1, 1))
+    if packing:
+        ranks = gates[SERVED_RANK : OWNED_RANK + 1, :]
+        place = jnp.where(ranks > 0.5, base_ref[...] + ranks - 1.0, -1.0)
+        place_ref[...] = jnp.concatenate([place, jnp.zeros((6, place.shape[1]), F32)], axis=0)
+    first_gate = 0 if slots[0] == COPY else (COLD_GATE if slots[0] == COLD else 1)
+
+    @pl.loop(0, len(slots))
+    def _(number):
+        for copy in slot_copies(number, slots[-1]):
+            copy.wait()
+        to = pl.ds(pl.multiple_of(number * hidden, hidden), hidden)
+
+        for g in range(blocks // 2):
+            here = slice(g * group, (g + 1) * group)
+            gate = gates[pl.ds(first_gate + number, 1), here]
+            linear = dot(ups[number], together[here, :width], (0, 1))
+            raw_grad = dot(downs[number], together[here, width : 2 * width], (1, 1))
+            sigma = 0.5 * jnp.tanh(0.5 * linear) + 0.5
+            active = (linear * sigma).astype(BF16).astype(F32)
+            if part_ref is not None:
+                part = jnp.sum(active * raw_grad, axis=0, keepdims=True)
+                part_high, part_low = split_two(part)
+                part_ref[pl.ds(pl.multiple_of(16 * number, 16), 16), here] = jnp.concatenate(
+                    [part_high, part_low, jnp.zeros((14, group), BF16)], axis=0
+                )
+            active_ref[to, here] = (gate * active).astype(BF16)
+            slope = sigma * (1.0 + linear * (1.0 - sigma))
+            grad_ref[to, here] = (gate * raw_grad * slope).astype(BF16)
+
+    if packing:
+        moved_rows = packed_ref.shape[1]
+        index = lax.broadcasted_iota(jnp.int32, (moved_rows, blocks * rows), 0)
+        chosen = (index == place_ref[0:1, :].astype(jnp.int32)).astype(F32).astype(BF16)
+        for half, ref in enumerate((grad_ref, active_ref)):
+            to = slice(half * hidden, (half + 1) * hidden)
+            found = dot(ref[:hidden, :], chosen, (1, 1))
+            if before_ref is not None:
+                found = found + before_ref[to, :].astype(F32)
+            packed_ref[to, :] = found.astype(BF16)
+
+
+def hidden_call(hot, blocks, weights, pick, base, slots, moved_rows=0, before=None):
+    count = len(blocks)
+    rows, columns = blocks[0].shape
+    width, hidden = weights[0].shape[1:]
+    total = count * rows
+    packing = 0 if moved_rows == 0 else (1 if before is None else 2)
+    vmem = pl.BlockSpec(memory_space=pltpu.VMEM)
+    operands = [hot, *blocks, *weights, pick, base]
+    in_specs = [pl.BlockSpec(memory_space=pltpu.SMEM)] + [ANYWHERE] * (count + 4) + [vmem] * 2
+    if packing == 2:
+        operands.append(before)
+        in_specs.append(vmem)
+    out_shape = [jax.ShapeDtypeStruct((len(slots) * hidden, total), BF16)] * 2
+    if COLD not in slots:
+        out_shape.append(jax.ShapeDtypeStruct((len(slots) * 16, total), BF16))
+    if packing:
+        out_shape.append(jax.ShapeDtypeStruct((8, total), F32))
+        out_shape.append(jax.ShapeDtypeStruct((2 * hidden, moved_rows), BF16))
+    return pl.pallas_call(
+        functools.partial(hidden_kernel, count, slots, packing, width),
+        in_specs=in_specs,
+        out_specs=[vmem] * len(out_shape),
+        out_shape=out_shape,
+        scratch_shapes=[
+            pltpu.VMEM((total, columns), BF16),
+            pltpu.VMEM((len(slots), width, hidden), BF16),
+            pltpu.VMEM((len(slots), hidden, width), BF16),
+            pltpu.VMEM((16, total), F32),
+            pltpu.SemaphoreType.DMA((len(slots), 2)),
+            pltpu.SemaphoreType.DMA((count,)),
+        ],
+        compiler_params=call_params(),
+        cost_estimate=small_cost(),
+        name="hidden_units",
+    )(*operands)
+
+
+def fetch_pieces(fetches, pieces, expert, target):
+    hidden = target.shape[0]
+    found, column = [], 0
+    for piece, first in pieces:
+        count = piece.shape[1]
+        source = piece
+        if first is not None:
+            start = pl.multiple_of((first + expert) * hidden, hidden)
+            source = piece.at[pl.ds(start, hidden)]
+        found.append(fetches.add(source, target.at[:, pl.ds(column, count)]))
+        column += count
+    return found
+
+
+def chunk_copies_of(row_refs, tokens, cotan, width, sems):
+    rows, chunk = row_refs[0].shape[0], tokens.shape[2]
+
+    def copies(place, number, half):
+        columns = pl.ds(pl.multiple_of(half * width + number * chunk, chunk), chunk)
+        target = (tokens, cotan)[half]
+        return [
+            pltpu.make_async_copy(
+                ref.at[:, columns],
+                target.at[place, pl.ds(i * rows, rows)],
+                sems.at[place, half, i],
+            )
+            for i, ref in enumerate(row_refs)
+        ]
+
+    return copies
+
+
+def hot_kernel(blocks, firsts, width, *refs):
+    hot_ref, refs = refs[0], refs[1:]
+    row_refs, refs = refs[:blocks], refs[blocks:]
+    pieces = len(firsts)
+    grad_refs, active_refs, place_refs, refs = (
+        refs[:pieces], refs[pieces : 2 * pieces], refs[2 * pieces : 3 * pieces], refs[3 * pieces :]
+    )
+    packed_ref, out_ref, grads, actives, tokens, cotan, sems, chunk_sems = refs
+    chunks, total, chunk = tokens.shape
+    hidden = grads.shape[0]
+    fetches = Fetches(sems)
+    of_rows = []
+    for sources, target in ((grad_refs, grads), (active_refs, actives)):
+        of_rows.append(fetch_pieces(fetches, list(zip(sources, firsts)), hot_ref[0], target))
+    chunk_copies = chunk_copies_of(row_refs, tokens, cotan, width, chunk_sems)
+    fetches.start()
+
+    @pl.loop(0, chunks)
+    def _(j):
+        for copy in chunk_copies(j, j, 0) + chunk_copies(j, j, 1):
+            copy.start()
+
+    place = jnp.concatenate([ref[1:2, :] for ref in place_refs], axis=1)
+    index = lax.broadcasted_iota(jnp.int32, (packed_ref.shape[1], total), 0)
+    chosen = (index == place.astype(jnp.int32)).astype(F32).astype(BF16)
+    for half, target in enumerate((grads, actives)):
+        fetches.wait(of_rows[half])
+        spread = dot(packed_ref[half * hidden : (half + 1) * hidden, :], chosen, (1, 0))
+        target[...] = (target[...].astype(F32) + spread).astype(BF16)
+
+    @pl.loop(0, chunks)
+    def _(j):
+        for half, (left, right) in enumerate(((grads, tokens), (actives, cotan))):
+            for copy in chunk_copies(j, j, half):
+                copy.wait()
+            out_ref[j, half] = dot(left[...], right[j], (1, 0)).astype(BF16)
+
+
+def hot_call(hot, blocks, firsts, grads, actives, places, packed, width, chunks):
+    count = len(blocks)
+    total = count * blocks[0].shape[0]
+    chunk = width // chunks
+    hidden = packed.shape[0] // 2
+    vmem = pl.BlockSpec(memory_space=pltpu.VMEM)
+    return pl.pallas_call(
+        functools.partial(hot_kernel, count, firsts, width),
+        in_specs=[pl.BlockSpec(memory_space=pltpu.SMEM)]
+        + [ANYWHERE] * (count + 2 * len(firsts))
+        + [vmem] * (len(firsts) + 1),
+        out_specs=vmem,
+        out_shape=jax.ShapeDtypeStruct((chunks, 2, hidden, chunk), BF16),
+        scratch_shapes=[
+            pltpu.VMEM((hidden, total), BF16),
+            pltpu.VMEM((hidden, total), BF16),
+            pltpu.VMEM((chunks, total, chunk), BF16),
+            pltpu.VMEM((chunks, total, chunk), BF16),
+            pltpu.SemaphoreType.DMA((2 * len(firsts),)),
+            pltpu.SemaphoreType.DMA((chunks, 2, count)),
+        ],
+        compiler_params=call_params(),
+        cost_estimate=small_cost(),
+        name="hot_weight_grads",
+    )(hot, *blocks, *grads, *actives, *places, packed)
+
+
+def cold_kernel(blocks, firsts, width, *refs):
+    hot_ref, chunk_ref, refs = refs[0], refs[1], refs[2:]
+    row_refs, refs = refs[:blocks], refs[blocks:]
+    pieces = len(firsts)
+    grad_refs, active_refs, refs = refs[:pieces], refs[pieces : 2 * pieces], refs[2 * pieces :]
+    near_ref, far_ref, grads, actives, tokens, cotan, sems, chunk_sems = refs
+    fetches = Fetches(sems)
+    of_rows = []
+    for sources, target in ((grad_refs, grads), (active_refs, actives)):
+        of_rows.append(fetch_pieces(fetches, list(zip(sources, firsts)), 1 - hot_ref[0], target))
+    chunk_copies = chunk_copies_of(row_refs, tokens, cotan, width, chunk_sems)
+    fetches.start()
+
+    @pl.loop(0, 2)
+    def _(j):
+        for copy in chunk_copies(j, chunk_ref[j], 0) + chunk_copies(j, chunk_ref[j], 1):
+            copy.start()
+
+    for j, out_ref in enumerate((near_ref, far_ref)):
+        for half, (left, right) in enumerate(((grads, tokens), (actives, cotan))):
+            if j == 0:
+                fetches.wait(of_rows[half])
+            for copy in chunk_copies(j, chunk_ref[j], half):
+                copy.wait()
+            out_ref[half] = dot(left[...], right[j], (1, 0)).astype(BF16)
+
+
+def cold_call(hot, chunk_pair, blocks, firsts, grads, actives, width, chunk):
+    count = len(blocks)
+    total = count * blocks[0].shape[0]
+    hidden = grads[-1].shape[0]
+    vmem = pl.BlockSpec(memory_space=pltpu.VMEM)
+    smem = pl.BlockSpec(memory_space=pltpu.SMEM)
+    return pl.pallas_call(
+        functools.partial(cold_kernel, count, firsts, width),
+        in_specs=[smem, smem] + [ANYWHERE] * (count + 2 * len(firsts)),
+        out_specs=[vmem, vmem],
+        out_shape=[jax.ShapeDtypeStruct((2, hidden, chunk), BF16)] * 2,
+        scratch_shapes=[
+            pltpu.VMEM((hidden, total), BF16),
+            pltpu.VMEM((hidden, total), BF16),
+            pltpu.VMEM((2, total, chunk), BF16),
+            pltpu.VMEM((2, total, chunk), BF16),
+            pltpu.SemaphoreType.DMA((2 * len(firsts),)),
+            pltpu.SemaphoreType.DMA((2, 2, count)),
+        ],
+        compiler_params=call_params(),
+        cost_estimate=small_cost(),
+        name="cold_weight_grads",
+    )(hot, chunk_pair, *blocks, *grads, *actives)
+
+
+def rows_kernel(half, pieces, is_output, with_arrived, *refs):
+    left_refs, refs = refs[:pieces], refs[pieces:]
+    own_ref, copy_ref, *refs = refs
+    part_refs, pick_ref = (), None
+    if is_output:
+        part_refs, pick_ref, refs = refs[:pieces], refs[pieces], refs[pieces + 1 :]
+    arrived_ref = refs.pop(0) if with_arrived else None
+    outs = 4 if with_arrived else 1
+    out_refs, refs = refs[:outs], refs[outs:]
+    left, weights, out, *refs = refs
+    arrived = refs.pop(0) if with_arrived else None
+    sems, chunk_sems, out_sems = refs
+    hidden = own_ref.shape[1] if is_output else own_ref.shape[2]
+    width = own_ref.shape[2] if is_output else own_ref.shape[1]
+    step = weights.shape[3] if is_output else weights.shape[2]
+    chunks = width // step
+    slots = weights.shape[1]
+    fetches = Fetches(sems)
+    of_left = []
+    row, column = 0, 0
+    for ref in left_refs:
+        count = ref.shape[1] // 2
+        of_left.append(
+            fetches.add(
+                ref.at[:, pl.ds(half * count, count)],
+                left.at[pl.ds(row, ref.shape[0]), pl.ds(column, count)],
+            )
+        )
+        row += ref.shape[0]
+        if row == left.shape[0]:
+            row, column = 0, column + count
+    fetches.start()
+    tail = pl.ds(width, out.shape[1] - width)
+
+    def chunk_copies(j):
+        here = pl.ds(pl.multiple_of(j * step, step), step)
+        found = []
+        for slot in range(slots):
+            source = copy_ref.at[0] if slot == 0 else own_ref.at[slot - 1]
+            source = source.at[:, here] if is_output else source.at[here]
+            found.append(
+                pltpu.make_async_copy(source, weights.at[j, slot], chunk_sems.at[j, slot])
+            )
+        if with_arrived:
+            found.append(
+                pltpu.make_async_copy(
+                    arrived_ref.at[:, here], arrived.at[:, here], chunk_sems.at[j, slots]
+                )
+            )
+        return found
+
+    def stores_of(here, number):
+        rows = out.shape[0] // outs
+        return [
+            pltpu.make_async_copy(
+                out.at[pl.ds(i * rows, rows), here], ref.at[:, here], out_sems.at[number, i]
+            )
+            for i, ref in enumerate(out_refs)
+        ]
+
+    tail_copies = []
+    if with_arrived and is_output:
+        tail_copies.append(
+            pltpu.make_async_copy(
+                arrived_ref.at[:, tail], arrived.at[:, tail], chunk_sems.at[chunks, 0]
+            )
+        )
+
+    @pl.loop(0, chunks)
+    def _(j):
+        for copy in chunk_copies(j):
+            copy.start()
+
+    for copy in tail_copies:
+        copy.start()
+    fetches.wait(of_left)
+
+    def store(here, number, values):
+        if with_arrived:
+            values = values + arrived[:, here].astype(F32)
+        out[:, here] = values.astype(BF16)
+        for copy in stores_of(here, number):
+            copy.start()
+
+    @pl.loop(0, chunks)
+    def _(j):
+        here = pl.ds(pl.multiple_of(j * step, step), step)
+        for copy in chunk_copies(j):
+            copy.wait()
+        if is_output:
+            right = weights[j].reshape(slots * hidden, step)
+            values = dot(left[...], right, (0, 0))
+        else:
+            right = jnp.concatenate([weights[j, slot] for slot in range(slots)], axis=1)
+            values = dot(left[...], right, (0, 1))
+        store(here, j, values)
+
+    if is_output:
+        tables, stacked = [], []
+        for ref in part_refs:
+            count = ref.shape[1] // 2
+            stacked.append(ref[:, half * count : (half + 1) * count])
+            if sum(values.shape[0] for values in stacked) == pick_ref.shape[0]:
+                tables.append(jnp.concatenate(stacked, axis=0))
+                stacked = []
+        table = jnp.concatenate(tables, axis=1)
+        for copy in tail_copies:
+            copy.wait()
+        store(tail, chunks, dot(table, pick_ref[...], (0, 0)))
+
+    @pl.loop(0, chunks)
+    def _(j):
+        for copy in stores_of(pl.ds(pl.multiple_of(j * step, step), step), j):
+            copy.wait()
+
+    if is_output:
+        for copy in stores_of(tail, chunks):
+            copy.wait()
+
+
+def rows_call(half, lefts, own, copied, parts=None, pick=None, arrived=None):
+    is_output = parts is not None
+    slots = own.shape[0] + 1
+    width, hidden = (own.shape[2], own.shape[1]) if is_output else own.shape[1:]
+    total = sum(a.shape[1] * a.shape[0] for a in lefts) // (2 * slots * hidden)
+    columns = width + (pick.shape[1] if is_output else 0)
+    step = 512
+    chunks = width // step
+    vmem = pl.BlockSpec(memory_space=pltpu.VMEM)
+    operands = [*lefts, own, copied]
+    in_specs = [ANYWHERE] * len(operands)
+    if is_output:
+        operands += [*parts, pick]
+        in_specs += [vmem] * (len(parts) + 1)
+    scratch = [
+        pltpu.VMEM((slots * hidden, total), BF16),
+        pltpu.VMEM((chunks, slots) + ((hidden, step) if is_output else (step, hidden)), BF16),
+        pltpu.VMEM((total, columns), BF16),
+    ]
+    if arrived is not None:
+        operands.append(arrived)
+        in_specs.append(ANYWHERE)
+        scratch.append(pltpu.VMEM((total, columns), BF16))
+    scratch.append(pltpu.SemaphoreType.DMA((len(lefts),)))
+    scratch.append(pltpu.SemaphoreType.DMA((chunks + 1, slots + 1)))
+    outs = 1 if arrived is None else 4
+    scratch.append(pltpu.SemaphoreType.DMA((chunks + 1, outs)))
+    return pl.pallas_call(
+        functools.partial(rows_kernel, half, len(lefts), is_output, arrived is not None),
+        in_specs=in_specs,
+        out_specs=[ANYWHERE] * outs,
+        out_shape=[jax.ShapeDtypeStruct((total // outs, columns), BF16)] * outs,
+        scratch_shapes=scratch,
+        compiler_params=call_params(),
+        cost_estimate=small_cost(),
+        name="output_rows" if is_output else "gradient_rows",
+    )(*operands)
 
 
 class CubeExchange:
@@ -27,34 +486,30 @@
         self.mate = [(i, i ^ 1) for i in range(8)]
 
     def sources(self, me):
-        core = me % 2
-        first = jnp.where(core == 1, 4, 2)
+        first = jnp.where(me % 2 == 1, 4, 2)
         second = 6 - first
         zero = jnp.zeros_like(me)
-        mine = [zero, first, second, zero + 6]
-        mates = [zero + 1, second + 1, first + 1, zero + 7]
-        return jnp.stack([me ^ m for m in mine + mates])
-
-    def gather(self, block):
-        a = lax.ppermute(block, "expert", self.first)
-        b = lax.ppermute(block, "expert", self.second)
-        own_mate = lax.ppermute(block, "expert", self.mate)
-        d = lax.ppermute(a, "expert", self.second)
-        a_mate = lax.ppermute(a, "expert", self.mate)
-        b_mate = lax.ppermute(b, "expert", self.mate)
-        d_mate = lax.ppermute(d, "expert", self.mate)
-        return jnp.concatenate([block, a, b, d, own_mate, a_mate, b_mate, d_mate], axis=0)
-
-    def reduce(self, partial):
-        rows = partial.shape[0] // 8
-        arrived = lax.ppermute(partial[4 * rows :].astype(BF16), "expert", self.mate)
-        mine = partial[: 4 * rows].astype(F32) + arrived.astype(F32)
-        own, a, b, d = (mine[i * rows : (i + 1) * rows] for i in range(4))
-        d_arrived = lax.ppermute(d.astype(BF16), "expert", self.second)
-        b_arrived = lax.ppermute(b.astype(BF16), "expert", self.second)
-        a = a + d_arrived.astype(F32)
-        a_arrived = lax.ppermute(a.astype(BF16), "expert", self.first)
-        return own + a_arrived.astype(F32) + b_arrived.astype(F32)
+        return me ^ jnp.stack(
+            [zero, zero + 1, first, second, second + 1, first + 1, zero + 6, zero + 7]
+        )
+
+    def first_hop(self, block):
+        return lax.ppermute(block, "expert", self.first)
+
+    def far(self, first_block):
+        return lax.ppermute(first_block, "expert", self.second)
+
+    def to_mate(self, block):
+        return lax.ppermute(block, "expert", self.mate)
+
+    def reduce(self, blocks, before_last):
+        own, a, b, d = blocks
+        d_arrived = lax.ppermute(d, "expert", self.second)
+        b_arrived = lax.ppermute(b, "expert", self.second)
+        d_arrived, _ = lax.optimization_barrier((d_arrived, before_last))
+        a = (a.astype(F32) + d_arrived.astype(F32)).astype(BF16)
+        a_arrived = lax.ppermute(a, "expert", self.first)
+        return own.astype(F32) + a_arrived.astype(F32) + b_arrived.astype(F32)
 
 
 class PlainExchange:
@@ -94,7 +549,6 @@
     expert_count = local_count * device_count
     moved_most = 3 * (rows * chosen // expert_count) // 8
     moved_rows = padded(device_count * moved_most, 128)
-    exchange = CubeExchange() if device_count == 8 else PlainExchange(device_count)
 
     column_count = expert_count + device_count
     owner = expert_ids // local_count
@@ -126,13 +580,138 @@
     low_pick = (table_rows[:, None] == wanted[None, :] + column_count).astype(BF16)
     wanted_rank = 2 * column_count + jnp.stack([behind, me])
     rank_pick = (table_rows[:, None] == wanted_rank[None, :]).astype(BF16)
+    to_owner = [(i, (i - 1) % device_count) for i in range(device_count)]
+    hot_slot = copy_expert[(me + 1) % device_count] % local_count
+    own_width = local_count * hidden
+
+    def finish(output_sum, gradient_sum, table_sum):
+        grads = table_sum[:, :column_count] + table_sum[:, column_count : 2 * column_count]
+        gate_grad = jnp.sum(jnp.where(hit, grads[:, None, :], 0.0), axis=2)
+        return output_sum.astype(BF16), gradient_sum.astype(BF16), gate_grad
+
+    replicas = lax.axis_size("dp")
+    if device_count == 8 and local_count == 2 and replicas == 4:
+        exchange = CubeExchange()
+        replica = lax.axis_index("dp")
+        hot = hot_slot.reshape(1).astype(jnp.int32)
+        cold_column = local_count * me + 1 - hot_slot
+        weights = (up_weight, down_weight, copy_up, copy_down)
+        base = jnp.repeat((exchange.sources(me) * moved_most).astype(F32), rows)[None, :]
+        slot_columns = jnp.stack([wanted[slots - 1], wanted[0], wanted[1]])
+        pick_columns = jnp.stack(
+            [wanted[slots - 1], wanted[0], wanted[1], wanted_rank[0], wanted_rank[1], cold_column]
+            + [jnp.int32(-1)] * 10
+        )
+        is_gate = jnp.array([1, 1, 1, 0, 0, 1] + [0] * 10, jnp.int32)
+        pick = (
+            (table_rows[None, :] == pick_columns[:, None])
+            | (
+                (table_rows[None, :] == pick_columns[:, None] + column_count)
+                & (is_gate[:, None] == 1)
+            )
+        ).astype(BF16)
+        part_columns = jnp.stack(
+            [slot_columns, slot_columns + column_count] + [jnp.full((slots,), -1, jnp.int32)] * 14,
+            axis=1,
+        ).reshape(-1)
+        part_pick = (table_rows[None, :] == part_columns[:, None]).astype(BF16)
+
+        own = jnp.concatenate([tokens, cotangent, table], axis=1)
+        own_mate = exchange.to_mate(own)
+        a, b = exchange.first_hop(own), exchange.far(own)
+        replica_pairs = [(0, 1), (1, 0), (2, 3), (3, 2)]
+        other = lax.ppermute(own, "dp", replica_pairs)
+        blocks_1 = [own, own_mate]
+        ends = (2 * rows, 6 * rows)
+        grad_1, active_1, part_1, place_1, packed = hidden_call(
+            hot, blocks_1, weights, pick, base[:, : ends[0]], (COPY, 0, 1), moved_rows
+        )
+        a, b, grad_1 = lax.optimization_barrier((a, b, grad_1))
+        d = exchange.far(a)
+        a_mate = exchange.to_mate(a)
+        other, a_mate = lax.optimization_barrier((other, a_mate))
+        blocks_2 = [a, b, a_mate, exchange.to_mate(b)]
+        grad_2, active_2, part_2, place_2, packed = hidden_call(
+            hot, blocks_2, weights, pick, base[:, ends[0] : ends[1]], (COPY, 0, 1), moved_rows,
+            packed,
+        )
+        grad_2, d = lax.optimization_barrier((grad_2, d))
+        blocks_3 = [d, exchange.to_mate(d)]
+        blocks = blocks_1 + blocks_2 + blocks_3
+
+        other_a = exchange.first_hop(other)
+
+        late_base = base[:, ends[1] :]
+        grad_copy, active_copy, part_copy, place_3, packed = hidden_call(
+            hot, blocks_3, weights, pick, late_base, (COPY,), moved_rows, packed
+        )
+        packed = lax.ppermute(packed, "expert", to_owner)
+        grad_3, active_3, part_3 = hidden_call(hot, blocks_3, weights, pick, late_base, (0, 1))
+        packed, grad_3, other, other_a = lax.optimization_barrier(
+            (packed, grad_3, other, other_a)
+        )
+        other_b = exchange.far(other)
+        other_d = exchange.far(other_a)
+        hot_grads = hot_call(
+            hot, blocks, (1, 1, 0), (grad_1, grad_2, grad_3), (active_1, active_2, active_3),
+            (place_1, place_2, place_3), packed, width, replicas,
+        )
+        hot_sum = lax.psum_scatter(hot_grads, "dp", scatter_dimension=0, tiled=True)[0]
+
+        grad_3, active_3, other_b, _ = lax.optimization_barrier(
+            (grad_3, active_3, other_b, hot_grads)
+        )
+        outputs = ((active_1, active_2, active_copy, active_3), down_weight, copy_down)
+        output_parts = ((part_1, part_2, part_copy, part_3), part_pick)
+        gradients = ((grad_1, grad_2, grad_copy, grad_3), up_weight, copy_up)
+        (mates_gradient,) = rows_call(1, *gradients)
+        active_3, other_d, _ = lax.optimization_barrier((active_3, other_d, mates_gradient))
+        outputs = ((active_1, active_2, active_copy, active_3), down_weight, copy_down)
+        (mates_output,) = rows_call(1, *outputs, *output_parts)
+        arrived_gradient = exchange.to_mate(mates_gradient)
+        arrived_output = exchange.to_mate(mates_output)
+
+        pair_blocks = [other, other_a, other_b, other_d]
+        pair_blocks = pair_blocks + [exchange.to_mate(block) for block in pair_blocks]
+        gradient_rows = rows_call(0, *gradients, None, None, arrived_gradient)
+        *pair_blocks, arrived_output, _ = lax.optimization_barrier(
+            (*pair_blocks, arrived_output, gradient_rows[0])
+        )
+        output_rows = rows_call(0, *outputs, *output_parts, arrived_output)
+
+        *pair_blocks, _, _ = lax.optimization_barrier((*pair_blocks, gradient_rows[0], output_rows[0]))
+        grad_pair, active_pair = hidden_call(hot, pair_blocks, weights, pick, base, (COLD,))
+        even = replica % 2 == 0
+        chunk_pair = jnp.where(even, jnp.array([1, 0]), jnp.array([2, 3])).astype(jnp.int32)
+        near, far = cold_call(
+            hot, chunk_pair, blocks + pair_blocks, (1, 1, 0, None),
+            (grad_1, grad_2, grad_3, grad_pair), (active_1, active_2, active_3, active_pair),
+            width, width // replicas,
+        )
+        gradient_sum = exchange.reduce(gradient_rows, near)
+        output_sum = exchange.reduce(output_rows, near)
+        over = lax.ppermute(far, "dp", [(1, 3), (2, 0)])
+        over, across = lax.optimization_barrier((over, near))
+        across = lax.ppermute(across, "dp", [(1, 2), (2, 1)])
+        inward = lax.ppermute(near, "dp", [(0, 1), (3, 2)])
+        at_end = (replica == 0) | (replica == replicas - 1)
+        kept = jnp.where(at_end, far, jnp.zeros((), BF16))
+        cold_sum = (
+            across.astype(F32) + over.astype(F32) + inward.astype(F32) + kept.astype(F32)
+        ).astype(BF16)
+        hot_first = hot_slot == 0
+        both = jnp.stack(
+            [jnp.where(hot_first, hot_sum, cold_sum), jnp.where(hot_first, cold_sum, hot_sum)]
+        )
+        up_grad = jnp.swapaxes(both[:, 0], 1, 2)
+        down_grad = both[:, 1]
+        return (*finish(output_sum[:, :width], gradient_sum, output_sum[:, width:]), up_grad, down_grad)
+
+    exchange = PlainExchange(device_count)
     up_all = jnp.concatenate([up_weight[i] for i in range(local_count)] + [copy_up[0]], axis=1)
     down_all = jnp.concatenate(
         [down_weight[i] for i in range(local_count)] + [copy_down[0]], axis=0
     )
-    to_owner = [(i, (i - 1) % device_count) for i in range(device_count)]
-    hot_slot = copy_expert[(me + 1) % device_count] % local_count
-    own_width = local_count * hidden
 
     def some_rows(own_block):
         gathered = exchange.gather(own_block)
@@ -194,12 +773,8 @@
         summed = summed.reshape(rows, own.shape[1])
     up_grad = lax.psum_scatter(up_sum.astype(BF16), "dp", scatter_dimension=1, tiled=True)
     down_grad = lax.psum_scatter(down_sum.astype(BF16), "dp", scatter_dimension=2, tiled=True)
-    layer_output = summed[:, :width].astype(BF16)
-    token_grad = summed[:, width : 2 * width].astype(BF16)
-    grads = summed[:, 2 * width : 2 * width + column_count]
-    grads = grads + summed[:, 2 * width + column_count : 2 * width + 2 * column_count]
-    gate_grad = jnp.sum(jnp.where(hit, grads[:, None, :], 0.0), axis=2)
-    return layer_output, token_grad, gate_grad, up_grad, down_grad
+    parts = (summed[:, :width], summed[:, width : 2 * width], summed[:, 2 * width :])
+    return (*finish(*parts), up_grad, down_grad)
 
 
 def solution(mesh):

time: 255 us -> 208 us (0.82)
  Pallas kernels: 0 us -> 91.7 us
  waiting for transfers between devices: 118 us -> 45.3 us
  matrix products: 49.3 us -> 0.14 us
  local copies, waits for them, and re-layouts: 41 us -> 9.13 us
  starting transfers between devices: 8.34 us -> 28.9 us
  other arithmetic: 19.5 us -> 15.8 us
    pallas_call x0 -> x11, Pallas kernels: none -> 91.7 us  [the longest x5 45.6 us: hidden_call(): pl.pallas_call(functools.partial(hidden_kernel, count, slots, packing, wi...]
    reduce_scatter x2 -> x1, waiting for transfers between devices: 57.4 us -> 0.01 us  [local(): lax.psum_scatter(hot_grads, 'dp', scatter_dimension=0, tiled=True)[0]]
    dot_general x15 -> x1, matrix products: 49.3 us -> 0.14 us  [dot(): lax.dot_general(a, b, ((contract[:1], contract[1:]), ((), ())), preferred...]
    ppermute x12 -> x27, starting transfers between devices: 8.26 us -> 28.9 us  [the longest x4 5.06 us: far(): return lax.ppermute(first_block, 'expert', self.second)]
    ppermute x12 -> x27, waiting for transfers between devices: 60.4 us -> 45.2 us  [the longest x4 15.7 us: far(): return lax.ppermute(first_block, 'expert', self.second)]
    unnamed x39 -> x19, local copies, waits for them, and re-layouts: 10.4 us -> 1.77 us
    squeeze x2 -> x0, local copies, waits for them, and re-layouts: 7.56 us -> none  [the longest x1 4.19 us: local(): down_weight[i]]
    reshape x1 -> x0, local copies, waits for them, and re-layouts: 6.09 us -> none  [some_rows(): spread = jnp.repeat(slot_gates, hidden, axis=1)]
  transfers between devices with their start and end apart: 14 -> 28, of which waited for: 8 -> 12; matrix products, arithmetic and copies ran while one was open for 19% -> 7% of each run, Pallas kernels for 0% -> 44%
where the time goes in v2:
time: 208 us; the launch traced here: 207 us
  Pallas kernels  91.7 us (44%)
  waiting for transfers between devices  45.3 us (22%)
  starting transfers between devices  28.9 us (14%)
  between operations  16.3 us (8%)
  other arithmetic  15.8 us (8%)
  local copies, waits for them, and re-layouts  9.13 us (4%)
    pallas_call x5, Pallas kernels, hidden_call(): pl.pallas_call(functools.partial(hidden_kernel, count, slots, packing, wi...  45.6 us
    pallas_call x4, Pallas kernels, rows_call(): pl.pallas_call(functools.partial(rows_kernel, half, len(lefts), is_output...  27.5 us
    ppermute x4, waiting for transfers between devices, far(): return lax.ppermute(first_block, 'expert', self.second)  15.7 us
    ppermute x1, waiting for transfers between devices, local(): inward = lax.ppermute(near, 'dp', [(0, 1), (3, 2)])  11.9 us
    ppermute x1, waiting for transfers between devices, local(): over = lax.ppermute(far, 'dp', [(1, 3), (2, 0)])  11 us
    pallas_call x1, Pallas kernels, hot_call(): pl.pallas_call(functools.partial(hot_kernel, count, firsts, width), in_sp...  9.85 us
    pallas_call x1, Pallas kernels, cold_call(): pl.pallas_call(functools.partial(cold_kernel, count, firsts, width), in_s...  8.74 us
    ppermute x4, starting transfers between devices, far(): return lax.ppermute(first_block, 'expert', self.second)  5.06 us
  transfers between devices with their start and end apart: 28, of which 12 were waited for; matrix products, arithmetic and copies ran while one was open for 7% of the time, Pallas kernels for 44%

profile of v2, /device:TPU:8, one launch (start us, length us, event | category | flops | bytes accessed | tf_op | source)
XLA Modules:
  0.0 207.2 jit_solution(7119918255342714726)
XLA Ops:
  9.3 3.1 %concatenate.16.refs_1_.refs_2_ = bf16[128,4224]{1,0:T(8,128)(2,1)} concatenate(bf16[128,2048]{1,0:T(8,128)(2,1)} %param.13, bf16[128,2048]{1,0:T(8,128)(2,1)} %param.14, bf16[128,24]{1,0:T(8,128)(2,1)S(1)} %copy.39, bf16[128,24]{1,0:T(8,128)(2,1)S(1)} %subtract_convert_fusion, bf16[128,8]{1,0:T(8,128)(2,1)S(1)} %copy.40, bf16[128,72]{1,0:T(8,128)(2,1)S(1)} %broadcast_in_dim.46), dimensions={1} | concatenate | bytes 2162688 | tf_op jit(solution)/shard_map/concatenate | solution.py:619
  20.5 9.4 %hidden_units.5 = (bf16[1152,256]{1,0:T(8,128)(2,1)}, bf16[1152,256]{1,0:T(8,128)(2,1)}, bf16[48,256]{1,0:T(8,128)(2,1)}, f32[8,256]{1,0:T(8,128)}, bf16[768,256]{1,0:T(8,128)(2,1)}) custom-call(s32[1]{0:T(128)} %bitcast.1.refs_0_, bf16[128,4224]{1,0:T(8,128)(2,1)} %concatenate.16.refs_1_.refs_2_, bf16[128,4224]{1,0:T(8,128)(2,1)} %collective-permute-done.refs_2_.refs_3_, ...), custom_call_target="tpu_custom_call" | custom-call | flops 1 | bytes 1 | tf_op jit(solution)/shard_map/hidden_units/pallas_call | solution.py:155
  29.9 8.8 %collective-permute-done.2.refs_2_.refs_4_.refs_5_ = bf16[128,4224]{1,0:T(8,128)(2,1)} collective-permute-done((bf16[128,4224]{1,0:T(8,128)(2,1)}, bf16[128,4224]{1,0:T(8,128)(2,1)}, u32[]{:S(2)}, u32[]{:S(2)}) %collective-permute-start.2) | collective-permute-done | bytes 1081376 | tf_op jit(solution)/shard_map/ppermute | solution.py:500
  43.7 13.3 %hidden_units.6 = (bf16[1152,512]{1,0:T(8,128)(2,1)}, bf16[1152,512]{1,0:T(8,128)(2,1)}, bf16[48,512]{1,0:T(8,128)(2,1)}, f32[8,512]{1,0:T(8,128)}, bf16[768,256]{1,0:T(8,128)(2,1)}) custom-call(s32[1]{0:T(128)} %bitcast.1.refs_0_, bf16[128,4224]{1,0:T(8,128)(2,1)} %collective-permute-done.1.refs_1_.refs_3_.refs_4_, ...), custom_call_target="tpu_custom_call" | custom-call | flops 1 | bytes 1 | tf_op jit(solution)/shard_map/hidden_units/pallas_call | solution.py:155
  60.2 5.8 %hidden_units.7 = (bf16[384,256]{1,0:T(8,128)(2,1)}, bf16[384,256]{1,0:T(8,128)(2,1)}, bf16[16,256]{1,0:T(8,128)(2,1)}, f32[8,256]{1,0:T(8,128)}, bf16[768,256]{1,0:T(8,128)(2,1)}) custom-call(s32[1]{0:T(128)} %bitcast.1.refs_0_, bf16[128,4224]{1,0:T(8,128)(2,1)} %collective-permute-done.6.refs_1_.refs_7_.refs_8_, ...), custom_call_target="tpu_custom_call" | custom-call | flops 1 | bytes 1 | tf_op jit(solution)/shard_map/hidden_units/pallas_call | solution.py:155
  66.0 2.5 %collective-permute-start.8 = (bf16[768,256]{1,0:T(8,128)(2,1)}, bf16[768,256]{1,0:T(8,128)(2,1)}, u32[]{:S(2)}, u32[]{:S(2)}) collective-permute-start(bf16[768,256]{1,0:T(8,128)(2,1)} %get-tuple-element.83), channel_id=1, source_target_pairs={{0,28},{4,0},{8,4},{12,8},{16,12},{20,16},{24,20},{28,24},{1,29},{... | collective-permute-start | bytes 1179656 | tf_op jit(solution)/shard_map/ppermute | solution.py:648
  68.5 7.0 %hidden_units.8 = (bf16[768,256]{1,0:T(8,128)(2,1)}, bf16[768,256]{1,0:T(8,128)(2,1)}, bf16[32,256]{1,0:T(8,128)(2,1)}) custom-call(s32[1]{0:T(128)} %bitcast.1.refs_0_, bf16[128,4224]{1,0:T(8,128)(2,1)} %collective-permute-done.6.refs_1_.refs_7_.refs_8_, bf16[128,4224]{1,0:T(8,128)(2,1)} %collective-permute-done.7.refs_2_.refs_8_.refs_9_, ...), custom_call_target="tpu_custom_call" | custom-call | flops 1 | bytes 1 | tf_op jit(solution)/shard_map/hidden_units/pallas_call | solution.py:155
  78.0 9.9 %hot_weight_grads.1 = bf16[4,2,384,512]{3,2,1,0:T(8,128)(2,1)} custom-call(s32[1]{0:T(128)} %bitcast.1.refs_0_, bf16[128,4224]{1,0:T(8,128)(2,1)} %concatenate.16.refs_1_.refs_2_, bf16[128,4224]{1,0:T(8,128)(2,1)} %collective-permute-done.refs_2_.refs_3_, bf16[128,4224]{1,0:T(8,128)(2,1)} %collective-permute-done.1.refs_1_.refs_3_.refs_4_, ...), custom_call_target="tpu_custom_call" | custom-call | flops 1 | bytes 1 | tf_op jit(solution)/shard_map/hot_weight_grads/pallas_call | solution.py:250
  87.9 3.6 %collective-permute-done.10.refs_3_.refs_12_ = bf16[128,4224]{1,0:T(8,128)(2,1)} collective-permute-done((bf16[128,4224]{1,0:T(8,128)(2,1)}, bf16[128,4224]{1,0:T(8,128)(2,1)}, u32[]{:S(2)}, u32[]{:S(2)}) %collective-permute-start.10) | collective-permute-done | bytes 1081376 | tf_op jit(solution)/shard_map/ppermute | solution.py:500
  91.5 6.2 %gradient_rows.2 = bf16[512,2048]{1,0:T(8,128)(2,1)} custom-call(bf16[1152,256]{1,0:T(8,128)(2,1)} %get-tuple-element.89.refs_9_.refs_0_.refs_18_, bf16[1152,512]{1,0:T(8,128)(2,1)} %get-tuple-element.90.refs_10_.refs_1_.refs_19_, bf16[384,256]{1,0:T(8,128)(2,1)} %get-tuple-element.97.refs_2_, bf16[768,256]{1,0:T(8,128)(2,1)} %get-tuple-element.98.refs_11_.refs_3_.refs_20_, ...), custom_call_target="tpu_custom_call" | custom-call | flops 1 | bytes 1 | tf_op jit(solution)/shard_map/gradient_rows/pallas_call | solution.py:470
  99.7 3.4 %collective-permute-done.11.refs_4_.refs_13_ = bf16[128,4224]{1,0:T(8,128)(2,1)} collective-permute-done((bf16[128,4224]{1,0:T(8,128)(2,1)}, bf16[128,4224]{1,0:T(8,128)(2,1)}, u32[]{:S(2)}, u32[]{:S(2)}) %collective-permute-start.11) | collective-permute-done | bytes 1081376 | tf_op jit(solution)/shard_map/ppermute | solution.py:500
  103.1 7.2 %output_rows.2 = bf16[512,2176]{1,0:T(8,128)(2,1)} custom-call(bf16[1152,256]{1,0:T(8,128)(2,1)} %get-tuple-element.72.refs_12_.refs_0_.refs_22_, bf16[1152,512]{1,0:T(8,128)(2,1)} %get-tuple-element.78.refs_13_.refs_1_.refs_23_, bf16[384,256]{1,0:T(8,128)(2,1)} %get-tuple-element.82.refs_2_, bf16[768,256]{1,0:T(8,128)(2,1)} %get-tuple-element.99.refs_14_.refs_3_.refs_24_, ...), custom_call_target="tpu_custom_call" | custom-call | flops 1 | bytes 1 | tf_op jit(solution)/shard_map/output_rows/pallas_call | solution.py:470
  111.9 6.5 %gradient_rows.3 = (bf16[128,2048]{1,0:T(8,128)(2,1)}, bf16[128,2048]{1,0:T(8,128)(2,1)}, bf16[128,2048]{1,0:T(8,128)(2,1)}, bf16[128,2048]{1,0:T(8,128)(2,1)}) custom-call(bf16[1152,256]{1,0:T(8,128)(2,1)} %get-tuple-element.89.refs_9_.refs_0_.refs_18_, bf16[1152,512]{1,0:T(8,128)(2,1)} %get-tuple-element.90.refs_10_.refs_1_.refs_19_, ...), custom_call_target="tpu_custom_call" | custom-call | flops 1 | bytes 1 | tf_op jit(solution)/shard_map/gradient_rows/pallas_call | solution.py:470
  121.4 7.4 %output_rows.3 = (bf16[128,2176]{1,0:T(8,128)(2,1)}, bf16[128,2176]{1,0:T(8,128)(2,1)}, bf16[128,2176]{1,0:T(8,128)(2,1)}, bf16[128,2176]{1,0:T(8,128)(2,1)}) custom-call(bf16[1152,256]{1,0:T(8,128)(2,1)} %get-tuple-element.72.refs_12_.refs_0_.refs_22_, bf16[1152,512]{1,0:T(8,128)(2,1)} %get-tuple-element.78.refs_13_.refs_1_.refs_23_, ...), custom_call_target="tpu_custom_call" | custom-call | flops 1 | bytes 1 | tf_op jit(solution)/shard_map/output_rows/pallas_call | solution.py:470
  133.6 10.0 %hidden_units.9 = (bf16[384,1024]{1,0:T(8,128)(2,1)}, bf16[384,1024]{1,0:T(8,128)(2,1)}) custom-call(s32[1]{0:T(128)} %bitcast.1.refs_0_, bf16[128,4224]{1,0:T(8,128)(2,1)} %collective-permute-done.3.refs_1_.refs_10_, bf16[128,4224]{1,0:T(8,128)(2,1)} %collective-permute-done.9.refs_2_.refs_11_, bf16[128,4224]{1,0:T(8,128)(2,1)} %collective-permute-done.10.refs_3_.refs_12_, ...), custom_call_target="tpu_custom_call" | custom-call | flops 1 | bytes 1 | tf_op jit(solution)/shard_map/hidden_units/pallas_call | solution.py:155
  143.6 8.7 %cold_weight_grads.1 = (bf16[2,384,512]{2,1,0:T(8,128)(2,1)}, bf16[2,384,512]{2,1,0:T(8,128)(2,1)}) custom-call(s32[1]{0:T(128)} %bitcast.1.refs_0_, s32[2]{0:T(128)} %broadcast_select_fusion.refs_1_, bf16[128,4224]{1,0:T(8,128)(2,1)} %concatenate.16.refs_1_.refs_2_, bf16[128,4224]{1,0:T(8,128)(2,1)} %collective-permute-done.refs_2_.refs_3_, ...), custom_call_target="tpu_custom_call" | custom-call | flops 1 | bytes 1 | tf_op jit(solution)/shard_map/cold_weight_grads/pallas_call | solution.py:304
  152.3 4.9 %collective-permute-start.24 = (bf16[2,384,512]{2,1,0:T(8,128)(2,1)}, bf16[2,384,512]{2,1,0:T(8,128)(2,1)S(1)}, u32[]{:S(2)}, u32[]{:S(2)}) collective-permute-start(bf16[2,384,512]{2,1,0:T(8,128)(2,1)} %get-tuple-element.136), channel_id=1, source_target_pairs={{1,3},{2,0},{5,7},{6,4},{9,11},{10,8},{13,15},{14,12},{17,19},{18,... | collective-permute-start | bytes 2359304 | tf_op jit(solution)/shard_map/ppermute | solution.py:693
  157.2 2.1 %add_convert_fusion.3 = bf16[128,2048]{1,0:T(8,128)(2,1)} fusion(bf16[128,2048]{1,0:T(8,128)(2,1)} %collective-permute-done.21, bf16[128,2048]{1,0:T(8,128)(2,1)} %get-tuple-element.132), kind=kLoop, calls=%fused_computation.9 | loop fusion | flops 1048576 | bytes 1572864 | tf_op jit(solution)/shard_map/convert_element_type | solution.py:510
  159.8 2.0 add_convert_fusion.1
  163.4 11.0 %collective-permute-done.24 = bf16[2,384,512]{2,1,0:T(8,128)(2,1)S(1)} collective-permute-done((bf16[2,384,512]{2,1,0:T(8,128)(2,1)}, bf16[2,384,512]{2,1,0:T(8,128)(2,1)S(1)}, u32[]{:S(2)}, u32[]{:S(2)}) %collective-permute-start.24) | collective-permute-done | bytes 786464 | tf_op jit(solution)/shard_map/ppermute | solution.py:693
  175.7 1.9 collective-permute-start.25
  177.6 2.4 %add_convert_fusion.2 = bf16[128,2048]{1,0:T(8,128)(2,1)} fusion(bf16[128,2048]{1,0:T(8,128)(2,1)} %collective-permute-done.23, bf16[128,2048]{1,0:T(8,128)(2,1)} %collective-permute-done.22, bf16[128,2048]{1,0:T(8,128)(2,1)} %get-tuple-element.106), kind=kLoop, calls=%fused_computation.8 | loop fusion | flops 1572864 | bytes 2097152 | tf_op jit(solution)/shard_map/convert_element_type | solution.py:590
  183.1 11.9 %collective-permute-done.26 = bf16[2,384,512]{2,1,0:T(8,128)(2,1)S(1)} collective-permute-done((bf16[2,384,512]{2,1,0:T(8,128)(2,1)}, bf16[2,384,512]{2,1,0:T(8,128)(2,1)S(1)}, u32[]{:S(2)}, u32[]{:S(2)}) %collective-permute-start.26) | collective-permute-done | bytes 786464 | tf_op jit(solution)/shard_map/ppermute | solution.py:696
  196.3 1.8 fusion.5
  (109 shorter events, 40.0 us)
Async XLA Ops:
  7.2 189.2 %reduce-scatter.2.cloned.1.call-start = ((), (), s32[]{:S(2)}) async-start(), calls=%async_computation.1 | async-start | bytes 3932160 | tf_op jit(solution)/shard_map/reduce_scatter | solution.py:659
  12.3 8.2 %collective-permute-start = (bf16[128,4224]{1,0:T(8,128)(2,1)}, bf16[128,4224]{1,0:T(8,128)(2,1)}, u32[]{:S(2)}, u32[]{:S(2)}) collective-permute-start(bf16[128,4224]{1,0:T(8,128)(2,1)} %concatenate.16.refs_1_.refs_2_), channel_id=1, source_target_pairs={{0,4},{4,0},{8,12},{12,8},{16,20},{20,16},{24,28},{28,24},{1,5},{5... | collective-permute-start | bytes 3244040 | tf_op jit(solution)/shard_map/ppermute | solution.py:503
  12.3 26.3 %collective-permute-start.2 = (bf16[128,4224]{1,0:T(8,128)(2,1)}, bf16[128,4224]{1,0:T(8,128)(2,1)}, u32[]{:S(2)}, u32[]{:S(2)}) collective-permute-start(bf16[128,4224]{1,0:T(8,128)(2,1)} %concatenate.16.refs_1_.refs_2_), channel_id=1, source_target_pairs={{0,16},{4,12},{8,24},{12,4},{16,0},{20,28},{24,8},{28,20},{1,17},{... | collective-permute-start | bytes 3244040 | tf_op jit(solution)/shard_map/ppermute | solution.py:500
  13.8 25.1 %collective-permute-start.1 = (bf16[128,4224]{1,0:T(8,128)(2,1)}, bf16[128,4224]{1,0:T(8,128)(2,1)}, u32[]{:S(2)}, u32[]{:S(2)}) collective-permute-start(bf16[128,4224]{1,0:T(8,128)(2,1)} %concatenate.16.refs_1_.refs_2_), channel_id=1, source_target_pairs={{0,8},{4,20},{8,0},{12,28},{16,24},{20,4},{24,16},{28,12},{1,9},{5... | collective-permute-start | bytes 3244040 | tf_op jit(solution)/shard_map/ppermute | solution.py:497
  15.3 26.9 %collective-permute-start.3 = (bf16[128,4224]{1,0:T(8,128)(2,1)}, bf16[128,4224]{1,0:T(8,128)(2,1)}, u32[]{:S(2)}, u32[]{:S(2)}) collective-permute-start(bf16[128,4224]{1,0:T(8,128)(2,1)} %concatenate.16.refs_1_.refs_2_), channel_id=1, source_target_pairs={{0,1},{1,0},{2,3},{3,2},{4,5},{5,4},{6,7},{7,6},{8,9},{9,8},{10,11... | collective-permute-start | bytes 3244040 | tf_op jit(solution)/shard_map/ppermute | solution.py:623
  39.5 17.6 %collective-permute-start.6 = (bf16[128,4224]{1,0:T(8,128)(2,1)}, bf16[128,4224]{1,0:T(8,128)(2,1)}, u32[]{:S(2)}, u32[]{:S(2)}) collective-permute-start(bf16[128,4224]{1,0:T(8,128)(2,1)} %collective-permute-done.1.refs_1_.refs_3_.refs_4_), channel_id=1, source_target_pairs={{0,16},{4,12},{8,24},{12,4},{16,0},{20,28},{24,8},{28,20},{1,17},{... | collective-permute-start | bytes 3244040 | tf_op jit(solution)/shard_map/ppermute | solution.py:500
  57.5 18.0 %collective-permute-start.9 = (bf16[128,4224]{1,0:T(8,128)(2,1)}, bf16[128,4224]{1,0:T(8,128)(2,1)}, u32[]{:S(2)}, u32[]{:S(2)}) collective-permute-start(bf16[128,4224]{1,0:T(8,128)(2,1)} %collective-permute-done.3.refs_1_.refs_10_), channel_id=1, source_target_pairs={{0,8},{4,20},{8,0},{12,28},{16,24},{20,4},{24,16},{28,12},{1,9},{5... | collective-permute-start | bytes 3244040 | tf_op jit(solution)/shard_map/ppermute | solution.py:497
  66.0 10.0 %collective-permute-start.8 = (bf16[768,256]{1,0:T(8,128)(2,1)}, bf16[768,256]{1,0:T(8,128)(2,1)}, u32[]{:S(2)}, u32[]{:S(2)}) collective-permute-start(bf16[768,256]{1,0:T(8,128)(2,1)} %get-tuple-element.83), channel_id=1, source_target_pairs={{0,28},{4,0},{8,4},{12,8},{16,12},{20,16},{24,20},{28,24},{1,29},{... | collective-permute-start | bytes 1179656 | tf_op jit(solution)/shard_map/ppermute | solution.py:648
  76.0 15.5 %collective-permute-start.10 = (bf16[128,4224]{1,0:T(8,128)(2,1)}, bf16[128,4224]{1,0:T(8,128)(2,1)}, u32[]{:S(2)}, u32[]{:S(2)}) collective-permute-start(bf16[128,4224]{1,0:T(8,128)(2,1)} %collective-permute-done.3.refs_1_.refs_10_), channel_id=1, source_target_pairs={{0,16},{4,12},{8,24},{12,4},{16,0},{20,28},{24,8},{28,20},{1,17},{... | collective-permute-start | bytes 3244040 | tf_op jit(solution)/shard_map/ppermute | solution.py:500
  77.5 25.5 %collective-permute-start.11 = (bf16[128,4224]{1,0:T(8,128)(2,1)}, bf16[128,4224]{1,0:T(8,128)(2,1)}, u32[]{:S(2)}, u32[]{:S(2)}) collective-permute-start(bf16[128,4224]{1,0:T(8,128)(2,1)} %collective-permute-done.9.refs_2_.refs_11_), channel_id=1, source_target_pairs={{0,16},{4,12},{8,24},{12,4},{16,0},{20,28},{24,8},{28,20},{1,17},{... | collective-permute-start | bytes 3244040 | tf_op jit(solution)/shard_map/ppermute | solution.py:500
  97.7 13.8 %collective-permute-start.17 = (bf16[512,2048]{1,0:T(8,128)(2,1)}, bf16[512,2048]{1,0:T(8,128)(2,1)}, u32[]{:S(2)}, u32[]{:S(2)}) collective-permute-start(bf16[512,2048]{1,0:T(8,128)(2,1)} %gradient_rows.2), channel_id=1, source_target_pairs={{0,4},{4,0},{8,12},{12,8},{16,20},{20,16},{24,28},{28,24},{1,5},{5... | collective-permute-start | bytes 6291464 | tf_op jit(solution)/shard_map/ppermute | solution.py:503
  110.3 11.1 %collective-permute-start.16 = (bf16[512,2176]{1,0:T(8,128)(2,1)}, bf16[512,2176]{1,0:T(8,128)(2,1)}, u32[]{:S(2)}, u32[]{:S(2)}) collective-permute-start(bf16[512,2176]{1,0:T(8,128)(2,1)} %output_rows.2), channel_id=1, source_target_pairs={{0,4},{4,0},{8,12},{12,8},{16,20},{20,16},{24,28},{28,24},{1,5},{5... | collective-permute-start | bytes 6684680 | tf_op jit(solution)/shard_map/ppermute | solution.py:503
  111.0 8.7 %collective-permute-start.13 = (bf16[128,4224]{1,0:T(8,128)(2,1)}, bf16[128,4224]{1,0:T(8,128)(2,1)}, u32[]{:S(2)}, u32[]{:S(2)}) collective-permute-start(bf16[128,4224]{1,0:T(8,128)(2,1)} %collective-permute-done.9.refs_2_.refs_11_), channel_id=1, source_target_pairs={{0,4},{4,0},{8,12},{12,8},{16,20},{20,16},{24,28},{28,24},{1,5},{5... | collective-permute-start | bytes 3244040 | tf_op jit(solution)/shard_map/ppermute | solution.py:503
  111.4 8.4 %collective-permute-start.14 = (bf16[128,4224]{1,0:T(8,128)(2,1)}, bf16[128,4224]{1,0:T(8,128)(2,1)}, u32[]{:S(2)}, u32[]{:S(2)}) collective-permute-start(bf16[128,4224]{1,0:T(8,128)(2,1)} %collective-permute-done.10.refs_3_.refs_12_), channel_id=1, source_target_pairs={{0,4},{4,0},{8,12},{12,8},{16,20},{20,16},{24,28},{28,24},{1,5},{5... | collective-permute-start | bytes 3244040 | tf_op jit(solution)/shard_map/ppermute | solution.py:503
  111.5 9.9 %collective-permute-start.15 = (bf16[128,4224]{1,0:T(8,128)(2,1)}, bf16[128,4224]{1,0:T(8,128)(2,1)}, u32[]{:S(2)}, u32[]{:S(2)}) collective-permute-start(bf16[128,4224]{1,0:T(8,128)(2,1)} %collective-permute-done.11.refs_4_.refs_13_), channel_id=1, source_target_pairs={{0,4},{4,0},{8,12},{12,8},{16,20},{20,16},{24,28},{28,24},{1,5},{5... | collective-permute-start | bytes 3244040 | tf_op jit(solution)/shard_map/ppermute | solution.py:503
  118.5 38.7 %collective-permute-start.21 = (bf16[128,2048]{1,0:T(8,128)(2,1)}, bf16[128,2048]{1,0:T(8,128)(2,1)}, u32[]{:S(2)}, u32[]{:S(2)}) collective-permute-start(bf16[128,2048]{1,0:T(8,128)(2,1)} %get-tuple-element.133), channel_id=1, source_target_pairs={{0,16},{4,12},{8,24},{12,4},{16,0},{20,28},{24,8},{28,20},{1,17},{... | collective-permute-start | bytes 1572872 | tf_op jit(solution)/shard_map/ppermute | solution.py:507
  128.8 30.9 %collective-permute-start.18 = (bf16[128,2176]{1,0:T(8,128)(2,1)}, bf16[128,2176]{1,0:T(8,128)(2,1)}, u32[]{:S(2)}, u32[]{:S(2)}) collective-permute-start(bf16[128,2176]{1,0:T(8,128)(2,1)} %get-tuple-element.110), channel_id=1, source_target_pairs={{0,16},{4,12},{8,24},{12,4},{16,0},{20,28},{24,8},{28,20},{1,17},{... | collective-permute-start | bytes 1671176 | tf_op jit(solution)/shard_map/ppermute | solution.py:507
  131.5 44.1 %collective-permute-start.23 = (bf16[128,2048]{1,0:T(8,128)(2,1)}, bf16[128,2048]{1,0:T(8,128)(2,1)}, u32[]{:S(2)}, u32[]{:S(2)}) collective-permute-start(bf16[128,2048]{1,0:T(8,128)(2,1)} %get-tuple-element.135), channel_id=1, source_target_pairs={{0,16},{4,12},{8,24},{12,4},{16,0},{20,28},{24,8},{28,20},{1,17},{... | collective-permute-start | bytes 1572872 | tf_op jit(solution)/shard_map/ppermute | solution.py:508
  132.1 47.9 %collective-permute-start.20 = (bf16[128,2176]{1,0:T(8,128)(2,1)}, bf16[128,2176]{1,0:T(8,128)(2,1)}, u32[]{:S(2)}, u32[]{:S(2)}) collective-permute-start(bf16[128,2176]{1,0:T(8,128)(2,1)} %get-tuple-element.131), channel_id=1, source_target_pairs={{0,16},{4,12},{8,24},{12,4},{16,0},{20,28},{24,8},{28,20},{1,17},{... | collective-permute-start | bytes 1671176 | tf_op jit(solution)/shard_map/ppermute | solution.py:508
  152.3 22.0 %collective-permute-start.24 = (bf16[2,384,512]{2,1,0:T(8,128)(2,1)}, bf16[2,384,512]{2,1,0:T(8,128)(2,1)S(1)}, u32[]{:S(2)}, u32[]{:S(2)}) collective-permute-start(bf16[2,384,512]{2,1,0:T(8,128)(2,1)} %get-tuple-element.136), channel_id=1, source_target_pairs={{1,3},{2,0},{5,7},{6,4},{9,11},{10,8},{13,15},{14,12},{17,19},{18,... | collective-permute-start | bytes 2359304 | tf_op jit(solution)/shard_map/ppermute | solution.py:693
  159.4 18.3 %collective-permute-start.22 = (bf16[128,2048]{1,0:T(8,128)(2,1)}, bf16[128,2048]{1,0:T(8,128)(2,1)}, u32[]{:S(2)}, u32[]{:S(2)}) collective-permute-start(bf16[128,2048]{1,0:T(8,128)(2,1)} %add_convert_fusion.3), channel_id=1, source_target_pairs={{0,8},{4,20},{8,0},{12,28},{16,24},{20,4},{24,16},{28,12},{1,9},{5... | collective-permute-start | bytes 1572872 | tf_op jit(solution)/shard_map/ppermute | solution.py:511
  161.8 18.3 %collective-permute-start.19 = (bf16[128,2176]{1,0:T(8,128)(2,1)}, bf16[128,2176]{1,0:T(8,128)(2,1)}, u32[]{:S(2)}, u32[]{:S(2)}) collective-permute-start(bf16[128,2176]{1,0:T(8,128)(2,1)} %add_convert_fusion.1), channel_id=1, source_target_pairs={{0,8},{4,20},{8,0},{12,28},{16,24},{20,4},{24,16},{28,12},{1,9},{5... | collective-permute-start | bytes 1671176 | tf_op jit(solution)/shard_map/ppermute | solution.py:511
  174.4 20.6 %collective-permute-start.26 = (bf16[2,384,512]{2,1,0:T(8,128)(2,1)}, bf16[2,384,512]{2,1,0:T(8,128)(2,1)S(1)}, u32[]{:S(2)}, u32[]{:S(2)}) collective-permute-start(bf16[2,384,512]{2,1,0:T(8,128)(2,1)} %get-tuple-element.137), channel_id=1, source_target_pairs={{0,1},{3,2},{4,5},{7,6},{8,9},{11,10},{12,13},{15,14},{16,17},{19,... | collective-permute-start | bytes 2359304 | tf_op jit(solution)/shard_map/ppermute | solution.py:696
  175.7 20.6 %collective-permute-start.25 = (bf16[2,384,512]{2,1,0:T(8,128)(2,1)}, bf16[2,384,512]{2,1,0:T(8,128)(2,1)S(1)}, u32[]{:S(2)}, u32[]{:S(2)}) collective-permute-start(bf16[2,384,512]{2,1,0:T(8,128)(2,1)} %get-tuple-element.137), channel_id=1, source_target_pairs={{1,2},{2,1},{5,6},{6,5},{9,10},{10,9},{13,14},{14,13},{17,18},{18,... | collective-permute-start | bytes 2359304 | tf_op jit(solution)/shard_map/ppermute | solution.py:695
  (13 other events, 80.1 us)
Sparse Core Ops, SparseCore 0:
  98.6 60.4 reduce-scatter.1

commit v3 on v2

--- a/solution.py
+++ b/solution.py
@@ -32,8 +32,12 @@
     return pltpu.CompilerParams(vmem_limit_bytes=VMEM_LIMIT)
 
 
-def small_cost():
-    return pl.CostEstimate(flops=1, bytes_accessed=1, transcendentals=0)
+def small_cost(microseconds=0):
+    return pl.CostEstimate(
+        flops=1 + int(microseconds * 1e9),
+        bytes_accessed=1 + int(microseconds * 3e6),
+        transcendentals=0,
+    )
 
 
 class Fetches:
@@ -90,24 +94,27 @@
     for number in range(1, len(slots)):
         for copy in slot_copies(number, slots[number]):
             copy.start()
-    for copy in block_copies:
-        copy.wait()
-    gates[...] = dot(pick_ref[...], together[:, 2 * width :], (1, 1))
-    if packing:
-        ranks = gates[SERVED_RANK : OWNED_RANK + 1, :]
-        place = jnp.where(ranks > 0.5, base_ref[...] + ranks - 1.0, -1.0)
-        place_ref[...] = jnp.concatenate([place, jnp.zeros((6, place.shape[1]), F32)], axis=0)
     first_gate = 0 if slots[0] == COPY else (COLD_GATE if slots[0] == COLD else 1)
 
-    @pl.loop(0, len(slots))
-    def _(number):
-        for copy in slot_copies(number, slots[-1]):
+    for number, slot in enumerate(slots):
+        for copy in slot_copies(number, slot):
             copy.wait()
-        to = pl.ds(pl.multiple_of(number * hidden, hidden), hidden)
+        to = pl.ds(number * hidden, hidden)
 
         for g in range(blocks // 2):
             here = slice(g * group, (g + 1) * group)
-            gate = gates[pl.ds(first_gate + number, 1), here]
+            if number == 0:
+                for copy in block_copies[2 * g : 2 * g + 2]:
+                    copy.wait()
+                found = dot(pick_ref[...], together[here, 2 * width :], (1, 1))
+                gates[:, here] = found
+                if packing:
+                    ranks = found[SERVED_RANK : OWNED_RANK + 1]
+                    place = jnp.where(ranks > 0.5, base_ref[:, here] + ranks - 1.0, -1.0)
+                    place_ref[:, here] = jnp.concatenate(
+                        [place, jnp.zeros((6, group), F32)], axis=0
+                    )
+            gate = gates[first_gate + number : first_gate + number + 1, here]
             linear = dot(ups[number], together[here, :width], (0, 1))
             raw_grad = dot(downs[number], together[here, width : 2 * width], (1, 1))
             sigma = 0.5 * jnp.tanh(0.5 * linear) + 0.5
@@ -115,7 +122,7 @@
             if part_ref is not None:
                 part = jnp.sum(active * raw_grad, axis=0, keepdims=True)
                 part_high, part_low = split_two(part)
-                part_ref[pl.ds(pl.multiple_of(16 * number, 16), 16), here] = jnp.concatenate(
+                part_ref[pl.ds(16 * number, 16), here] = jnp.concatenate(
                     [part_high, part_low, jnp.zeros((14, group), BF16)], axis=0
                 )
             active_ref[to, here] = (gate * active).astype(BF16)
@@ -166,7 +173,7 @@
             pltpu.SemaphoreType.DMA((count,)),
         ],
         compiler_params=call_params(),
-        cost_estimate=small_cost(),
+        cost_estimate=small_cost(2 if COLD in slots else 0),
         name="hidden_units",
     )(*operands)
 
@@ -315,167 +322,243 @@
             pltpu.SemaphoreType.DMA((2, 2, count)),
         ],
         compiler_params=call_params(),
-        cost_estimate=small_cost(),
+        cost_estimate=small_cost(2),
         name="cold_weight_grads",
     )(hot, chunk_pair, *blocks, *grads, *actives)
 
 
-def rows_kernel(half, pieces, is_output, with_arrived, *refs):
-    left_refs, refs = refs[:pieces], refs[pieces:]
-    own_ref, copy_ref, *refs = refs
-    part_refs, pick_ref = (), None
-    if is_output:
-        part_refs, pick_ref, refs = refs[:pieces], refs[pieces], refs[pieces + 1 :]
-    arrived_ref = refs.pop(0) if with_arrived else None
-    outs = 4 if with_arrived else 1
-    out_refs, refs = refs[:outs], refs[outs:]
-    left, weights, out, *refs = refs
-    arrived = refs.pop(0) if with_arrived else None
-    sems, chunk_sems, out_sems = refs
-    hidden = own_ref.shape[1] if is_output else own_ref.shape[2]
-    width = own_ref.shape[2] if is_output else own_ref.shape[1]
-    step = weights.shape[3] if is_output else weights.shape[2]
-    chunks = width // step
-    slots = weights.shape[1]
-    fetches = Fetches(sems)
-    of_left = []
-    row, column = 0, 0
-    for ref in left_refs:
-        count = ref.shape[1] // 2
-        of_left.append(
-            fetches.add(
+def place_kernel(flags_ref, hot_ref, moved_ref, kept_ref, across_ref, up_ref, down_ref):
+    hot_slot = flags_ref[0]
+    up_ref[hot_slot] = hot_ref[0].T
+    down_ref[hot_slot] = hot_ref[1]
+
+    def place_cold(other_ref):
+        up = (moved_ref[0].astype(F32) + other_ref[0].astype(F32)).astype(BF16)
+        up_ref[1 - hot_slot] = up.T
+        down = (moved_ref[1].astype(F32) + other_ref[1].astype(F32)).astype(BF16)
+        down_ref[1 - hot_slot] = down
+
+    at_end = flags_ref[1] == 1
+    pl.when(at_end)(lambda: place_cold(kept_ref))
+    pl.when(jnp.logical_not(at_end))(lambda: place_cold(across_ref))
+
+
+def place_call(flags, hot_sum, moved, kept, across):
+    hidden, chunk = hot_sum.shape[1:]
+    vmem = pl.BlockSpec(memory_space=pltpu.VMEM)
+    return pl.pallas_call(
+        place_kernel,
+        in_specs=[pl.BlockSpec(memory_space=pltpu.SMEM)] + [vmem] * 4,
+        out_specs=[vmem, vmem],
+        out_shape=[
+            jax.ShapeDtypeStruct((2, chunk, hidden), BF16),
+            jax.ShapeDtypeStruct((2, hidden, chunk), BF16),
+        ],
+        compiler_params=call_params(),
+        cost_estimate=small_cost(),
+        name="place_weight_grads",
+    )(flags, hot_sum, moved, kept, across)
+
+
+class RowSums:
+    def __init__(self, half, lefts, own, copied, outs, scratch, parts=None, pick=None, arrived=None):
+        self.half, self.own, self.copied, self.outs = half, own, copied, outs
+        self.parts, self.pick, self.arrived_ref = parts, pick, arrived
+        self.is_output = parts is not None
+        self.left, self.weights, self.out, *rest = scratch
+        self.arrived = rest.pop(0) if arrived is not None else None
+        left_sems, self.chunk_sems, self.out_sems = rest
+        self.hidden, self.width = own.shape[1:] if self.is_output else own.shape[:0:-1]
+        self.step = self.weights.shape[3] if self.is_output else self.weights.shape[2]
+        self.chunks, self.slots = self.weights.shape[:2]
+        self.tail = pl.ds(self.width, self.out.shape[1] - self.width)
+        self.of_left = Fetches(left_sems)
+        row, column = 0, 0
+        for ref in lefts:
+            count = ref.shape[1] // 2
+            self.of_left.add(
                 ref.at[:, pl.ds(half * count, count)],
-                left.at[pl.ds(row, ref.shape[0]), pl.ds(column, count)],
+                self.left.at[pl.ds(row, ref.shape[0]), pl.ds(column, count)],
             )
-        )
-        row += ref.shape[0]
-        if row == left.shape[0]:
-            row, column = 0, column + count
-    fetches.start()
-    tail = pl.ds(width, out.shape[1] - width)
-
-    def chunk_copies(j):
-        here = pl.ds(pl.multiple_of(j * step, step), step)
+            row += ref.shape[0]
+            if row == self.left.shape[0]:
+                row, column = 0, column + count
+
+    def columns(self, j):
+        return pl.ds(pl.multiple_of(j * self.step, self.step), self.step)
+
+    def chunk_copies(self, j):
+        here = self.columns(j)
         found = []
-        for slot in range(slots):
-            source = copy_ref.at[0] if slot == 0 else own_ref.at[slot - 1]
-            source = source.at[:, here] if is_output else source.at[here]
-            found.append(
-                pltpu.make_async_copy(source, weights.at[j, slot], chunk_sems.at[j, slot])
-            )
-        if with_arrived:
+        for slot in range(self.slots):
+            source = self.copied.at[0] if slot == 0 else self.own.at[slot - 1]
+            source = source.at[:, here] if self.is_output else source.at[here]
             found.append(
                 pltpu.make_async_copy(
-                    arrived_ref.at[:, here], arrived.at[:, here], chunk_sems.at[j, slots]
+                    source, self.weights.at[j, slot], self.chunk_sems.at[j, slot]
+                )
+            )
+        if self.arrived is not None:
+            found.append(
+                pltpu.make_async_copy(
+                    self.arrived_ref.at[:, here],
+                    self.arrived.at[:, here],
+                    self.chunk_sems.at[j, self.slots],
                 )
             )
         return found
 
-    def stores_of(here, number):
-        rows = out.shape[0] // outs
+    def tail_copies(self):
+        if self.arrived is None or not self.is_output:
+            return []
         return [
             pltpu.make_async_copy(
-                out.at[pl.ds(i * rows, rows), here], ref.at[:, here], out_sems.at[number, i]
+                self.arrived_ref.at[:, self.tail],
+                self.arrived.at[:, self.tail],
+                self.chunk_sems.at[self.chunks, 0],
             )
-            for i, ref in enumerate(out_refs)
         ]
 
-    tail_copies = []
-    if with_arrived and is_output:
-        tail_copies.append(
+    def stores(self, here, number):
+        rows = self.out.shape[0] // len(self.outs)
+        return [
             pltpu.make_async_copy(
-                arrived_ref.at[:, tail], arrived.at[:, tail], chunk_sems.at[chunks, 0]
+                self.out.at[pl.ds(i * rows, rows), here],
+                ref.at[:, here],
+                self.out_sems.at[number, i],
             )
-        )
-
-    @pl.loop(0, chunks)
-    def _(j):
-        for copy in chunk_copies(j):
+            for i, ref in enumerate(self.outs)
+        ]
+
+    def store(self, here, number, values):
+        if self.arrived is not None:
+            values = values + self.arrived[:, here].astype(F32)
+        self.out[:, here] = values.astype(BF16)
+        for copy in self.stores(here, number):
             copy.start()
 
-    for copy in tail_copies:
-        copy.start()
-    fetches.wait(of_left)
-
-    def store(here, number, values):
-        if with_arrived:
-            values = values + arrived[:, here].astype(F32)
-        out[:, here] = values.astype(BF16)
-        for copy in stores_of(here, number):
+    def start(self):
+        self.of_left.start()
+
+        @pl.loop(0, self.chunks)
+        def _(j):
+            for copy in self.chunk_copies(j):
+                copy.start()
+
+        for copy in self.tail_copies():
             copy.start()
 
-    @pl.loop(0, chunks)
-    def _(j):
-        here = pl.ds(pl.multiple_of(j * step, step), step)
-        for copy in chunk_copies(j):
-            copy.wait()
-        if is_output:
-            right = weights[j].reshape(slots * hidden, step)
-            values = dot(left[...], right, (0, 0))
-        else:
-            right = jnp.concatenate([weights[j, slot] for slot in range(slots)], axis=1)
-            values = dot(left[...], right, (0, 1))
-        store(here, j, values)
-
-    if is_output:
-        tables, stacked = [], []
-        for ref in part_refs:
-            count = ref.shape[1] // 2
-            stacked.append(ref[:, half * count : (half + 1) * count])
-            if sum(values.shape[0] for values in stacked) == pick_ref.shape[0]:
-                tables.append(jnp.concatenate(stacked, axis=0))
-                stacked = []
-        table = jnp.concatenate(tables, axis=1)
-        for copy in tail_copies:
-            copy.wait()
-        store(tail, chunks, dot(table, pick_ref[...], (0, 0)))
-
-    @pl.loop(0, chunks)
-    def _(j):
-        for copy in stores_of(pl.ds(pl.multiple_of(j * step, step), step), j):
-            copy.wait()
-
-    if is_output:
-        for copy in stores_of(tail, chunks):
-            copy.wait()
-
-
-def rows_call(half, lefts, own, copied, parts=None, pick=None, arrived=None):
-    is_output = parts is not None
-    slots = own.shape[0] + 1
-    width, hidden = (own.shape[2], own.shape[1]) if is_output else own.shape[1:]
-    total = sum(a.shape[1] * a.shape[0] for a in lefts) // (2 * slots * hidden)
-    columns = width + (pick.shape[1] if is_output else 0)
+    def compute(self):
+        self.of_left.wait(range(len(self.of_left.copies)))
+
+        @pl.loop(0, self.chunks)
+        def _(j):
+            for copy in self.chunk_copies(j):
+                copy.wait()
+            if self.is_output:
+                right = self.weights[j].reshape(self.slots * self.hidden, self.step)
+                values = dot(self.left[...], right, (0, 0))
+            else:
+                right = jnp.concatenate(
+                    [self.weights[j, slot] for slot in range(self.slots)], axis=1
+                )
+                values = dot(self.left[...], right, (0, 1))
+            self.store(self.columns(j), j, values)
+
+        if self.is_output:
+            tables, stacked = [], []
+            for ref in self.parts:
+                count = ref.shape[1] // 2
+                stacked.append(ref[:, self.half * count : (self.half + 1) * count])
+                if sum(values.shape[0] for values in stacked) == self.pick.shape[0]:
+                    tables.append(jnp.concatenate(stacked, axis=0))
+                    stacked = []
+            table = jnp.concatenate(tables, axis=1)
+            for copy in self.tail_copies():
+                copy.wait()
+            self.store(self.tail, self.chunks, dot(table, self.pick[...], (0, 0)))
+
+    def finish(self):
+        @pl.loop(0, self.chunks)
+        def _(j):
+            for copy in self.stores(self.columns(j), j):
+                copy.wait()
+
+        if self.is_output:
+            for copy in self.stores(self.tail, self.chunks):
+                copy.wait()
+
+
+def rows_kernel(half, pieces, with_arrived, *refs):
+    def take(count):
+        nonlocal refs
+        found, refs = refs[:count], refs[count:]
+        return found
+
+    grads, actives, parts = take(pieces), take(pieces), take(pieces)
+    up, copy_up, down, copy_down, pick = take(5)
+    arrived = take(2) if with_arrived else (None, None)
+    outs = 4 if with_arrived else 1
+    gradient_outs, output_outs = take(outs), take(outs)
+    scratch = 7 if with_arrived else 6
+    gradient = RowSums(
+        half, grads, up, copy_up, gradient_outs, take(scratch), arrived=arrived[0]
+    )
+    output = RowSums(
+        half, actives, down, copy_down, output_outs, take(scratch), parts, pick, arrived[1]
+    )
+    for part in (gradient, output):
+        part.start()
+    for part in (gradient, output):
+        part.compute()
+    for part in (gradient, output):
+        part.finish()
+
+
+def rows_call(half, grads, actives, parts, weights, pick, arrived=()):
+    own_up, own_down, copy_up, copy_down = weights
+    slots = own_up.shape[0] + 1
+    width, hidden = own_up.shape[1:]
+    total = sum(a.shape[1] * a.shape[0] for a in grads) // (2 * slots * hidden)
     step = 512
     chunks = width // step
+    outs = 4 if arrived else 1
     vmem = pl.BlockSpec(memory_space=pltpu.VMEM)
-    operands = [*lefts, own, copied]
-    in_specs = [ANYWHERE] * len(operands)
-    if is_output:
-        operands += [*parts, pick]
-        in_specs += [vmem] * (len(parts) + 1)
-    scratch = [
-        pltpu.VMEM((slots * hidden, total), BF16),
-        pltpu.VMEM((chunks, slots) + ((hidden, step) if is_output else (step, hidden)), BF16),
-        pltpu.VMEM((total, columns), BF16),
-    ]
-    if arrived is not None:
-        operands.append(arrived)
-        in_specs.append(ANYWHERE)
-        scratch.append(pltpu.VMEM((total, columns), BF16))
-    scratch.append(pltpu.SemaphoreType.DMA((len(lefts),)))
-    scratch.append(pltpu.SemaphoreType.DMA((chunks + 1, slots + 1)))
-    outs = 1 if arrived is None else 4
-    scratch.append(pltpu.SemaphoreType.DMA((chunks + 1, outs)))
+    operands = [*grads, *actives, *parts, own_up, copy_up, own_down, copy_down, pick, *arrived]
+    in_specs = (
+        [ANYWHERE] * (2 * len(grads))
+        + [vmem] * len(parts)
+        + [ANYWHERE] * 4
+        + [vmem]
+        + [ANYWHERE] * len(arrived)
+    )
+    out_shape, scratch = [], []
+    for columns, tile in (
+        (width, (step, hidden)),
+        (width + pick.shape[1], (hidden, step)),
+    ):
+        out_shape += [jax.ShapeDtypeStruct((total // outs, columns), BF16)] * outs
+        scratch += [
+            pltpu.VMEM((slots * hidden, total), BF16),
+            pltpu.VMEM((chunks, slots) + tile, BF16),
+            pltpu.VMEM((total, columns), BF16),
+        ]
+        if arrived:
+            scratch.append(pltpu.VMEM((total, columns), BF16))
+        scratch += [
+            pltpu.SemaphoreType.DMA((len(grads),)),
+            pltpu.SemaphoreType.DMA((chunks + 1, slots + 1)),
+            pltpu.SemaphoreType.DMA((chunks + 1, outs)),
+        ]
     return pl.pallas_call(
-        functools.partial(rows_kernel, half, len(lefts), is_output, arrived is not None),
+        functools.partial(rows_kernel, half, len(grads), bool(arrived)),
         in_specs=in_specs,
-        out_specs=[ANYWHERE] * outs,
-        out_shape=[jax.ShapeDtypeStruct((total // outs, columns), BF16)] * outs,
+        out_specs=[ANYWHERE] * len(out_shape),
+        out_shape=out_shape,
         scratch_shapes=scratch,
         compiler_params=call_params(),
         cost_estimate=small_cost(),
-        name="output_rows" if is_output else "gradient_rows",
+        name="row_sums",
     )(*operands)
 
 
@@ -502,11 +585,10 @@
     def to_mate(self, block):
         return lax.ppermute(block, "expert", self.mate)
 
-    def reduce(self, blocks, before_last):
+    def reduce(self, blocks):
         own, a, b, d = blocks
         d_arrived = lax.ppermute(d, "expert", self.second)
         b_arrived = lax.ppermute(b, "expert", self.second)
-        d_arrived, _ = lax.optimization_barrier((d_arrived, before_last))
         a = (a.astype(F32) + d_arrived.astype(F32)).astype(BF16)
         a_arrived = lax.ppermute(a, "expert", self.first)
         return own.astype(F32) + a_arrived.astype(F32) + b_arrived.astype(F32)
@@ -661,50 +743,38 @@
         grad_3, active_3, other_b, _ = lax.optimization_barrier(
             (grad_3, active_3, other_b, hot_grads)
         )
-        outputs = ((active_1, active_2, active_copy, active_3), down_weight, copy_down)
-        output_parts = ((part_1, part_2, part_copy, part_3), part_pick)
-        gradients = ((grad_1, grad_2, grad_copy, grad_3), up_weight, copy_up)
-        (mates_gradient,) = rows_call(1, *gradients)
-        active_3, other_d, _ = lax.optimization_barrier((active_3, other_d, mates_gradient))
-        outputs = ((active_1, active_2, active_copy, active_3), down_weight, copy_down)
-        (mates_output,) = rows_call(1, *outputs, *output_parts)
-        arrived_gradient = exchange.to_mate(mates_gradient)
-        arrived_output = exchange.to_mate(mates_output)
-
+        sides = (
+            (grad_1, grad_2, grad_copy, grad_3),
+            (active_1, active_2, active_copy, active_3),
+            (part_1, part_2, part_copy, part_3),
+            weights, part_pick,
+        )
+        mates_rows = rows_call(1, *sides)
+        arrived = [exchange.to_mate(block) for block in mates_rows]
+        other_d, _ = lax.optimization_barrier((other_d, mates_rows[0]))
         pair_blocks = [other, other_a, other_b, other_d]
         pair_blocks = pair_blocks + [exchange.to_mate(block) for block in pair_blocks]
-        gradient_rows = rows_call(0, *gradients, None, None, arrived_gradient)
-        *pair_blocks, arrived_output, _ = lax.optimization_barrier(
-            (*pair_blocks, arrived_output, gradient_rows[0])
-        )
-        output_rows = rows_call(0, *outputs, *output_parts, arrived_output)
-
-        *pair_blocks, _, _ = lax.optimization_barrier((*pair_blocks, gradient_rows[0], output_rows[0]))
+        *pair_blocks, _ = lax.optimization_barrier((*pair_blocks, mates_rows[0]))
         grad_pair, active_pair = hidden_call(hot, pair_blocks, weights, pick, base, (COLD,))
-        even = replica % 2 == 0
-        chunk_pair = jnp.where(even, jnp.array([1, 0]), jnp.array([2, 3])).astype(jnp.int32)
-        near, far = cold_call(
-            hot, chunk_pair, blocks + pair_blocks, (1, 1, 0, None),
+        chunk_pairs = jnp.array([[1, 0], [3, 2], [0, 1], [2, 3]], jnp.int32)
+        given, second = cold_call(
+            hot, chunk_pairs[replica], blocks + pair_blocks, (1, 1, 0, None),
             (grad_1, grad_2, grad_3, grad_pair), (active_1, active_2, active_3, active_pair),
             width, width // replicas,
         )
-        gradient_sum = exchange.reduce(gradient_rows, near)
-        output_sum = exchange.reduce(output_rows, near)
-        over = lax.ppermute(far, "dp", [(1, 3), (2, 0)])
-        over, across = lax.optimization_barrier((over, near))
-        across = lax.ppermute(across, "dp", [(1, 2), (2, 1)])
-        inward = lax.ppermute(near, "dp", [(0, 1), (3, 2)])
+        *arrived, _ = lax.optimization_barrier((*arrived, given))
+        own_rows = rows_call(0, *sides, tuple(arrived))
+        gradient_rows, output_rows = own_rows[:4], own_rows[4:]
+        gradient_sum = exchange.reduce(gradient_rows)
+        output_sum = exchange.reduce(output_rows)
+        moved = lax.ppermute(given, "dp", [(0, 1), (1, 3), (2, 0), (3, 2)])
+        moved, to_middle = lax.optimization_barrier((moved, second))
+        across = lax.ppermute(to_middle, "dp", [(1, 2), (2, 1)])
         at_end = (replica == 0) | (replica == replicas - 1)
-        kept = jnp.where(at_end, far, jnp.zeros((), BF16))
-        cold_sum = (
-            across.astype(F32) + over.astype(F32) + inward.astype(F32) + kept.astype(F32)
-        ).astype(BF16)
-        hot_first = hot_slot == 0
-        both = jnp.stack(
-            [jnp.where(hot_first, hot_sum, cold_sum), jnp.where(hot_first, cold_sum, hot_sum)]
-        )
-        up_grad = jnp.swapaxes(both[:, 0], 1, 2)
-        down_grad = both[:, 1]
+        up_grad, down_grad = place_call(
+            jnp.stack([hot_slot, at_end.astype(jnp.int32)]).astype(jnp.int32),
+            hot_sum, moved, second, across,
+        )
         return (*finish(output_sum[:, :width], gradient_sum, output_sum[:, width:]), up_grad, down_grad)
 
     exchange = PlainExchange(device_count)

time: 208 us -> 200 us (0.962)
  other arithmetic: 15.8 us -> 6.9 us
  waiting for transfers between devices: 45.3 us -> 47.8 us
  Pallas kernels: 91.7 us -> 89.3 us
    ppermute x3 -> x2, waiting for transfers between devices: 24.2 us -> 4.92 us  [the longest x1 3.3 us: local(): across = lax.ppermute(to_middle, 'dp', [(1, 2), (2, 1)])]
    ppermute x2, waiting for transfers between devices: 0.01 us -> 11.8 us  [reduce(): b_arrived = lax.ppermute(b, 'expert', self.second)]
    ppermute x2, waiting for transfers between devices: 0.01 us -> 7.41 us  [reduce(): d_arrived = lax.ppermute(d, 'expert', self.second)]
    ppermute x10, waiting for transfers between devices: 4.57 us -> 11.4 us  [to_mate(): return lax.ppermute(block, 'expert', self.mate)]
    ppermute x4, waiting for transfers between devices: 15.7 us -> 10.9 us  [far(): return lax.ppermute(first_block, 'expert', self.second)]
    ppermute x2, starting transfers between devices: 2.03 us -> 4.96 us  [reduce(): a_arrived = lax.ppermute(a, 'expert', self.first)]
    convert_element_type x2, other arithmetic: 4.11 us -> 1.3 us  [reduce(): a = (a.astype(F32) + d_arrived.astype(F32)).astype(BF16)]
    ppermute x3 -> x2, starting transfers between devices: 8.07 us -> 5.63 us  [the longest x1 3.11 us: local(): across = lax.ppermute(to_middle, 'dp', [(1, 2), (2, 1)])]
  transfers between devices with their start and end apart: 28 -> 27, of which waited for: 12 -> 16; matrix products, arithmetic and copies ran while one was open for 7% -> 5% of each run, Pallas kernels for 44% -> 43%
where the time goes in v3:
time: 200 us
  Pallas kernels  89.3 us (45%)
  waiting for transfers between devices  47.8 us (24%)
  starting transfers between devices  29.3 us (15%)
  between operations  16.3 us (8%)
  local copies, waits for them, and re-layouts  10 us (5%)
  other arithmetic  6.9 us (3%)
    pallas_call x5, Pallas kernels, hidden_call(): pl.pallas_call(functools.partial(hidden_kernel, count, slots, packing, wi...  45 us
    pallas_call x2, Pallas kernels, rows_call(): pl.pallas_call(functools.partial(rows_kernel, half, len(grads), bool(arri...  22.2 us
    ppermute x2, waiting for transfers between devices, reduce(): b_arrived = lax.ppermute(b, 'expert', self.second)  11.8 us
    ppermute x10, waiting for transfers between devices, to_mate(): return lax.ppermute(block, 'expert', self.mate)  11.4 us
    ppermute x4, waiting for transfers between devices, far(): return lax.ppermute(first_block, 'expert', self.second)  10.9 us
    pallas_call x1, Pallas kernels, hot_call(): pl.pallas_call(functools.partial(hot_kernel, count, firsts, width), in_sp...  9.86 us
    pallas_call x1, Pallas kernels, cold_call(): pl.pallas_call(functools.partial(cold_kernel, count, firsts, width), in_s...  8.78 us
    ppermute x2, waiting for transfers between devices, reduce(): d_arrived = lax.ppermute(d, 'expert', self.second)  7.41 us
  transfers between devices with their start and end apart: 27, of which 16 were waited for; matrix products, arithmetic and copies ran while one was open for 5% of the time, Pallas kernels for 43%

profile of v3, /device:TPU:8, one launch (start us, length us, event | category | flops | bytes accessed | tf_op | source)
XLA Modules:
  0.0 199.8 jit_solution(3828333111592329187)
XLA Ops:
  9.3 3.1 %concatenate.16.refs_1_.refs_2_ = bf16[128,4224]{1,0:T(8,128)(2,1)} concatenate(bf16[128,2048]{1,0:T(8,128)(2,1)} %param.12, bf16[128,2048]{1,0:T(8,128)(2,1)} %param.13, bf16[128,24]{1,0:T(8,128)(2,1)S(1)} %copy.35, bf16[128,24]{1,0:T(8,128)(2,1)S(1)} %subtract_convert_fusion, bf16[128,8]{1,0:T(8,128)(2,1)S(1)} %copy.36, bf16[128,72]{1,0:T(8,128)(2,1)S(1)} %broadcast_in_dim.24), dimensions={1} | concatenate | bytes 2162688 | tf_op jit(solution)/shard_map/concatenate | solution.py:701
  20.5 9.2 %hidden_units.5 = (bf16[1152,256]{1,0:T(8,128)(2,1)}, bf16[1152,256]{1,0:T(8,128)(2,1)}, bf16[48,256]{1,0:T(8,128)(2,1)}, f32[8,256]{1,0:T(8,128)}, bf16[768,256]{1,0:T(8,128)(2,1)}) custom-call(s32[1]{0:T(128)} %bitcast.1.refs_0_, bf16[128,4224]{1,0:T(8,128)(2,1)} %concatenate.16.refs_1_.refs_2_, bf16[128,4224]{1,0:T(8,128)(2,1)} %collective-permute-done.2.refs_2_.refs_3_, ...), custom_call_target="tpu_custom_call" | custom-call | flops 1 | bytes 1 | tf_op jit(solution)/shard_map/hidden_units/pallas_call | solution.py:162
  29.8 8.9 %collective-permute-done.1.refs_2_.refs_4_.refs_5_ = bf16[128,4224]{1,0:T(8,128)(2,1)} collective-permute-done((bf16[128,4224]{1,0:T(8,128)(2,1)}, bf16[128,4224]{1,0:T(8,128)(2,1)}, u32[]{:S(2)}, u32[]{:S(2)}) %collective-permute-start.1) | collective-permute-done | bytes 1081376 | tf_op jit(solution)/shard_map/ppermute | solution.py:583
  43.7 12.4 %hidden_units.6 = (bf16[1152,512]{1,0:T(8,128)(2,1)}, bf16[1152,512]{1,0:T(8,128)(2,1)}, bf16[48,512]{1,0:T(8,128)(2,1)}, f32[8,512]{1,0:T(8,128)}, bf16[768,256]{1,0:T(8,128)(2,1)}) custom-call(s32[1]{0:T(128)} %bitcast.1.refs_0_, bf16[128,4224]{1,0:T(8,128)(2,1)} %collective-permute-done.refs_1_.refs_3_.refs_4_, ...), custom_call_target="tpu_custom_call" | custom-call | flops 1 | bytes 1 | tf_op jit(solution)/shard_map/hidden_units/pallas_call | solution.py:162
  59.2 5.6 %hidden_units.7 = (bf16[384,256]{1,0:T(8,128)(2,1)}, bf16[384,256]{1,0:T(8,128)(2,1)}, bf16[16,256]{1,0:T(8,128)(2,1)}, f32[8,256]{1,0:T(8,128)}, bf16[768,256]{1,0:T(8,128)(2,1)}) custom-call(s32[1]{0:T(128)} %bitcast.1.refs_0_, bf16[128,4224]{1,0:T(8,128)(2,1)} %collective-permute-done.6.refs_1_.refs_7_.refs_8_, ...), custom_call_target="tpu_custom_call" | custom-call | flops 1 | bytes 1 | tf_op jit(solution)/shard_map/hidden_units/pallas_call | solution.py:162
  64.8 2.3 %collective-permute-start.8 = (bf16[768,256]{1,0:T(8,128)(2,1)}, bf16[768,256]{1,0:T(8,128)(2,1)}, u32[]{:S(2)}, u32[]{:S(2)}) collective-permute-start(bf16[768,256]{1,0:T(8,128)(2,1)} %get-tuple-element.77), channel_id=1, source_target_pairs={{0,28},{4,0},{8,4},{12,8},{16,12},{20,16},{24,20},{28,24},{1,29},{... | collective-permute-start | bytes 1179656 | tf_op jit(solution)/shard_map/ppermute | solution.py:730
  67.1 6.9 %hidden_units.8 = (bf16[768,256]{1,0:T(8,128)(2,1)}, bf16[768,256]{1,0:T(8,128)(2,1)}, bf16[32,256]{1,0:T(8,128)(2,1)}) custom-call(s32[1]{0:T(128)} %bitcast.1.refs_0_, bf16[128,4224]{1,0:T(8,128)(2,1)} %collective-permute-done.6.refs_1_.refs_7_.refs_8_, bf16[128,4224]{1,0:T(8,128)(2,1)} %collective-permute-done.7.refs_2_.refs_8_.refs_9_, ...), custom_call_target="tpu_custom_call" | custom-call | flops 1 | bytes 1 | tf_op jit(solution)/shard_map/hidden_units/pallas_call | solution.py:162
  76.6 9.9 %hot_weight_grads.1 = bf16[4,2,384,512]{3,2,1,0:T(8,128)(2,1)} custom-call(s32[1]{0:T(128)} %bitcast.1.refs_0_, bf16[128,4224]{1,0:T(8,128)(2,1)} %concatenate.16.refs_1_.refs_2_, bf16[128,4224]{1,0:T(8,128)(2,1)} %collective-permute-done.2.refs_2_.refs_3_, bf16[128,4224]{1,0:T(8,128)(2,1)} %collective-permute-done.refs_1_.refs_3_.refs_4_, ...), custom_call_target="tpu_custom_call" | custom-call | flops 1 | bytes 1 | tf_op jit(solution)/shard_map/hot_weight_grads/pallas_call | solution.py:257
  90.5 10.9 %row_sums.2 = (bf16[512,2048]{1,0:T(8,128)(2,1)}, bf16[512,2176]{1,0:T(8,128)(2,1)}) custom-call(bf16[1152,256]{1,0:T(8,128)(2,1)} %get-tuple-element.67.refs_9_.refs_0_.refs_18_, bf16[1152,512]{1,0:T(8,128)(2,1)} %get-tuple-element.73.refs_10_.refs_1_.refs_19_, bf16[384,256]{1,0:T(8,128)(2,1)} %get-tuple-element.76.refs_2_, ...), custom_call_target="tpu_custom_call" | custom-call | flops 1 | bytes 1 | tf_op jit(solution)/shard_map/row_sums/pallas_call | solution.py:553
  105.3 5.5 %collective-permute-done.15.refs_6_.refs_15_ = bf16[128,4224]{1,0:T(8,128)(2,1)} collective-permute-done((bf16[128,4224]{1,0:T(8,128)(2,1)}, bf16[128,4224]{1,0:T(8,128)(2,1)}, u32[]{:S(2)}, u32[]{:S(2)}) %collective-permute-start.15) | collective-permute-done | bytes 1081376 | tf_op jit(solution)/shard_map/ppermute | solution.py:586
  113.8 10.8 %hidden_units.9 = (bf16[384,1024]{1,0:T(8,128)(2,1)}, bf16[384,1024]{1,0:T(8,128)(2,1)}) custom-call(s32[1]{0:T(128)} %bitcast.1.refs_0_, bf16[128,4224]{1,0:T(8,128)(2,1)} %collective-permute-done.3.refs_1_.refs_10_, bf16[128,4224]{1,0:T(8,128)(2,1)} %collective-permute-done.9.refs_2_.refs_11_, bf16[128,4224]{1,0:T(8,128)(2,1)} %collective-permute-done.10.refs_3_.refs_12_, ...), custom_call_target="tpu_custom_call" | custom-call | flops 2000000000 | bytes 6000001 | tf_op jit(solution)/shard_map/hidden_units/pallas_call | solution.py:162
  124.7 8.8 %cold_weight_grads.1 = (bf16[2,384,512]{2,1,0:T(8,128)(2,1)}, bf16[2,384,512]{2,1,0:T(8,128)(2,1)}) custom-call(s32[1]{0:T(128)} %bitcast.1.refs_0_, s32[2]{0:T(128)} %dynamic-slice_bitcast_fusion.refs_1_, bf16[128,4224]{1,0:T(8,128)(2,1)} %concatenate.16.refs_1_.refs_2_, bf16[128,4224]{1,0:T(8,128)(2,1)} %collective-permute-done.2.refs_2_.refs_3_, ...), custom_call_target="tpu_custom_call" | custom-call | flops 2000000000 | bytes 6000001 | tf_op jit(solution)/shard_map/cold_weight_grads/pallas_call | solution.py:311
  133.5 11.3 %row_sums.3 = (bf16[128,2048]{1,0:T(8,128)(2,1)}, bf16[128,2048]{1,0:T(8,128)(2,1)}, bf16[128,2048]{1,0:T(8,128)(2,1)}, bf16[128,2048]{1,0:T(8,128)(2,1)}, bf16[...) custom-call(bf16[1152,256]{1,0:T(8,128)(2,1)} %get-tuple-element.67.ref, ...), custom_call_target="tpu_custom_call" | custom-call | flops 1 | bytes 1 | tf_op jit(solution)/shard_map/row_sums/pallas_call | solution.py:553
  146.9 2.5 %collective-permute-start.24 = (bf16[2,384,512]{2,1,0:T(8,128)(2,1)}, bf16[2,384,512]{2,1,0:T(8,128)(2,1)S(1)}, u32[]{:S(2)}, u32[]{:S(2)}) collective-permute-start(bf16[2,384,512]{2,1,0:T(8,128)(2,1)} %get-tuple-element.111), channel_id=1, source_target_pairs={{0,1},{1,3},{2,0},{3,2},{4,5},{5,7},{6,4},{7,6},{8,9},{9,11},{10,8... | collective-permute-start | bytes 2359304 | tf_op jit(solution)/shard_map/ppermute | solution.py:770
  151.5 2.8 %collective-permute-done.21 = bf16[128,2048]{1,0:T(8,128)(2,1)S(1)} collective-permute-done((bf16[128,2048]{1,0:T(8,128)(2,1)}, bf16[128,2048]{1,0:T(8,128)(2,1)S(1)}, u32[]{:S(2)}, u32[]{:S(2)}) %collective-permute-start.21) | collective-permute-done | bytes 524320 | tf_op jit(solution)/shard_map/ppermute | solution.py:590
  155.5 2.3 %collective-permute-start.22 = (bf16[128,2048]{1,0:T(8,128)(2,1)S(1)}, bf16[128,2048]{1,0:T(8,128)(2,1)S(1)}, u32[]{:S(2)}, u32[]{:S(2)}) collective-permute-start(bf16[128,2048]{1,0:T(8,128)(2,1)S(1)} %add_convert_fusion.2), channel_id=1, source_target_pairs={{0,8},{4,20},{8,0},{12,28},{16,24},{20,4},{24,16},{28,12},{1,9},{5... | collective-permute-start | bytes 1572872 | tf_op jit(solution)/shard_map/ppermute | solution.py:593
  157.7 4.6 %collective-permute-done.18 = bf16[128,2176]{1,0:T(8,128)(2,1)S(1)} collective-permute-done((bf16[128,2176]{1,0:T(8,128)(2,1)}, bf16[128,2176]{1,0:T(8,128)(2,1)S(1)}, u32[]{:S(2)}, u32[]{:S(2)}) %collective-permute-start.18) | collective-permute-done | bytes 557088 | tf_op jit(solution)/shard_map/ppermute | solution.py:590
  162.5 2.7 %collective-permute-start.19 = (bf16[128,2176]{1,0:T(8,128)(2,1)S(1)}, bf16[128,2176]{1,0:T(8,128)(2,1)S(1)}, u32[]{:S(2)}, u32[]{:S(2)}) collective-permute-start(bf16[128,2176]{1,0:T(8,128)(2,1)S(1)} %add_convert_fusion), channel_id=1, source_target_pairs={{0,8},{4,20},{8,0},{12,28},{16,24},{20,4},{24,16},{28,12},{1,9},{5... | collective-permute-start | bytes 1671176 | tf_op jit(solution)/shard_map/ppermute | solution.py:593
  165.8 1.6 collective-permute-done.24.moved_ref
  167.4 3.1 %collective-permute-start.25 = (bf16[2,384,512]{2,1,0:T(8,128)(2,1)S(1)}, bf16[2,384,512]{2,1,0:T(8,128)(2,1)S(1)}, u32[]{:S(2)}, u32[]{:S(2)}) collective-permute-start(bf16[2,384,512]{2,1,0:T(8,128)(2,1)S(1)} %copy-done), channel_id=1, source_target_pairs={{1,2},{2,1},{5,6},{6,5},{9,10},{10,9},{13,14},{14,13},{17,18},{18,... | collective-permute-start | bytes 2359304 | tf_op jit(solution)/shard_map/ppermute | solution.py:772
  170.6 3.0 %collective-permute-done.23 = bf16[128,2048]{1,0:T(8,128)(2,1)S(1)} collective-permute-done((bf16[128,2048]{1,0:T(8,128)(2,1)}, bf16[128,2048]{1,0:T(8,128)(2,1)S(1)}, u32[]{:S(2)}, u32[]{:S(2)}) %collective-permute-start.23) | collective-permute-done | bytes 524320 | tf_op jit(solution)/shard_map/ppermute | solution.py:591
  174.6 8.8 %collective-permute-done.20 = bf16[128,2176]{1,0:T(8,128)(2,1)S(1)} collective-permute-done((bf16[128,2176]{1,0:T(8,128)(2,1)}, bf16[128,2176]{1,0:T(8,128)(2,1)S(1)}, u32[]{:S(2)}, u32[]{:S(2)}) %collective-permute-start.20) | collective-permute-done | bytes 557088 | tf_op jit(solution)/shard_map/ppermute | solution.py:591
  185.3 3.3 %collective-permute-done.25.across_ref = bf16[2,384,512]{2,1,0:T(8,128)(2,1)S(1)} collective-permute-done((bf16[2,384,512]{2,1,0:T(8,128)(2,1)S(1)}, bf16[2,384,512]{2,1,0:T(8,128)(2,1)S(1)}, u32[]{:S(2)}, u32[]{:S(2)}) %collective-permute-start.25) | collective-permute-done | bytes 786464 | tf_op jit(solution)/shard_map/ppermute | solution.py:772
  189.5 3.4 %place_weight_grads.1 = (bf16[2,512,384]{2,1,0:T(8,128)(2,1)}, bf16[2,384,512]{2,1,0:T(8,128)(2,1)}) custom-call(s32[2]{0:T(128)} %pad_add_fusion.flags_ref, bf16[2,384,512]{2,1,0:T(8,128)(2,1)} %bitcast.22, bf16[2,384,512]{2,1,0:T(8,128)(2,1)} %copy-done.1, bf16[2,384,512]{2,1,0:T(8,128)(2,1)} %get-tuple-element.124.kept_ref, bf16[2,384,512]{2,1,0:T(8,128)(2,1)} %copy-done.2), custom_call_target="tpu_custom_call" | custom-call | flops 1 | bytes 1 | tf_op jit(solution)/shard_map/place_weight_grads/pallas_call | solution.py:349
  (107 shorter events, 39.7 us)
Async XLA Ops:
  7.2 182.3 %reduce-scatter.2.cloned.1.call-start = ((), (), s32[]{:S(2)}) async-start(), calls=%async_computation.1 | async-start | bytes 3932160 | tf_op jit(solution)/shard_map/reduce_scatter | solution.py:741
  12.3 8.2 %collective-permute-start.2 = (bf16[128,4224]{1,0:T(8,128)(2,1)}, bf16[128,4224]{1,0:T(8,128)(2,1)}, u32[]{:S(2)}, u32[]{:S(2)}) collective-permute-start(bf16[128,4224]{1,0:T(8,128)(2,1)} %concatenate.16.refs_1_.refs_2_), channel_id=1, source_target_pairs={{0,4},{4,0},{8,12},{12,8},{16,20},{20,16},{24,28},{28,24},{1,5},{5... | collective-permute-start | bytes 3244040 | tf_op jit(solution)/shard_map/ppermute | solution.py:586
  12.3 26.3 %collective-permute-start.1 = (bf16[128,4224]{1,0:T(8,128)(2,1)}, bf16[128,4224]{1,0:T(8,128)(2,1)}, u32[]{:S(2)}, u32[]{:S(2)}) collective-permute-start(bf16[128,4224]{1,0:T(8,128)(2,1)} %concatenate.16.refs_1_.refs_2_), channel_id=1, source_target_pairs={{0,16},{4,12},{8,24},{12,4},{16,0},{20,28},{24,8},{28,20},{1,17},{... | collective-permute-start | bytes 3244040 | tf_op jit(solution)/shard_map/ppermute | solution.py:583
  13.8 25.1 %collective-permute-start = (bf16[128,4224]{1,0:T(8,128)(2,1)}, bf16[128,4224]{1,0:T(8,128)(2,1)}, u32[]{:S(2)}, u32[]{:S(2)}) collective-permute-start(bf16[128,4224]{1,0:T(8,128)(2,1)} %concatenate.16.refs_1_.refs_2_), channel_id=1, source_target_pairs={{0,8},{4,20},{8,0},{12,28},{16,24},{20,4},{24,16},{28,12},{1,9},{5... | collective-permute-start | bytes 3244040 | tf_op jit(solution)/shard_map/ppermute | solution.py:580
  15.3 26.9 %collective-permute-start.3 = (bf16[128,4224]{1,0:T(8,128)(2,1)}, bf16[128,4224]{1,0:T(8,128)(2,1)}, u32[]{:S(2)}, u32[]{:S(2)}) collective-permute-start(bf16[128,4224]{1,0:T(8,128)(2,1)} %concatenate.16.refs_1_.refs_2_), channel_id=1, source_target_pairs={{0,1},{1,0},{2,3},{3,2},{4,5},{5,4},{6,7},{7,6},{8,9},{9,8},{10,11... | collective-permute-start | bytes 3244040 | tf_op jit(solution)/shard_map/ppermute | solution.py:705
  39.5 16.6 %collective-permute-start.6 = (bf16[128,4224]{1,0:T(8,128)(2,1)}, bf16[128,4224]{1,0:T(8,128)(2,1)}, u32[]{:S(2)}, u32[]{:S(2)}) collective-permute-start(bf16[128,4224]{1,0:T(8,128)(2,1)} %collective-permute-done.refs_1_.refs_3_.refs_4_), channel_id=1, source_target_pairs={{0,16},{4,12},{8,24},{12,4},{16,0},{20,28},{24,8},{28,20},{1,17},{... | collective-permute-start | bytes 3244040 | tf_op jit(solution)/shard_map/ppermute | solution.py:583
  56.6 17.5 %collective-permute-start.9 = (bf16[128,4224]{1,0:T(8,128)(2,1)}, bf16[128,4224]{1,0:T(8,128)(2,1)}, u32[]{:S(2)}, u32[]{:S(2)}) collective-permute-start(bf16[128,4224]{1,0:T(8,128)(2,1)} %collective-permute-done.3.refs_1_.refs_10_), channel_id=1, source_target_pairs={{0,8},{4,20},{8,0},{12,28},{16,24},{20,4},{24,16},{28,12},{1,9},{5... | collective-permute-start | bytes 3244040 | tf_op jit(solution)/shard_map/ppermute | solution.py:580
  64.8 10.2 %collective-permute-start.8 = (bf16[768,256]{1,0:T(8,128)(2,1)}, bf16[768,256]{1,0:T(8,128)(2,1)}, u32[]{:S(2)}, u32[]{:S(2)}) collective-permute-start(bf16[768,256]{1,0:T(8,128)(2,1)} %get-tuple-element.77), channel_id=1, source_target_pairs={{0,28},{4,0},{8,4},{12,8},{16,12},{20,16},{24,20},{28,24},{1,29},{... | collective-permute-start | bytes 1179656 | tf_op jit(solution)/shard_map/ppermute | solution.py:730
  75.1 15.5 %collective-permute-start.10 = (bf16[128,4224]{1,0:T(8,128)(2,1)}, bf16[128,4224]{1,0:T(8,128)(2,1)}, u32[]{:S(2)}, u32[]{:S(2)}) collective-permute-start(bf16[128,4224]{1,0:T(8,128)(2,1)} %collective-permute-done.3.refs_1_.refs_10_), channel_id=1, source_target_pairs={{0,16},{4,12},{8,24},{12,4},{16,0},{20,28},{24,8},{28,20},{1,17},{... | collective-permute-start | bytes 3244040 | tf_op jit(solution)/shard_map/ppermute | solution.py:583
  86.6 16.9 %collective-permute-start.14 = (bf16[128,4224]{1,0:T(8,128)(2,1)}, bf16[128,4224]{1,0:T(8,128)(2,1)}, u32[]{:S(2)}, u32[]{:S(2)}) collective-permute-start(bf16[128,4224]{1,0:T(8,128)(2,1)} %collective-permute-done.3.refs_1_.refs_10_), channel_id=1, source_target_pairs={{0,4},{4,0},{8,12},{12,8},{16,20},{20,16},{24,28},{28,24},{1,5},{5... | collective-permute-start | bytes 3244040 | tf_op jit(solution)/shard_map/ppermute | solution.py:586
  88.1 15.5 %collective-permute-start.13 = (bf16[128,4224]{1,0:T(8,128)(2,1)}, bf16[128,4224]{1,0:T(8,128)(2,1)}, u32[]{:S(2)}, u32[]{:S(2)}) collective-permute-start(bf16[128,4224]{1,0:T(8,128)(2,1)} %collective-permute-done.9.refs_2_.refs_11_), channel_id=1, source_target_pairs={{0,16},{4,12},{8,24},{12,4},{16,0},{20,28},{24,8},{28,20},{1,17},{... | collective-permute-start | bytes 3244040 | tf_op jit(solution)/shard_map/ppermute | solution.py:583
  101.4 32.0 %collective-permute-start.12 = (bf16[512,2176]{1,0:T(8,128)(2,1)}, bf16[512,2176]{1,0:T(8,128)(2,1)}, u32[]{:S(2)}, u32[]{:S(2)}) collective-permute-start(bf16[512,2176]{1,0:T(8,128)(2,1)} %get-tuple-element.97), channel_id=1, source_target_pairs={{0,4},{4,0},{8,12},{12,8},{16,20},{20,16},{24,28},{28,24},{1,5},{5... | collective-permute-start | bytes 6684680 | tf_op jit(solution)/shard_map/ppermute | solution.py:586
  101.9 31.6 %collective-permute-start.11 = (bf16[512,2048]{1,0:T(8,128)(2,1)}, bf16[512,2048]{1,0:T(8,128)(2,1)}, u32[]{:S(2)}, u32[]{:S(2)}) collective-permute-start(bf16[512,2048]{1,0:T(8,128)(2,1)} %get-tuple-element.96), channel_id=1, source_target_pairs={{0,4},{4,0},{8,12},{12,8},{16,20},{20,16},{24,28},{28,24},{1,5},{5... | collective-permute-start | bytes 6291464 | tf_op jit(solution)/shard_map/ppermute | solution.py:586
  102.0 8.7 %collective-permute-start.15 = (bf16[128,4224]{1,0:T(8,128)(2,1)}, bf16[128,4224]{1,0:T(8,128)(2,1)}, u32[]{:S(2)}, u32[]{:S(2)}) collective-permute-start(bf16[128,4224]{1,0:T(8,128)(2,1)} %collective-permute-done.9.refs_2_.refs_11_), channel_id=1, source_target_pairs={{0,4},{4,0},{8,12},{12,8},{16,20},{20,16},{24,28},{28,24},{1,5},{5... | collective-permute-start | bytes 3244040 | tf_op jit(solution)/shard_map/ppermute | solution.py:586
  103.6 8.7 %collective-permute-start.16 = (bf16[128,4224]{1,0:T(8,128)(2,1)}, bf16[128,4224]{1,0:T(8,128)(2,1)}, u32[]{:S(2)}, u32[]{:S(2)}) collective-permute-start(bf16[128,4224]{1,0:T(8,128)(2,1)} %collective-permute-done.10.refs_3_.refs_12_), channel_id=1, source_target_pairs={{0,4},{4,0},{8,12},{12,8},{16,20},{20,16},{24,28},{28,24},{1,5},{5... | collective-permute-start | bytes 3244040 | tf_op jit(solution)/shard_map/ppermute | solution.py:586
  103.6 10.3 %collective-permute-start.17 = (bf16[128,4224]{1,0:T(8,128)(2,1)}, bf16[128,4224]{1,0:T(8,128)(2,1)}, u32[]{:S(2)}, u32[]{:S(2)}) collective-permute-start(bf16[128,4224]{1,0:T(8,128)(2,1)} %collective-permute-done.13.refs_4_.refs_13_), channel_id=1, source_target_pairs={{0,4},{4,0},{8,12},{12,8},{16,20},{20,16},{24,28},{28,24},{1,5},{5... | collective-permute-start | bytes 3244040 | tf_op jit(solution)/shard_map/ppermute | solution.py:586
  144.8 9.5 %collective-permute-start.21 = (bf16[128,2048]{1,0:T(8,128)(2,1)}, bf16[128,2048]{1,0:T(8,128)(2,1)S(1)}, u32[]{:S(2)}, u32[]{:S(2)}) collective-permute-start(bf16[128,2048]{1,0:T(8,128)(2,1)} %get-tuple-element.120), channel_id=1, source_target_pairs={{0,16},{4,12},{8,24},{12,4},{16,0},{20,28},{24,8},{28,20},{1,17},{... | collective-permute-start | bytes 1572872 | tf_op jit(solution)/shard_map/ppermute | solution.py:590
  146.4 15.9 %collective-permute-start.18 = (bf16[128,2176]{1,0:T(8,128)(2,1)}, bf16[128,2176]{1,0:T(8,128)(2,1)S(1)}, u32[]{:S(2)}, u32[]{:S(2)}) collective-permute-start(bf16[128,2176]{1,0:T(8,128)(2,1)} %get-tuple-element.116), channel_id=1, source_target_pairs={{0,16},{4,12},{8,24},{12,4},{16,0},{20,28},{24,8},{28,20},{1,17},{... | collective-permute-start | bytes 1671176 | tf_op jit(solution)/shard_map/ppermute | solution.py:590
  146.9 20.5 %collective-permute-start.24 = (bf16[2,384,512]{2,1,0:T(8,128)(2,1)}, bf16[2,384,512]{2,1,0:T(8,128)(2,1)S(1)}, u32[]{:S(2)}, u32[]{:S(2)}) collective-permute-start(bf16[2,384,512]{2,1,0:T(8,128)(2,1)} %get-tuple-element.111), channel_id=1, source_target_pairs={{0,1},{1,3},{2,0},{3,2},{4,5},{5,7},{6,4},{7,6},{8,9},{9,11},{10,8... | collective-permute-start | bytes 2359304 | tf_op jit(solution)/shard_map/ppermute | solution.py:770
  149.5 24.1 %collective-permute-start.23 = (bf16[128,2048]{1,0:T(8,128)(2,1)}, bf16[128,2048]{1,0:T(8,128)(2,1)S(1)}, u32[]{:S(2)}, u32[]{:S(2)}) collective-permute-start(bf16[128,2048]{1,0:T(8,128)(2,1)} %get-tuple-element.121), channel_id=1, source_target_pairs={{0,16},{4,12},{8,24},{12,4},{16,0},{20,28},{24,8},{28,20},{1,17},{... | collective-permute-start | bytes 1572872 | tf_op jit(solution)/shard_map/ppermute | solution.py:591
  151.0 32.5 %collective-permute-start.20 = (bf16[128,2176]{1,0:T(8,128)(2,1)}, bf16[128,2176]{1,0:T(8,128)(2,1)S(1)}, u32[]{:S(2)}, u32[]{:S(2)}) collective-permute-start(bf16[128,2176]{1,0:T(8,128)(2,1)} %get-tuple-element.117), channel_id=1, source_target_pairs={{0,16},{4,12},{8,24},{12,4},{16,0},{20,28},{24,8},{28,20},{1,17},{... | collective-permute-start | bytes 1671176 | tf_op jit(solution)/shard_map/ppermute | solution.py:591
  155.5 18.1 %collective-permute-start.22 = (bf16[128,2048]{1,0:T(8,128)(2,1)S(1)}, bf16[128,2048]{1,0:T(8,128)(2,1)S(1)}, u32[]{:S(2)}, u32[]{:S(2)}) collective-permute-start(bf16[128,2048]{1,0:T(8,128)(2,1)S(1)} %add_convert_fusion.2), channel_id=1, source_target_pairs={{0,8},{4,20},{8,0},{12,28},{16,24},{20,4},{24,16},{28,12},{1,9},{5... | collective-permute-start | bytes 1572872 | tf_op jit(solution)/shard_map/ppermute | solution.py:593
  162.5 20.9 %collective-permute-start.19 = (bf16[128,2176]{1,0:T(8,128)(2,1)S(1)}, bf16[128,2176]{1,0:T(8,128)(2,1)S(1)}, u32[]{:S(2)}, u32[]{:S(2)}) collective-permute-start(bf16[128,2176]{1,0:T(8,128)(2,1)S(1)} %add_convert_fusion), channel_id=1, source_target_pairs={{0,8},{4,20},{8,0},{12,28},{16,24},{20,4},{24,16},{28,12},{1,9},{5... | collective-permute-start | bytes 1671176 | tf_op jit(solution)/shard_map/ppermute | solution.py:593
  167.4 21.2 %collective-permute-start.25 = (bf16[2,384,512]{2,1,0:T(8,128)(2,1)S(1)}, bf16[2,384,512]{2,1,0:T(8,128)(2,1)S(1)}, u32[]{:S(2)}, u32[]{:S(2)}) collective-permute-start(bf16[2,384,512]{2,1,0:T(8,128)(2,1)S(1)} %copy-done), channel_id=1, source_target_pairs={{1,2},{2,1},{5,6},{6,5},{9,10},{10,9},{13,14},{14,13},{17,18},{18,... | collective-permute-start | bytes 2359304 | tf_op jit(solution)/shard_map/ppermute | solution.py:772
  (14 other events, 102.7 us)
Sparse Core Ops, SparseCore 0:
  86.6 60.2 reduce-scatter.1

commit v4 on v3

--- a/solution.py
+++ b/solution.py
@@ -217,7 +217,7 @@
     grad_refs, active_refs, place_refs, refs = (
         refs[:pieces], refs[pieces : 2 * pieces], refs[2 * pieces : 3 * pieces], refs[3 * pieces :]
     )
-    packed_ref, out_ref, grads, actives, tokens, cotan, sems, chunk_sems = refs
+    packed_ref, out_ref, grads, actives, tokens, cotan, out, sems, chunk_sems, out_sems = refs
     chunks, total, chunk = tokens.shape
     hidden = grads.shape[0]
     fetches = Fetches(sems)
@@ -232,6 +232,9 @@
         for copy in chunk_copies(j, j, 0) + chunk_copies(j, j, 1):
             copy.start()
 
+    def store_of(j):
+        return pltpu.make_async_copy(out.at[j], out_ref.at[j], out_sems.at[j])
+
     place = jnp.concatenate([ref[1:2, :] for ref in place_refs], axis=1)
     index = lax.broadcasted_iota(jnp.int32, (packed_ref.shape[1], total), 0)
     chosen = (index == place.astype(jnp.int32)).astype(F32).astype(BF16)
@@ -245,7 +248,12 @@
         for half, (left, right) in enumerate(((grads, tokens), (actives, cotan))):
             for copy in chunk_copies(j, j, half):
                 copy.wait()
-            out_ref[j, half] = dot(left[...], right[j], (1, 0)).astype(BF16)
+            out[j, half] = dot(left[...], right[j], (1, 0)).astype(BF16)
+        store_of(j).start()
+
+    @pl.loop(0, chunks)
+    def _(j):
+        store_of(j).wait()
 
 
 def hot_call(hot, blocks, firsts, grads, actives, places, packed, width, chunks):
@@ -259,15 +267,17 @@
         in_specs=[pl.BlockSpec(memory_space=pltpu.SMEM)]
         + [ANYWHERE] * (count + 2 * len(firsts))
         + [vmem] * (len(firsts) + 1),
-        out_specs=vmem,
+        out_specs=ANYWHERE,
         out_shape=jax.ShapeDtypeStruct((chunks, 2, hidden, chunk), BF16),
         scratch_shapes=[
             pltpu.VMEM((hidden, total), BF16),
             pltpu.VMEM((hidden, total), BF16),
             pltpu.VMEM((chunks, total, chunk), BF16),
             pltpu.VMEM((chunks, total, chunk), BF16),
+            pltpu.VMEM((chunks, 2, hidden, chunk), BF16),
             pltpu.SemaphoreType.DMA((2 * len(firsts),)),
             pltpu.SemaphoreType.DMA((chunks, 2, count)),
+            pltpu.SemaphoreType.DMA((chunks,)),
         ],
         compiler_params=call_params(),
         cost_estimate=small_cost(),
@@ -327,37 +337,71 @@
     )(hot, chunk_pair, *blocks, *grads, *actives)
 
 
-def place_kernel(flags_ref, hot_ref, moved_ref, kept_ref, across_ref, up_ref, down_ref):
-    hot_slot = flags_ref[0]
-    up_ref[hot_slot] = hot_ref[0].T
-    down_ref[hot_slot] = hot_ref[1]
-
-    def place_cold(other_ref):
-        up = (moved_ref[0].astype(F32) + other_ref[0].astype(F32)).astype(BF16)
-        up_ref[1 - hot_slot] = up.T
-        down = (moved_ref[1].astype(F32) + other_ref[1].astype(F32)).astype(BF16)
-        down_ref[1 - hot_slot] = down
-
-    at_end = flags_ref[1] == 1
-    pl.when(at_end)(lambda: place_cold(kept_ref))
-    pl.when(jnp.logical_not(at_end))(lambda: place_cold(across_ref))
-
-
-def place_call(flags, hot_sum, moved, kept, across):
-    hidden, chunk = hot_sum.shape[1:]
-    vmem = pl.BlockSpec(memory_space=pltpu.VMEM)
+def place_kernel(is_hot, flags_ref, *refs):
+    values = refs[0] if is_hot else refs[:3]
+    up_ref, down_ref, held, up, down, sems = refs[-6:]
+    slot = flags_ref[0] if is_hot else 1 - flags_ref[0]
+    if is_hot:
+        fetch = pltpu.make_async_copy(values, held.at[0], sems.at[0])
+        fetch.start()
+        fetch.wait()
+        up[...] = held[0, 0].T
+        down[...] = held[0, 1]
+    else:
+        moved_ref, kept_ref, across_ref = values
+        at_end = flags_ref[1] == 1
+
+        @pl.when(at_end)
+        def _():
+            pltpu.make_async_copy(kept_ref, held.at[1], sems.at[1]).start()
+
+        @pl.when(jnp.logical_not(at_end))
+        def _():
+            pltpu.make_async_copy(across_ref, held.at[1], sems.at[1]).start()
+
+        fetch = pltpu.make_async_copy(moved_ref, held.at[0], sems.at[0])
+        fetch.start()
+        fetch.wait()
+        pltpu.make_async_copy(across_ref, held.at[1], sems.at[1]).wait()
+        total = (held[0].astype(F32) + held[1].astype(F32)).astype(BF16)
+        up[...] = total[0].T
+        down[...] = total[1]
+    stores = [
+        pltpu.make_async_copy(up, up_ref.at[slot], sems.at[2]),
+        pltpu.make_async_copy(down, down_ref.at[slot], sems.at[3]),
+    ]
+    for store in stores:
+        store.start()
+    for store in stores:
+        store.wait()
+
+
+def place_call(flags, values, filled=()):
+    hidden, chunk = values[0].shape[1:]
+    is_hot = not filled
+    shapes = [
+        jax.ShapeDtypeStruct((2, chunk, hidden), BF16),
+        jax.ShapeDtypeStruct((2, hidden, chunk), BF16),
+    ]
+    in_hbm = pl.BlockSpec(memory_space=pltpu.HBM)
+    aliases = {} if is_hot else {1 + len(values): 0, 2 + len(values): 1}
     return pl.pallas_call(
-        place_kernel,
-        in_specs=[pl.BlockSpec(memory_space=pltpu.SMEM)] + [vmem] * 4,
-        out_specs=[vmem, vmem],
-        out_shape=[
-            jax.ShapeDtypeStruct((2, chunk, hidden), BF16),
-            jax.ShapeDtypeStruct((2, hidden, chunk), BF16),
+        functools.partial(place_kernel, is_hot),
+        in_specs=[pl.BlockSpec(memory_space=pltpu.SMEM)]
+        + [in_hbm] * (len(values) + len(filled)),
+        out_specs=[in_hbm] * 2,
+        out_shape=shapes,
+        input_output_aliases=aliases,
+        scratch_shapes=[
+            pltpu.VMEM((2, 2, hidden, chunk), BF16),
+            pltpu.VMEM((chunk, hidden), BF16),
+            pltpu.VMEM((hidden, chunk), BF16),
+            pltpu.SemaphoreType.DMA((4,)),
         ],
         compiler_params=call_params(),
         cost_estimate=small_cost(),
         name="place_weight_grads",
-    )(flags, hot_sum, moved, kept, across)
+    )(flags, *values, *filled)
 
 
 class RowSums:
@@ -585,14 +629,6 @@
     def to_mate(self, block):
         return lax.ppermute(block, "expert", self.mate)
 
-    def reduce(self, blocks):
-        own, a, b, d = blocks
-        d_arrived = lax.ppermute(d, "expert", self.second)
-        b_arrived = lax.ppermute(b, "expert", self.second)
-        a = (a.astype(F32) + d_arrived.astype(F32)).astype(BF16)
-        a_arrived = lax.ppermute(a, "expert", self.first)
-        return own.astype(F32) + a_arrived.astype(F32) + b_arrived.astype(F32)
-
 
 class PlainExchange:
     def __init__(self, count):
@@ -740,9 +776,7 @@
         )
         hot_sum = lax.psum_scatter(hot_grads, "dp", scatter_dimension=0, tiled=True)[0]
 
-        grad_3, active_3, other_b, _ = lax.optimization_barrier(
-            (grad_3, active_3, other_b, hot_grads)
-        )
+        grad_3, active_3, _ = lax.optimization_barrier((grad_3, active_3, hot_grads))
         sides = (
             (grad_1, grad_2, grad_copy, grad_3),
             (active_1, active_2, active_copy, active_3),
@@ -750,31 +784,45 @@
             weights, part_pick,
         )
         mates_rows = rows_call(1, *sides)
+        *mates_rows, other_b = lax.optimization_barrier((*mates_rows, other_b))
         arrived = [exchange.to_mate(block) for block in mates_rows]
-        other_d, _ = lax.optimization_barrier((other_d, mates_rows[0]))
+        own_rows = rows_call(0, *sides, tuple(arrived))
+        gradient_rows, output_rows = own_rows[:4], own_rows[4:]
+        other_d, _ = lax.optimization_barrier((other_d, own_rows[0]))
         pair_blocks = [other, other_a, other_b, other_d]
         pair_blocks = pair_blocks + [exchange.to_mate(block) for block in pair_blocks]
-        *pair_blocks, _ = lax.optimization_barrier((*pair_blocks, mates_rows[0]))
+        from_diagonal = [exchange.far(rows_of[3]) for rows_of in (gradient_rows, output_rows)]
         grad_pair, active_pair = hidden_call(hot, pair_blocks, weights, pick, base, (COLD,))
+        grad_pair, *from_diagonal = lax.optimization_barrier((grad_pair, *from_diagonal))
         chunk_pairs = jnp.array([[1, 0], [3, 2], [0, 1], [2, 3]], jnp.int32)
         given, second = cold_call(
             hot, chunk_pairs[replica], blocks + pair_blocks, (1, 1, 0, None),
             (grad_1, grad_2, grad_3, grad_pair), (active_1, active_2, active_3, active_pair),
             width, width // replicas,
         )
-        *arrived, _ = lax.optimization_barrier((*arrived, given))
-        own_rows = rows_call(0, *sides, tuple(arrived))
-        gradient_rows, output_rows = own_rows[:4], own_rows[4:]
-        gradient_sum = exchange.reduce(gradient_rows)
-        output_sum = exchange.reduce(output_rows)
+        at_end = (replica == 0) | (replica == replicas - 1)
+        flags = jnp.stack([hot_slot, at_end.astype(jnp.int32)]).astype(jnp.int32)
+        filled = place_call(flags, [hot_sum])
+        *from_diagonal, first_filled = lax.optimization_barrier((*from_diagonal, filled[0]))
+        filled = (first_filled, filled[1])
+        relayed = [
+            (rows_of[1].astype(F32) + arrived.astype(F32)).astype(BF16)
+            for rows_of, arrived in zip((gradient_rows, output_rows), from_diagonal)
+        ]
         moved = lax.ppermute(given, "dp", [(0, 1), (1, 3), (2, 0), (3, 2)])
-        moved, to_middle = lax.optimization_barrier((moved, second))
+        hops = [exchange.far(rows_of[2]) for rows_of in (gradient_rows, output_rows)]
+        gradient_hop, output_hop = (exchange.first_hop(block) for block in relayed)
+        moved, to_middle, gradient_hop, *hops = lax.optimization_barrier(
+            (moved, second, gradient_hop, *hops)
+        )
+        gradient_sum, output_sum = (
+            rows_of[0].astype(F32) + first.astype(F32) + other_hop.astype(F32)
+            for rows_of, first, other_hop in zip(
+                (gradient_rows, output_rows), (gradient_hop, output_hop), hops
+            )
+        )
         across = lax.ppermute(to_middle, "dp", [(1, 2), (2, 1)])
-        at_end = (replica == 0) | (replica == replicas - 1)
-        up_grad, down_grad = place_call(
-            jnp.stack([hot_slot, at_end.astype(jnp.int32)]).astype(jnp.int32),
-            hot_sum, moved, second, across,
-        )
+        up_grad, down_grad = place_call(flags, [moved, second, across], filled)
         return (*finish(output_sum[:, :width], gradient_sum, output_sum[:, width:]), up_grad, down_grad)
 
     exchange = PlainExchange(device_count)

time: 200 us -> 196 us (0.980)
  waiting for transfers between devices: 47.8 us -> 40.5 us
  other arithmetic: 6.9 us -> 10.3 us
  starting transfers between devices: 29.3 us -> 26.8 us
    ppermute x6 -> x0, waiting for transfers between devices: 19.3 us -> none  [the longest x2 11.8 us: reduce(): b_arrived = lax.ppermute(b, 'expert', self.second)]
    ppermute x6 -> x0, starting transfers between devices: 9.07 us -> none  [the longest x2 4.96 us: reduce(): a_arrived = lax.ppermute(a, 'expert', self.first)]
    ppermute x1, waiting for transfers between devices: 3.3 us -> 11.3 us  [local(): across = lax.ppermute(to_middle, 'dp', [(1, 2), (2, 1)])]
    ppermute x1, waiting for transfers between devices: 1.62 us -> 8.96 us  [local(): moved = lax.ppermute(given, 'dp', [(0, 1), (1, 3), (2, 0), (3, 2)])]
    ppermute x4 -> x8, starting transfers between devices: 5.07 us -> 10 us  [far(): return lax.ppermute(first_block, 'expert', self.second)]
    ppermute x10, waiting for transfers between devices: 11.4 us -> 8.18 us  [to_mate(): return lax.ppermute(block, 'expert', self.mate)]
    pallas_call x1 -> x2, Pallas kernels: 3.45 us -> 6.01 us  [place_call(): pl.pallas_call(functools.partial(place_kernel, is_hot), in_specs=[pl.Bloc...]
    ppermute x2 -> x4, starting transfers between devices: 2.79 us -> 4.95 us  [first_hop(): return lax.ppermute(block, 'expert', self.first)]
  transfers between devices with their start and end apart: 27 -> 27, of which waited for: 16 -> 9; matrix products, arithmetic and copies ran while one was open for 5% -> 7% of each run, Pallas kernels for 43% -> 40%
where the time goes in v4:
time: 196 us; the launch traced here: 195 us
  Pallas kernels  91 us (46%)
  waiting for transfers between devices  40.5 us (21%)
  starting transfers between devices  26.8 us (14%)
  between operations  16.3 us (8%)
  other arithmetic  10.3 us (5%)
  local copies, waits for them, and re-layouts  10.1 us (5%)
    pallas_call x5, Pallas kernels, hidden_call(): pl.pallas_call(functools.partial(hidden_kernel, count, slots, packing, wi...  44.9 us
    pallas_call x2, Pallas kernels, rows_call(): pl.pallas_call(functools.partial(rows_kernel, half, len(grads), bool(arri...  22.3 us
    ppermute x1, waiting for transfers between devices, local(): across = lax.ppermute(to_middle, 'dp', [(1, 2), (2, 1)])  11.3 us
    ppermute x8, waiting for transfers between devices, far(): return lax.ppermute(first_block, 'expert', self.second)  10.8 us
    ppermute x8, starting transfers between devices, far(): return lax.ppermute(first_block, 'expert', self.second)  10 us
    pallas_call x1, Pallas kernels, hot_call(): pl.pallas_call(functools.partial(hot_kernel, count, firsts, width), in_sp...  9.15 us
    ppermute x1, waiting for transfers between devices, local(): moved = lax.ppermute(given, 'dp', [(0, 1), (1, 3), (2, 0), (3, 2)])  8.96 us
    pallas_call x1, Pallas kernels, cold_call(): pl.pallas_call(functools.partial(cold_kernel, count, firsts, width), in_s...  8.73 us
  transfers between devices with their start and end apart: 27, of which 9 were waited for; matrix products, arithmetic and copies ran while one was open for 7% of the time, Pallas kernels for 40%

profile of v4, /device:TPU:8, one launch (start us, length us, event | category | flops | bytes accessed | tf_op | source)
XLA Modules:
  0.0 195.1 jit_solution(14100314242846820254)
XLA Ops:
  9.3 3.1 %concatenate.16.refs_1_.refs_2_ = bf16[128,4224]{1,0:T(8,128)(2,1)} concatenate(bf16[128,2048]{1,0:T(8,128)(2,1)} %param.12, bf16[128,2048]{1,0:T(8,128)(2,1)} %param.13, bf16[128,24]{1,0:T(8,128)(2,1)S(1)} %copy.37, bf16[128,24]{1,0:T(8,128)(2,1)S(1)} %subtract_convert_fusion, bf16[128,8]{1,0:T(8,128)(2,1)S(1)} %copy.38, bf16[128,72]{1,0:T(8,128)(2,1)S(1)} %broadcast_in_dim.24), dimensions={1} | concatenate | bytes 2162688 | tf_op jit(solution)/shard_map/concatenate | solution.py:737
  12.3 1.5 collective-permute-start.1
  20.5 9.2 %hidden_units.5 = (bf16[1152,256]{1,0:T(8,128)(2,1)}, bf16[1152,256]{1,0:T(8,128)(2,1)}, bf16[48,256]{1,0:T(8,128)(2,1)}, f32[8,256]{1,0:T(8,128)}, bf16[768,256]{1,0:T(8,128)(2,1)}) custom-call(s32[1]{0:T(128)} %bitcast.1.refs_0_, bf16[128,4224]{1,0:T(8,128)(2,1)} %concatenate.16.refs_1_.refs_2_, bf16[128,4224]{1,0:T(8,128)(2,1)} %collective-permute-done.2.refs_2_.refs_3_, ...), custom_call_target="tpu_custom_call" | custom-call | flops 1 | bytes 1 | tf_op jit(solution)/shard_map/hidden_units/pallas_call | solution.py:162
  29.7 8.9 %collective-permute-done.1.refs_2_.refs_4_.refs_5_ = bf16[128,4224]{1,0:T(8,128)(2,1)} collective-permute-done((bf16[128,4224]{1,0:T(8,128)(2,1)}, bf16[128,4224]{1,0:T(8,128)(2,1)}, u32[]{:S(2)}, u32[]{:S(2)}) %collective-permute-start.1) | collective-permute-done | bytes 1081376 | tf_op jit(solution)/shard_map/ppermute | solution.py:627
  43.7 12.4 %hidden_units.6 = (bf16[1152,512]{1,0:T(8,128)(2,1)}, bf16[1152,512]{1,0:T(8,128)(2,1)}, bf16[48,512]{1,0:T(8,128)(2,1)}, f32[8,512]{1,0:T(8,128)}, bf16[768,256]{1,0:T(8,128)(2,1)}) custom-call(s32[1]{0:T(128)} %bitcast.1.refs_0_, bf16[128,4224]{1,0:T(8,128)(2,1)} %collective-permute-done.refs_1_.refs_3_.refs_4_, ...), custom_call_target="tpu_custom_call" | custom-call | flops 1 | bytes 1 | tf_op jit(solution)/shard_map/hidden_units/pallas_call | solution.py:162
  59.2 5.6 %hidden_units.7 = (bf16[384,256]{1,0:T(8,128)(2,1)}, bf16[384,256]{1,0:T(8,128)(2,1)}, bf16[16,256]{1,0:T(8,128)(2,1)}, f32[8,256]{1,0:T(8,128)}, bf16[768,256]{1,0:T(8,128)(2,1)}) custom-call(s32[1]{0:T(128)} %bitcast.1.refs_0_, bf16[128,4224]{1,0:T(8,128)(2,1)} %collective-permute-done.6.refs_1_.refs_7_.refs_8_, ...), custom_call_target="tpu_custom_call" | custom-call | flops 1 | bytes 1 | tf_op jit(solution)/shard_map/hidden_units/pallas_call | solution.py:162
  64.9 2.3 %collective-permute-start.8 = (bf16[768,256]{1,0:T(8,128)(2,1)}, bf16[768,256]{1,0:T(8,128)(2,1)}, u32[]{:S(2)}, u32[]{:S(2)}) collective-permute-start(bf16[768,256]{1,0:T(8,128)(2,1)} %get-tuple-element.80), channel_id=1, source_target_pairs={{0,28},{4,0},{8,4},{12,8},{16,12},{20,16},{24,20},{28,24},{1,29},{... | collective-permute-start | bytes 1179656 | tf_op jit(solution)/shard_map/ppermute | solution.py:766
  67.1 6.9 %hidden_units.8 = (bf16[768,256]{1,0:T(8,128)(2,1)}, bf16[768,256]{1,0:T(8,128)(2,1)}, bf16[32,256]{1,0:T(8,128)(2,1)}) custom-call(s32[1]{0:T(128)} %bitcast.1.refs_0_, bf16[128,4224]{1,0:T(8,128)(2,1)} %collective-permute-done.6.refs_1_.refs_7_.refs_8_, bf16[128,4224]{1,0:T(8,128)(2,1)} %collective-permute-done.7.refs_2_.refs_8_.refs_9_, ...), custom_call_target="tpu_custom_call" | custom-call | flops 1 | bytes 1 | tf_op jit(solution)/shard_map/hidden_units/pallas_call | solution.py:162
  75.1 9.1 %hot_weight_grads.1 = bf16[4,2,384,512]{3,2,1,0:T(8,128)(2,1)} custom-call(s32[1]{0:T(128)} %bitcast.1.refs_0_, bf16[128,4224]{1,0:T(8,128)(2,1)} %concatenate.16.refs_1_.refs_2_, bf16[128,4224]{1,0:T(8,128)(2,1)} %collective-permute-done.2.refs_2_.refs_3_, bf16[128,4224]{1,0:T(8,128)(2,1)} %collective-permute-done.refs_1_.refs_3_.refs_4_, ...), custom_call_target="tpu_custom_call" | custom-call | flops 1 | bytes 1 | tf_op jit(solution)/shard_map/hot_weight_grads/pallas_call | solution.py:265
  84.2 1.6 collective-permute-start.10
  87.1 10.9 %row_sums.2 = (bf16[512,2048]{1,0:T(8,128)(2,1)}, bf16[512,2176]{1,0:T(8,128)(2,1)}) custom-call(bf16[1152,256]{1,0:T(8,128)(2,1)} %get-tuple-element.70.refs_9_.refs_0_.refs_18_, bf16[1152,512]{1,0:T(8,128)(2,1)} %get-tuple-element.76.refs_10_.refs_1_.refs_19_, bf16[384,256]{1,0:T(8,128)(2,1)} %get-tuple-element.79.refs_2_, ...), custom_call_target="tpu_custom_call" | custom-call | flops 1 | bytes 1 | tf_op jit(solution)/shard_map/row_sums/pallas_call | solution.py:597
  98.0 1.8 collective-permute-done.10.refs_3_.refs_12_
  102.4 5.3 %collective-permute-done.11.refs_17_ = bf16[512,2048]{1,0:T(8,128)(2,1)} collective-permute-done((bf16[512,2048]{1,0:T(8,128)(2,1)}, bf16[512,2048]{1,0:T(8,128)(2,1)}, u32[]{:S(2)}, u32[]{:S(2)}) %collective-permute-start.11) | collective-permute-done | bytes 2097184 | tf_op jit(solution)/shard_map/ppermute | solution.py:630
  108.1 11.4 %row_sums.3 = (bf16[128,2048]{1,0:T(8,128)(2,1)}, bf16[128,2048]{1,0:T(8,128)(2,1)}, bf16[128,2048]{1,0:T(8,128)(2,1)}, bf16[128,2048]{1,0:T(8,128)(2,1)}, bf16[...) custom-call(bf16[1152,256]{1,0:T(8,128)(2,1)} %get-tuple-element.70.ref, ...), custom_call_target="tpu_custom_call" | custom-call | flops 1 | bytes 1 | tf_op jit(solution)/shard_map/row_sums/pallas_call | solution.py:597
  125.6 10.8 %hidden_units.9 = (bf16[384,1024]{1,0:T(8,128)(2,1)}, bf16[384,1024]{1,0:T(8,128)(2,1)}) custom-call(s32[1]{0:T(128)} %bitcast.1.refs_0_, bf16[128,4224]{1,0:T(8,128)(2,1)} %collective-permute-done.3.refs_1_.refs_10_, bf16[128,4224]{1,0:T(8,128)(2,1)} %collective-permute-done.9.refs_2_.refs_11_, bf16[128,4224]{1,0:T(8,128)(2,1)} %collective-permute-done.10.refs_3_.refs_12_, ...), custom_call_target="tpu_custom_call" | custom-call | flops 2000000000 | bytes 6000001 | tf_op jit(solution)/shard_map/hidden_units/pallas_call | solution.py:162
  136.4 8.7 %cold_weight_grads.1 = (bf16[2,384,512]{2,1,0:T(8,128)(2,1)}, bf16[2,384,512]{2,1,0:T(8,128)(2,1)}) custom-call(s32[1]{0:T(128)} %bitcast.1.refs_0_, s32[2]{0:T(128)} %dynamic-slice_bitcast_fusion.refs_1_, bf16[128,4224]{1,0:T(8,128)(2,1)} %concatenate.16.refs_1_.refs_2_, bf16[128,4224]{1,0:T(8,128)(2,1)} %collective-permute-done.2.refs_2_.refs_3_, ...), custom_call_target="tpu_custom_call" | custom-call | flops 2000000000 | bytes 6000001 | tf_op jit(solution)/shard_map/cold_weight_grads/pallas_call | solution.py:321
  145.1 2.7 %collective-permute-start.21 = (bf16[2,384,512]{2,1,0:T(8,128)(2,1)}, bf16[2,384,512]{2,1,0:T(8,128)(2,1)}, u32[]{:S(2)}, u32[]{:S(2)}) collective-permute-start(bf16[2,384,512]{2,1,0:T(8,128)(2,1)} %get-tuple-element.118), channel_id=1, source_target_pairs={{0,1},{1,3},{2,0},{3,2},{4,5},{5,7},{6,4},{7,6},{8,9},{9,11},{10,8... | collective-permute-start | bytes 2359304 | tf_op jit(solution)/shard_map/ppermute | solution.py:812
  147.8 2.9 %place_weight_grads.2 = (bf16[2,512,384]{2,1,0:T(8,128)(2,1)}, bf16[2,384,512]{2,1,0:T(8,128)(2,1)}) custom-call(s32[2]{0:T(128)} %pad_add_fusion.flags_ref, bf16[2,384,512]{2,1,0:T(8,128)(2,1)} %bitcast.22), custom_call_target="tpu_custom_call" | custom-call | flops 1 | bytes 1 | tf_op jit(solution)/shard_map/place_weight_grads/pallas_call | solution.py:388
  152.1 1.8 collective-permute-start.22
  155.5 9.0 %collective-permute-done.21.refs_0_ = bf16[2,384,512]{2,1,0:T(8,128)(2,1)} collective-permute-done((bf16[2,384,512]{2,1,0:T(8,128)(2,1)}, bf16[2,384,512]{2,1,0:T(8,128)(2,1)}, u32[]{:S(2)}, u32[]{:S(2)}) %collective-permute-start.21) | collective-permute-done | bytes 786464 | tf_op jit(solution)/shard_map/ppermute | solution.py:812
  164.4 3.4 %collective-permute-start.25 = (bf16[2,384,512]{2,1,0:T(8,128)(2,1)S(1)}, bf16[2,384,512]{2,1,0:T(8,128)(2,1)S(1)}, u32[]{:S(2)}, u32[]{:S(2)}) collective-permute-start(bf16[2,384,512]{2,1,0:T(8,128)(2,1)S(1)} %copy-done), channel_id=1, source_target_pairs={{1,2},{2,1},{5,6},{6,5},{9,10},{10,9},{13,14},{14,13},{17,18},{18,... | collective-permute-start | bytes 2359304 | tf_op jit(solution)/shard_map/ppermute | solution.py:824
  167.9 2.1 %add_convert_fusion.1 = bf16[128,2048]{1,0:T(8,128)(2,1)} fusion(bf16[128,2048]{1,0:T(8,128)(2,1)} %collective-permute-done.23, bf16[128,2048]{1,0:T(8,128)(2,1)S(1)} %collective-permute-done.22, bf16[128,2048]{1,0:T(8,128)(2,1)S(1)} %copy-done.4), kind=kLoop, calls=%fused_computation.5 | loop fusion | flops 1572864 | bytes 2097152 | tf_op jit(solution)/shard_map/convert_element_type | solution.py:708
  172.8 11.3 %collective-permute-done.25.refs_2_ = bf16[2,384,512]{2,1,0:T(8,128)(2,1)S(1)} collective-permute-done((bf16[2,384,512]{2,1,0:T(8,128)(2,1)S(1)}, bf16[2,384,512]{2,1,0:T(8,128)(2,1)S(1)}, u32[]{:S(2)}, u32[]{:S(2)}) %collective-permute-start.25) | collective-permute-done | bytes 786464 | tf_op jit(solution)/shard_map/ppermute | solution.py:824
  185.1 3.2 %place_weight_grads.3 = (bf16[2,512,384]{2,1,0:T(8,128)(2,1)}, bf16[2,384,512]{2,1,0:T(8,128)(2,1)}) custom-call(s32[2]{0:T(128)} %pad_add_fusion.flags_ref, bf16[2,384,512]{2,1,0:T(8,128)(2,1)} %collective-permute-done.21.refs_0_, bf16[2,384,512]{2,1,0:T(8,128)(2,1)} %get-tuple-element.128.refs_1_, ...), custom_call_target="tpu_custom_call", output_to_operand_aliasing={{0}: (4, {}), {1}: (5, {})} | custom-call | flops 1 | bytes 1 | tf_op jit(solution)/shard_map/place_weight_grads/pallas_call | solution.py:388
  (106 shorter events, 32.9 us)
Async XLA Ops:
  7.2 140.6 %reduce-scatter.2.cloned.1.call-start = ((), (), s32[]{:S(2)}) async-start(), calls=%async_computation.1 | async-start | bytes 3932160 | tf_op jit(solution)/shard_map/reduce_scatter | solution.py:777
  12.3 8.2 %collective-permute-start.2 = (bf16[128,4224]{1,0:T(8,128)(2,1)}, bf16[128,4224]{1,0:T(8,128)(2,1)}, u32[]{:S(2)}, u32[]{:S(2)}) collective-permute-start(bf16[128,4224]{1,0:T(8,128)(2,1)} %concatenate.16.refs_1_.refs_2_), channel_id=1, source_target_pairs={{0,4},{4,0},{8,12},{12,8},{16,20},{20,16},{24,28},{28,24},{1,5},{5... | collective-permute-start | bytes 3244040 | tf_op jit(solution)/shard_map/ppermute | solution.py:630
  12.3 26.3 %collective-permute-start.1 = (bf16[128,4224]{1,0:T(8,128)(2,1)}, bf16[128,4224]{1,0:T(8,128)(2,1)}, u32[]{:S(2)}, u32[]{:S(2)}) collective-permute-start(bf16[128,4224]{1,0:T(8,128)(2,1)} %concatenate.16.refs_1_.refs_2_), channel_id=1, source_target_pairs={{0,16},{4,12},{8,24},{12,4},{16,0},{20,28},{24,8},{28,20},{1,17},{... | collective-permute-start | bytes 3244040 | tf_op jit(solution)/shard_map/ppermute | solution.py:627
  13.8 25.1 %collective-permute-start = (bf16[128,4224]{1,0:T(8,128)(2,1)}, bf16[128,4224]{1,0:T(8,128)(2,1)}, u32[]{:S(2)}, u32[]{:S(2)}) collective-permute-start(bf16[128,4224]{1,0:T(8,128)(2,1)} %concatenate.16.refs_1_.refs_2_), channel_id=1, source_target_pairs={{0,8},{4,20},{8,0},{12,28},{16,24},{20,4},{24,16},{28,12},{1,9},{5... | collective-permute-start | bytes 3244040 | tf_op jit(solution)/shard_map/ppermute | solution.py:624
  15.3 26.9 %collective-permute-start.3 = (bf16[128,4224]{1,0:T(8,128)(2,1)}, bf16[128,4224]{1,0:T(8,128)(2,1)}, u32[]{:S(2)}, u32[]{:S(2)}) collective-permute-start(bf16[128,4224]{1,0:T(8,128)(2,1)} %concatenate.16.refs_1_.refs_2_), channel_id=1, source_target_pairs={{0,1},{1,0},{2,3},{3,2},{4,5},{5,4},{6,7},{7,6},{8,9},{9,8},{10,11... | collective-permute-start | bytes 3244040 | tf_op jit(solution)/shard_map/ppermute | solution.py:741
  39.5 16.6 %collective-permute-start.6 = (bf16[128,4224]{1,0:T(8,128)(2,1)}, bf16[128,4224]{1,0:T(8,128)(2,1)}, u32[]{:S(2)}, u32[]{:S(2)}) collective-permute-start(bf16[128,4224]{1,0:T(8,128)(2,1)} %collective-permute-done.refs_1_.refs_3_.refs_4_), channel_id=1, source_target_pairs={{0,16},{4,12},{8,24},{12,4},{16,0},{20,28},{24,8},{28,20},{1,17},{... | collective-permute-start | bytes 3244040 | tf_op jit(solution)/shard_map/ppermute | solution.py:627
  56.6 17.5 %collective-permute-start.9 = (bf16[128,4224]{1,0:T(8,128)(2,1)}, bf16[128,4224]{1,0:T(8,128)(2,1)}, u32[]{:S(2)}, u32[]{:S(2)}) collective-permute-start(bf16[128,4224]{1,0:T(8,128)(2,1)} %collective-permute-done.3.refs_1_.refs_10_), channel_id=1, source_target_pairs={{0,8},{4,20},{8,0},{12,28},{16,24},{20,4},{24,16},{28,12},{1,9},{5... | collective-permute-start | bytes 3244040 | tf_op jit(solution)/shard_map/ppermute | solution.py:624
  64.9 10.2 %collective-permute-start.8 = (bf16[768,256]{1,0:T(8,128)(2,1)}, bf16[768,256]{1,0:T(8,128)(2,1)}, u32[]{:S(2)}, u32[]{:S(2)}) collective-permute-start(bf16[768,256]{1,0:T(8,128)(2,1)} %get-tuple-element.80), channel_id=1, source_target_pairs={{0,28},{4,0},{8,4},{12,8},{16,12},{20,16},{24,20},{28,24},{1,29},{... | collective-permute-start | bytes 1179656 | tf_op jit(solution)/shard_map/ppermute | solution.py:766
  84.2 15.5 %collective-permute-start.10 = (bf16[128,4224]{1,0:T(8,128)(2,1)}, bf16[128,4224]{1,0:T(8,128)(2,1)}, u32[]{:S(2)}, u32[]{:S(2)}) collective-permute-start(bf16[128,4224]{1,0:T(8,128)(2,1)} %collective-permute-done.3.refs_1_.refs_10_), channel_id=1, source_target_pairs={{0,16},{4,12},{8,24},{12,4},{16,0},{20,28},{24,8},{28,20},{1,17},{... | collective-permute-start | bytes 3244040 | tf_op jit(solution)/shard_map/ppermute | solution.py:627
  99.8 8.4 %collective-permute-start.12 = (bf16[512,2176]{1,0:T(8,128)(2,1)}, bf16[512,2176]{1,0:T(8,128)(2,1)}, u32[]{:S(2)}, u32[]{:S(2)}) collective-permute-start(bf16[512,2176]{1,0:T(8,128)(2,1)} %get-tuple-element.102), channel_id=1, source_target_pairs={{0,4},{4,0},{8,12},{12,8},{16,20},{20,16},{24,28},{28,24},{1,5},{5... | collective-permute-start | bytes 6684680 | tf_op jit(solution)/shard_map/ppermute | solution.py:630
  100.4 7.3 %collective-permute-start.11 = (bf16[512,2048]{1,0:T(8,128)(2,1)}, bf16[512,2048]{1,0:T(8,128)(2,1)}, u32[]{:S(2)}, u32[]{:S(2)}) collective-permute-start(bf16[512,2048]{1,0:T(8,128)(2,1)} %get-tuple-element.101), channel_id=1, source_target_pairs={{0,4},{4,0},{8,12},{12,8},{16,20},{20,16},{24,28},{28,24},{1,5},{5... | collective-permute-start | bytes 6291464 | tf_op jit(solution)/shard_map/ppermute | solution.py:630
  100.5 19.1 %collective-permute-start.13 = (bf16[128,4224]{1,0:T(8,128)(2,1)}, bf16[128,4224]{1,0:T(8,128)(2,1)}, u32[]{:S(2)}, u32[]{:S(2)}) collective-permute-start(bf16[128,4224]{1,0:T(8,128)(2,1)} %collective-permute-done.9.refs_2_.refs_11_), channel_id=1, source_target_pairs={{0,16},{4,12},{8,24},{12,4},{16,0},{20,28},{24,8},{28,20},{1,17},{... | collective-permute-start | bytes 3244040 | tf_op jit(solution)/shard_map/ppermute | solution.py:627
  101.8 19.1 %collective-permute-start.14 = (bf16[128,4224]{1,0:T(8,128)(2,1)}, bf16[128,4224]{1,0:T(8,128)(2,1)}, u32[]{:S(2)}, u32[]{:S(2)}) collective-permute-start(bf16[128,4224]{1,0:T(8,128)(2,1)} %collective-permute-done.3.refs_1_.refs_10_), channel_id=1, source_target_pairs={{0,4},{4,0},{8,12},{12,8},{16,20},{20,16},{24,28},{28,24},{1,5},{5... | collective-permute-start | bytes 3244040 | tf_op jit(solution)/shard_map/ppermute | solution.py:630
  102.4 21.1 %collective-permute-start.15 = (bf16[128,4224]{1,0:T(8,128)(2,1)}, bf16[128,4224]{1,0:T(8,128)(2,1)}, u32[]{:S(2)}, u32[]{:S(2)}) collective-permute-start(bf16[128,4224]{1,0:T(8,128)(2,1)} %collective-permute-done.9.refs_2_.refs_11_), channel_id=1, source_target_pairs={{0,4},{4,0},{8,12},{12,8},{16,20},{20,16},{24,28},{28,24},{1,5},{5... | collective-permute-start | bytes 3244040 | tf_op jit(solution)/shard_map/ppermute | solution.py:630
  107.8 17.0 %collective-permute-start.16 = (bf16[128,4224]{1,0:T(8,128)(2,1)}, bf16[128,4224]{1,0:T(8,128)(2,1)}, u32[]{:S(2)}, u32[]{:S(2)}) collective-permute-start(bf16[128,4224]{1,0:T(8,128)(2,1)} %collective-permute-done.10.refs_3_.refs_12_), channel_id=1, source_target_pairs={{0,4},{4,0},{8,12},{12,8},{16,20},{20,16},{24,28},{28,24},{1,5},{5... | collective-permute-start | bytes 3244040 | tf_op jit(solution)/shard_map/ppermute | solution.py:630
  119.5 6.1 %collective-permute-start.17 = (bf16[128,4224]{1,0:T(8,128)(2,1)}, bf16[128,4224]{1,0:T(8,128)(2,1)}, u32[]{:S(2)}, u32[]{:S(2)}) collective-permute-start(bf16[128,4224]{1,0:T(8,128)(2,1)} %collective-permute-done.13.refs_4_.refs_13_), channel_id=1, source_target_pairs={{0,4},{4,0},{8,12},{12,8},{16,20},{20,16},{24,28},{28,24},{1,5},{5... | collective-permute-start | bytes 3244040 | tf_op jit(solution)/shard_map/ppermute | solution.py:630
  119.7 16.7 %collective-permute-start.19 = (bf16[128,2176]{1,0:T(8,128)(2,1)}, bf16[128,2176]{1,0:T(8,128)(2,1)}, u32[]{:S(2)}, u32[]{:S(2)}) collective-permute-start(bf16[128,2176]{1,0:T(8,128)(2,1)} %get-tuple-element.111), channel_id=1, source_target_pairs={{0,16},{4,12},{8,24},{12,4},{16,0},{20,28},{24,8},{28,20},{1,17},{... | collective-permute-start | bytes 1671176 | tf_op jit(solution)/shard_map/ppermute | solution.py:627
  121.0 15.4 %collective-permute-start.18 = (bf16[128,2048]{1,0:T(8,128)(2,1)}, bf16[128,2048]{1,0:T(8,128)(2,1)}, u32[]{:S(2)}, u32[]{:S(2)}) collective-permute-start(bf16[128,2048]{1,0:T(8,128)(2,1)} %get-tuple-element.110), channel_id=1, source_target_pairs={{0,16},{4,12},{8,24},{12,4},{16,0},{20,28},{24,8},{28,20},{1,17},{... | collective-permute-start | bytes 1572872 | tf_op jit(solution)/shard_map/ppermute | solution.py:627
  123.6 31.9 %collective-permute-start.23 = (bf16[128,2048]{1,0:T(8,128)(2,1)}, bf16[128,2048]{1,0:T(8,128)(2,1)}, u32[]{:S(2)}, u32[]{:S(2)}) collective-permute-start(bf16[128,2048]{1,0:T(8,128)(2,1)} %get-tuple-element.122), channel_id=1, source_target_pairs={{0,16},{4,12},{8,24},{12,4},{16,0},{20,28},{24,8},{28,20},{1,17},{... | collective-permute-start | bytes 1572872 | tf_op jit(solution)/shard_map/ppermute | solution.py:627
  124.8 30.7 %collective-permute-start.24 = (bf16[128,2176]{1,0:T(8,128)(2,1)}, bf16[128,2176]{1,0:T(8,128)(2,1)}, u32[]{:S(2)}, u32[]{:S(2)}) collective-permute-start(bf16[128,2176]{1,0:T(8,128)(2,1)} %get-tuple-element.123), channel_id=1, source_target_pairs={{0,16},{4,12},{8,24},{12,4},{16,0},{20,28},{24,8},{28,20},{1,17},{... | collective-permute-start | bytes 1671176 | tf_op jit(solution)/shard_map/ppermute | solution.py:627
  145.1 19.3 %collective-permute-start.21 = (bf16[2,384,512]{2,1,0:T(8,128)(2,1)}, bf16[2,384,512]{2,1,0:T(8,128)(2,1)}, u32[]{:S(2)}, u32[]{:S(2)}) collective-permute-start(bf16[2,384,512]{2,1,0:T(8,128)(2,1)} %get-tuple-element.118), channel_id=1, source_target_pairs={{0,1},{1,3},{2,0},{3,2},{4,5},{5,7},{6,4},{7,6},{8,9},{9,11},{10,8... | collective-permute-start | bytes 2359304 | tf_op jit(solution)/shard_map/ppermute | solution.py:812
  152.1 12.3 %collective-permute-start.22 = (bf16[128,2048]{1,0:T(8,128)(2,1)S(1)}, bf16[128,2048]{1,0:T(8,128)(2,1)S(1)}, u32[]{:S(2)}, u32[]{:S(2)}) collective-permute-start(bf16[128,2048]{1,0:T(8,128)(2,1)S(1)} %add_convert_fusion.2), channel_id=1, source_target_pairs={{0,8},{4,20},{8,0},{12,28},{16,24},{20,4},{24,16},{28,12},{1,9},{5... | collective-permute-start | bytes 1572872 | tf_op jit(solution)/shard_map/ppermute | solution.py:624
  155.1 14.9 %collective-permute-start.20 = (bf16[128,2176]{1,0:T(8,128)(2,1)S(1)}, bf16[128,2176]{1,0:T(8,128)(2,1)S(1)}, u32[]{:S(2)}, u32[]{:S(2)}) collective-permute-start(bf16[128,2176]{1,0:T(8,128)(2,1)S(1)} %add_convert_fusion), channel_id=1, source_target_pairs={{0,8},{4,20},{8,0},{12,28},{16,24},{20,4},{24,16},{28,12},{1,9},{5... | collective-permute-start | bytes 1671176 | tf_op jit(solution)/shard_map/ppermute | solution.py:624
  164.4 19.7 %collective-permute-start.25 = (bf16[2,384,512]{2,1,0:T(8,128)(2,1)S(1)}, bf16[2,384,512]{2,1,0:T(8,128)(2,1)S(1)}, u32[]{:S(2)}, u32[]{:S(2)}) collective-permute-start(bf16[2,384,512]{2,1,0:T(8,128)(2,1)S(1)} %copy-done), channel_id=1, source_target_pairs={{1,2},{2,1},{5,6},{6,5},{9,10},{10,9},{13,14},{14,13},{17,18},{18,... | collective-permute-start | bytes 2359304 | tf_op jit(solution)/shard_map/ppermute | solution.py:824
  (13 other events, 77.3 us)
Sparse Core Ops, SparseCore 0:
  84.4 61.3 reduce-scatter.1

commit v5 on v4

--- a/solution.py
+++ b/solution.py
@@ -72,7 +72,8 @@
     grad_ref, active_ref, *refs = refs
     part_ref = refs.pop(0) if COLD not in slots else None
     place_ref, packed_ref = (refs.pop(0), refs.pop(0)) if packing else (None, None)
-    together, ups, downs, gates, slot_sems, block_sems = refs
+    together, ups, downs, slot_sems, block_sems = refs
+    gates = {}
     rows = row_refs[0].shape[0]
     hidden = down_ref.shape[1]
     group = 2 * rows
@@ -107,14 +108,14 @@
                 for copy in block_copies[2 * g : 2 * g + 2]:
                     copy.wait()
                 found = dot(pick_ref[...], together[here, 2 * width :], (1, 1))
-                gates[:, here] = found
+                gates[g] = found
                 if packing:
                     ranks = found[SERVED_RANK : OWNED_RANK + 1]
                     place = jnp.where(ranks > 0.5, base_ref[:, here] + ranks - 1.0, -1.0)
                     place_ref[:, here] = jnp.concatenate(
                         [place, jnp.zeros((6, group), F32)], axis=0
                     )
-            gate = gates[first_gate + number : first_gate + number + 1, here]
+            gate = gates[g][first_gate + number : first_gate + number + 1]
             linear = dot(ups[number], together[here, :width], (0, 1))
             raw_grad = dot(downs[number], together[here, width : 2 * width], (1, 1))
             sigma = 0.5 * jnp.tanh(0.5 * linear) + 0.5
@@ -168,7 +169,6 @@
             pltpu.VMEM((total, columns), BF16),
             pltpu.VMEM((len(slots), width, hidden), BF16),
             pltpu.VMEM((len(slots), hidden, width), BF16),
-            pltpu.VMEM((16, total), F32),
             pltpu.SemaphoreType.DMA((len(slots), 2)),
             pltpu.SemaphoreType.DMA((count,)),
         ],
@@ -350,22 +350,30 @@
     else:
         moved_ref, kept_ref, across_ref = values
         at_end = flags_ref[1] == 1
-
-        @pl.when(at_end)
-        def _():
-            pltpu.make_async_copy(kept_ref, held.at[1], sems.at[1]).start()
-
-        @pl.when(jnp.logical_not(at_end))
-        def _():
-            pltpu.make_async_copy(across_ref, held.at[1], sems.at[1]).start()
-
-        fetch = pltpu.make_async_copy(moved_ref, held.at[0], sems.at[0])
-        fetch.start()
-        fetch.wait()
-        pltpu.make_async_copy(across_ref, held.at[1], sems.at[1]).wait()
-        total = (held[0].astype(F32) + held[1].astype(F32)).astype(BF16)
-        up[...] = total[0].T
-        down[...] = total[1]
+        for half in range(2):
+
+            @pl.when(at_end)
+            def _(half=half):
+                pltpu.make_async_copy(
+                    kept_ref.at[half], held.at[1, half], sems.at[4 + half]
+                ).start()
+
+            @pl.when(jnp.logical_not(at_end))
+            def _(half=half):
+                pltpu.make_async_copy(
+                    across_ref.at[half], held.at[1, half], sems.at[4 + half]
+                ).start()
+
+            pltpu.make_async_copy(moved_ref.at[half], held.at[0, half], sems.at[half]).start()
+        for half, (target, out) in enumerate(((up, up_ref), (down, down_ref))):
+            pltpu.make_async_copy(moved_ref.at[half], held.at[0, half], sems.at[half]).wait()
+            pltpu.make_async_copy(across_ref.at[half], held.at[1, half], sems.at[4 + half]).wait()
+            total = (held[0, half].astype(F32) + held[1, half].astype(F32)).astype(BF16)
+            target[...] = total.T if half == 0 else total
+            pltpu.make_async_copy(target, out.at[slot], sems.at[2 + half]).start()
+        for half, (target, out) in enumerate(((up, up_ref), (down, down_ref))):
+            pltpu.make_async_copy(target, out.at[slot], sems.at[2 + half]).wait()
+        return
     stores = [
         pltpu.make_async_copy(up, up_ref.at[slot], sems.at[2]),
         pltpu.make_async_copy(down, down_ref.at[slot], sems.at[3]),
@@ -383,22 +391,21 @@
         jax.ShapeDtypeStruct((2, chunk, hidden), BF16),
         jax.ShapeDtypeStruct((2, hidden, chunk), BF16),
     ]
-    in_hbm = pl.BlockSpec(memory_space=pltpu.HBM)
     aliases = {} if is_hot else {1 + len(values): 0, 2 + len(values): 1}
     return pl.pallas_call(
         functools.partial(place_kernel, is_hot),
         in_specs=[pl.BlockSpec(memory_space=pltpu.SMEM)]
-        + [in_hbm] * (len(values) + len(filled)),
-        out_specs=[in_hbm] * 2,
+        + [ANYWHERE] * (len(values) + len(filled)),
+        out_specs=[ANYWHERE] * 2,
         out_shape=shapes,
         input_output_aliases=aliases,
         scratch_shapes=[
             pltpu.VMEM((2, 2, hidden, chunk), BF16),
             pltpu.VMEM((chunk, hidden), BF16),
             pltpu.VMEM((hidden, chunk), BF16),
-            pltpu.SemaphoreType.DMA((4,)),
+            pltpu.SemaphoreType.DMA((6,)),
         ],
-        compiler_params=call_params(),
+        compiler_params=pltpu.CompilerParams(vmem_limit_bytes=16 * 1024 * 1024),
         cost_estimate=small_cost(),
         name="place_weight_grads",
     )(flags, *values, *filled)

time: 196 us -> 194 us (0.990)
  Pallas kernels: 91 us -> 88.9 us
where the time goes in v5:
time: 194 us; the launch traced here: 193 us
  Pallas kernels  88.9 us (46%)
  waiting for transfers between devices  40.1 us (21%)
  starting transfers between devices  26.6 us (14%)
  between operations  16.3 us (8%)
  local copies, waits for them, and re-layouts  11 us (6%)
  other arithmetic  10.2 us (5%)
    pallas_call x5, Pallas kernels, hidden_call(): pl.pallas_call(functools.partial(hidden_kernel, count, slots, packing, wi...  44.7 us
    pallas_call x2, Pallas kernels, rows_call(): pl.pallas_call(functools.partial(rows_kernel, half, len(grads), bool(arri...  22.2 us
    ppermute x1, waiting for transfers between devices, local(): across = lax.ppermute(to_middle, 'dp', [(1, 2), (2, 1)])  11.4 us
    ppermute x8, waiting for transfers between devices, far(): return lax.ppermute(first_block, 'expert', self.second)  10.8 us
    ppermute x8, starting transfers between devices, far(): return lax.ppermute(first_block, 'expert', self.second)  10 us
    pallas_call x1, Pallas kernels, hot_call(): pl.pallas_call(functools.partial(hot_kernel, count, firsts, width), in_sp...  9.16 us
    pallas_call x1, Pallas kernels, cold_call(): pl.pallas_call(functools.partial(cold_kernel, count, firsts, width), in_s...  8.77 us
    ppermute x1, waiting for transfers between devices, local(): moved = lax.ppermute(given, 'dp', [(0, 1), (1, 3), (2, 0), (3, 2)])  8.42 us
  transfers between devices with their start and end apart: 27, of which 9 were waited for; matrix products, arithmetic and copies ran while one was open for 7% of the time, Pallas kernels for 40%

profile of v5, /device:TPU:8, one launch (start us, length us, event | category | flops | bytes accessed | tf_op | source)
XLA Modules:
  0.0 193.3 jit_solution(15893022548101813382)
XLA Ops:
  9.3 3.1 %concatenate.16.refs_1_.refs_2_ = bf16[128,4224]{1,0:T(8,128)(2,1)} concatenate(bf16[128,2048]{1,0:T(8,128)(2,1)} %param.12, bf16[128,2048]{1,0:T(8,128)(2,1)} %param.13, bf16[128,24]{1,0:T(8,128)(2,1)S(1)} %copy.37, bf16[128,24]{1,0:T(8,128)(2,1)S(1)} %subtract_convert_fusion, bf16[128,8]{1,0:T(8,128)(2,1)S(1)} %copy.38, bf16[128,72]{1,0:T(8,128)(2,1)S(1)} %broadcast_in_dim.24), dimensions={1} | concatenate | bytes 2162688 | tf_op jit(solution)/shard_map/concatenate | solution.py:744
  12.3 1.5 collective-permute-start.1
  20.5 9.2 %hidden_units.5 = (bf16[1152,256]{1,0:T(8,128)(2,1)}, bf16[1152,256]{1,0:T(8,128)(2,1)}, bf16[48,256]{1,0:T(8,128)(2,1)}, f32[8,256]{1,0:T(8,128)}, bf16[768,256]{1,0:T(8,128)(2,1)}) custom-call(s32[1]{0:T(128)} %bitcast.1.refs_0_, bf16[128,4224]{1,0:T(8,128)(2,1)} %concatenate.16.refs_1_.refs_2_, bf16[128,4224]{1,0:T(8,128)(2,1)} %collective-permute-done.2.refs_2_.refs_3_, ...), custom_call_target="tpu_custom_call" | custom-call | flops 1 | bytes 1 | tf_op jit(solution)/shard_map/hidden_units/pallas_call | solution.py:163
  29.7 8.9 %collective-permute-done.1.refs_2_.refs_4_.refs_5_ = bf16[128,4224]{1,0:T(8,128)(2,1)} collective-permute-done((bf16[128,4224]{1,0:T(8,128)(2,1)}, bf16[128,4224]{1,0:T(8,128)(2,1)}, u32[]{:S(2)}, u32[]{:S(2)}) %collective-permute-start.1) | collective-permute-done | bytes 1081376 | tf_op jit(solution)/shard_map/ppermute | solution.py:634
  43.7 12.3 %hidden_units.6 = (bf16[1152,512]{1,0:T(8,128)(2,1)}, bf16[1152,512]{1,0:T(8,128)(2,1)}, bf16[48,512]{1,0:T(8,128)(2,1)}, f32[8,512]{1,0:T(8,128)}, bf16[768,256]{1,0:T(8,128)(2,1)}) custom-call(s32[1]{0:T(128)} %bitcast.1.refs_0_, bf16[128,4224]{1,0:T(8,128)(2,1)} %collective-permute-done.refs_1_.refs_3_.refs_4_, ...), custom_call_target="tpu_custom_call" | custom-call | flops 1 | bytes 1 | tf_op jit(solution)/shard_map/hidden_units/pallas_call | solution.py:163
  59.2 5.6 %hidden_units.7 = (bf16[384,256]{1,0:T(8,128)(2,1)}, bf16[384,256]{1,0:T(8,128)(2,1)}, bf16[16,256]{1,0:T(8,128)(2,1)}, f32[8,256]{1,0:T(8,128)}, bf16[768,256]{1,0:T(8,128)(2,1)}) custom-call(s32[1]{0:T(128)} %bitcast.1.refs_0_, bf16[128,4224]{1,0:T(8,128)(2,1)} %collective-permute-done.6.refs_1_.refs_7_.refs_8_, ...), custom_call_target="tpu_custom_call" | custom-call | flops 1 | bytes 1 | tf_op jit(solution)/shard_map/hidden_units/pallas_call | solution.py:163
  64.8 2.3 %collective-permute-start.8 = (bf16[768,256]{1,0:T(8,128)(2,1)}, bf16[768,256]{1,0:T(8,128)(2,1)}, u32[]{:S(2)}, u32[]{:S(2)}) collective-permute-start(bf16[768,256]{1,0:T(8,128)(2,1)} %get-tuple-element.80), channel_id=1, source_target_pairs={{0,28},{4,0},{8,4},{12,8},{16,12},{20,16},{24,20},{28,24},{1,29},{... | collective-permute-start | bytes 1179656 | tf_op jit(solution)/shard_map/ppermute | solution.py:773
  67.1 6.9 %hidden_units.8 = (bf16[768,256]{1,0:T(8,128)(2,1)}, bf16[768,256]{1,0:T(8,128)(2,1)}, bf16[32,256]{1,0:T(8,128)(2,1)}) custom-call(s32[1]{0:T(128)} %bitcast.1.refs_0_, bf16[128,4224]{1,0:T(8,128)(2,1)} %collective-permute-done.6.refs_1_.refs_7_.refs_8_, bf16[128,4224]{1,0:T(8,128)(2,1)} %collective-permute-done.7.refs_2_.refs_8_.refs_9_, ...), custom_call_target="tpu_custom_call" | custom-call | flops 1 | bytes 1 | tf_op jit(solution)/shard_map/hidden_units/pallas_call | solution.py:163
  75.0 9.2 %hot_weight_grads.1 = bf16[4,2,384,512]{3,2,1,0:T(8,128)(2,1)} custom-call(s32[1]{0:T(128)} %bitcast.1.refs_0_, bf16[128,4224]{1,0:T(8,128)(2,1)} %concatenate.16.refs_1_.refs_2_, bf16[128,4224]{1,0:T(8,128)(2,1)} %collective-permute-done.2.refs_2_.refs_3_, bf16[128,4224]{1,0:T(8,128)(2,1)} %collective-permute-done.refs_1_.refs_3_.refs_4_, ...), custom_call_target="tpu_custom_call" | custom-call | flops 1 | bytes 1 | tf_op jit(solution)/shard_map/hot_weight_grads/pallas_call | solution.py:265
  84.2 1.6 collective-permute-start.10
  87.0 10.9 %row_sums.2 = (bf16[512,2048]{1,0:T(8,128)(2,1)}, bf16[512,2176]{1,0:T(8,128)(2,1)}) custom-call(bf16[1152,256]{1,0:T(8,128)(2,1)} %get-tuple-element.70.refs_9_.refs_0_.refs_18_, bf16[1152,512]{1,0:T(8,128)(2,1)} %get-tuple-element.76.refs_10_.refs_1_.refs_19_, bf16[384,256]{1,0:T(8,128)(2,1)} %get-tuple-element.79.refs_2_, ...), custom_call_target="tpu_custom_call" | custom-call | flops 1 | bytes 1 | tf_op jit(solution)/shard_map/row_sums/pallas_call | solution.py:604
  97.8 1.9 collective-permute-done.10.refs_3_.refs_12_
  102.3 5.3 %collective-permute-done.11.refs_17_ = bf16[512,2048]{1,0:T(8,128)(2,1)} collective-permute-done((bf16[512,2048]{1,0:T(8,128)(2,1)}, bf16[512,2048]{1,0:T(8,128)(2,1)}, u32[]{:S(2)}, u32[]{:S(2)}) %collective-permute-start.11) | collective-permute-done | bytes 2097184 | tf_op jit(solution)/shard_map/ppermute | solution.py:637
  108.1 11.4 %row_sums.3 = (bf16[128,2048]{1,0:T(8,128)(2,1)}, bf16[128,2048]{1,0:T(8,128)(2,1)}, bf16[128,2048]{1,0:T(8,128)(2,1)}, bf16[128,2048]{1,0:T(8,128)(2,1)}, bf16[...) custom-call(bf16[1152,256]{1,0:T(8,128)(2,1)} %get-tuple-element.70.ref, ...), custom_call_target="tpu_custom_call" | custom-call | flops 1 | bytes 1 | tf_op jit(solution)/shard_map/row_sums/pallas_call | solution.py:604
  125.5 10.7 %hidden_units.9 = (bf16[384,1024]{1,0:T(8,128)(2,1)}, bf16[384,1024]{1,0:T(8,128)(2,1)}) custom-call(s32[1]{0:T(128)} %bitcast.1.refs_0_, bf16[128,4224]{1,0:T(8,128)(2,1)} %collective-permute-done.3.refs_1_.refs_10_, bf16[128,4224]{1,0:T(8,128)(2,1)} %collective-permute-done.9.refs_2_.refs_11_, bf16[128,4224]{1,0:T(8,128)(2,1)} %collective-permute-done.10.refs_3_.refs_12_, ...), custom_call_target="tpu_custom_call" | custom-call | flops 2000000000 | bytes 6000001 | tf_op jit(solution)/shard_map/hidden_units/pallas_call | solution.py:163
  136.3 8.8 %cold_weight_grads.1 = (bf16[2,384,512]{2,1,0:T(8,128)(2,1)}, bf16[2,384,512]{2,1,0:T(8,128)(2,1)}) custom-call(s32[1]{0:T(128)} %bitcast.1.refs_0_, s32[2]{0:T(128)} %dynamic-slice_bitcast_fusion.refs_1_, bf16[128,4224]{1,0:T(8,128)(2,1)} %concatenate.16.refs_1_.refs_2_, bf16[128,4224]{1,0:T(8,128)(2,1)} %collective-permute-done.2.refs_2_.refs_3_, ...), custom_call_target="tpu_custom_call" | custom-call | flops 2000000000 | bytes 6000001 | tf_op jit(solution)/shard_map/cold_weight_grads/pallas_call | solution.py:321
  145.1 2.7 %collective-permute-start.21 = (bf16[2,384,512]{2,1,0:T(8,128)(2,1)}, bf16[2,384,512]{2,1,0:T(8,128)(2,1)S(1)}, u32[]{:S(2)}, u32[]{:S(2)}) collective-permute-start(bf16[2,384,512]{2,1,0:T(8,128)(2,1)} %get-tuple-element.118), channel_id=1, source_target_pairs={{0,1},{1,3},{2,0},{3,2},{4,5},{5,7},{6,4},{7,6},{8,9},{9,11},{10,8... | collective-permute-start | bytes 2359304 | tf_op jit(solution)/shard_map/ppermute | solution.py:819
  149.5 1.7 place_weight_grads.2
  152.5 1.8 collective-permute-start.22
  155.9 8.4 %collective-permute-done.21.refs_0_ = bf16[2,384,512]{2,1,0:T(8,128)(2,1)S(1)} collective-permute-done((bf16[2,384,512]{2,1,0:T(8,128)(2,1)}, bf16[2,384,512]{2,1,0:T(8,128)(2,1)S(1)}, u32[]{:S(2)}, u32[]{:S(2)}) %collective-permute-start.21) | collective-permute-done | bytes 786464 | tf_op jit(solution)/shard_map/ppermute | solution.py:819
  164.3 3.3 %collective-permute-start.25 = (bf16[2,384,512]{2,1,0:T(8,128)(2,1)S(1)}, bf16[2,384,512]{2,1,0:T(8,128)(2,1)S(1)}, u32[]{:S(2)}, u32[]{:S(2)}) collective-permute-start(bf16[2,384,512]{2,1,0:T(8,128)(2,1)S(1)} %copy-done.1), channel_id=1, source_target_pairs={{1,2},{2,1},{5,6},{6,5},{9,10},{10,9},{13,14},{14,13},{17,18},{18,... | collective-permute-start | bytes 2359304 | tf_op jit(solution)/shard_map/ppermute | solution.py:831
  167.7 2.1 %add_convert_fusion.1 = bf16[128,2048]{1,0:T(8,128)(2,1)} fusion(bf16[128,2048]{1,0:T(8,128)(2,1)} %collective-permute-done.23, bf16[128,2048]{1,0:T(8,128)(2,1)S(1)} %collective-permute-done.22, bf16[128,2048]{1,0:T(8,128)(2,1)S(1)} %copy-done.6), kind=kLoop, calls=%fused_computation.5 | loop fusion | flops 1572864 | bytes 2097152 | tf_op jit(solution)/shard_map/convert_element_type | solution.py:715
  172.7 11.4 %collective-permute-done.25.refs_2_ = bf16[2,384,512]{2,1,0:T(8,128)(2,1)S(1)} collective-permute-done((bf16[2,384,512]{2,1,0:T(8,128)(2,1)S(1)}, bf16[2,384,512]{2,1,0:T(8,128)(2,1)S(1)}, u32[]{:S(2)}, u32[]{:S(2)}) %collective-permute-start.25) | collective-permute-done | bytes 786464 | tf_op jit(solution)/shard_map/ppermute | solution.py:831
  184.1 2.4 %place_weight_grads.3 = (bf16[2,512,384]{2,1,0:T(8,128)(2,1)}, bf16[2,384,512]{2,1,0:T(8,128)(2,1)}) custom-call(s32[2]{0:T(128)S(1)} %copy-done.3, bf16[2,384,512]{2,1,0:T(8,128)(2,1)S(1)} %collective-permute-done.21.refs_0_, bf16[2,384,512]{2,1,0:T(8,128)(2,1)S(1)} %copy-done.1, ...), custom_call_target="tpu_custom_call", output_to_operand_aliasing={{0}: (4, {}), {1}: (5, {})} | custom-call | flops 1 | bytes 1 | tf_op jit(solution)/shard_map/place_weight_grads/pallas_call | solution.py:395
  (110 shorter events, 33.8 us)
Async XLA Ops:
  7.2 140.6 %reduce-scatter.2.cloned.1.call-start = ((), (), s32[]{:S(2)}) async-start(), calls=%async_computation.1 | async-start | bytes 3932160 | tf_op jit(solution)/shard_map/reduce_scatter | solution.py:784
  12.3 8.2 %collective-permute-start.2 = (bf16[128,4224]{1,0:T(8,128)(2,1)}, bf16[128,4224]{1,0:T(8,128)(2,1)}, u32[]{:S(2)}, u32[]{:S(2)}) collective-permute-start(bf16[128,4224]{1,0:T(8,128)(2,1)} %concatenate.16.refs_1_.refs_2_), channel_id=1, source_target_pairs={{0,4},{4,0},{8,12},{12,8},{16,20},{20,16},{24,28},{28,24},{1,5},{5... | collective-permute-start | bytes 3244040 | tf_op jit(solution)/shard_map/ppermute | solution.py:637
  12.3 26.3 %collective-permute-start.1 = (bf16[128,4224]{1,0:T(8,128)(2,1)}, bf16[128,4224]{1,0:T(8,128)(2,1)}, u32[]{:S(2)}, u32[]{:S(2)}) collective-permute-start(bf16[128,4224]{1,0:T(8,128)(2,1)} %concatenate.16.refs_1_.refs_2_), channel_id=1, source_target_pairs={{0,16},{4,12},{8,24},{12,4},{16,0},{20,28},{24,8},{28,20},{1,17},{... | collective-permute-start | bytes 3244040 | tf_op jit(solution)/shard_map/ppermute | solution.py:634
  13.8 25.1 %collective-permute-start = (bf16[128,4224]{1,0:T(8,128)(2,1)}, bf16[128,4224]{1,0:T(8,128)(2,1)}, u32[]{:S(2)}, u32[]{:S(2)}) collective-permute-start(bf16[128,4224]{1,0:T(8,128)(2,1)} %concatenate.16.refs_1_.refs_2_), channel_id=1, source_target_pairs={{0,8},{4,20},{8,0},{12,28},{16,24},{20,4},{24,16},{28,12},{1,9},{5... | collective-permute-start | bytes 3244040 | tf_op jit(solution)/shard_map/ppermute | solution.py:631
  15.3 26.9 %collective-permute-start.3 = (bf16[128,4224]{1,0:T(8,128)(2,1)}, bf16[128,4224]{1,0:T(8,128)(2,1)}, u32[]{:S(2)}, u32[]{:S(2)}) collective-permute-start(bf16[128,4224]{1,0:T(8,128)(2,1)} %concatenate.16.refs_1_.refs_2_), channel_id=1, source_target_pairs={{0,1},{1,0},{2,3},{3,2},{4,5},{5,4},{6,7},{7,6},{8,9},{9,8},{10,11... | collective-permute-start | bytes 3244040 | tf_op jit(solution)/shard_map/ppermute | solution.py:748
  39.5 16.6 %collective-permute-start.6 = (bf16[128,4224]{1,0:T(8,128)(2,1)}, bf16[128,4224]{1,0:T(8,128)(2,1)}, u32[]{:S(2)}, u32[]{:S(2)}) collective-permute-start(bf16[128,4224]{1,0:T(8,128)(2,1)} %collective-permute-done.refs_1_.refs_3_.refs_4_), channel_id=1, source_target_pairs={{0,16},{4,12},{8,24},{12,4},{16,0},{20,28},{24,8},{28,20},{1,17},{... | collective-permute-start | bytes 3244040 | tf_op jit(solution)/shard_map/ppermute | solution.py:634
  56.5 17.5 %collective-permute-start.9 = (bf16[128,4224]{1,0:T(8,128)(2,1)}, bf16[128,4224]{1,0:T(8,128)(2,1)}, u32[]{:S(2)}, u32[]{:S(2)}) collective-permute-start(bf16[128,4224]{1,0:T(8,128)(2,1)} %collective-permute-done.3.refs_1_.refs_10_), channel_id=1, source_target_pairs={{0,8},{4,20},{8,0},{12,28},{16,24},{20,4},{24,16},{28,12},{1,9},{5... | collective-permute-start | bytes 3244040 | tf_op jit(solution)/shard_map/ppermute | solution.py:631
  64.8 10.2 %collective-permute-start.8 = (bf16[768,256]{1,0:T(8,128)(2,1)}, bf16[768,256]{1,0:T(8,128)(2,1)}, u32[]{:S(2)}, u32[]{:S(2)}) collective-permute-start(bf16[768,256]{1,0:T(8,128)(2,1)} %get-tuple-element.80), channel_id=1, source_target_pairs={{0,28},{4,0},{8,4},{12,8},{16,12},{20,16},{24,20},{28,24},{1,29},{... | collective-permute-start | bytes 1179656 | tf_op jit(solution)/shard_map/ppermute | solution.py:773
  84.2 15.5 %collective-permute-start.10 = (bf16[128,4224]{1,0:T(8,128)(2,1)}, bf16[128,4224]{1,0:T(8,128)(2,1)}, u32[]{:S(2)}, u32[]{:S(2)}) collective-permute-start(bf16[128,4224]{1,0:T(8,128)(2,1)} %collective-permute-done.3.refs_1_.refs_10_), channel_id=1, source_target_pairs={{0,16},{4,12},{8,24},{12,4},{16,0},{20,28},{24,8},{28,20},{1,17},{... | collective-permute-start | bytes 3244040 | tf_op jit(solution)/shard_map/ppermute | solution.py:634
  99.7 8.4 %collective-permute-start.12 = (bf16[512,2176]{1,0:T(8,128)(2,1)}, bf16[512,2176]{1,0:T(8,128)(2,1)}, u32[]{:S(2)}, u32[]{:S(2)}) collective-permute-start(bf16[512,2176]{1,0:T(8,128)(2,1)} %get-tuple-element.102), channel_id=1, source_target_pairs={{0,4},{4,0},{8,12},{12,8},{16,20},{20,16},{24,28},{28,24},{1,5},{5... | collective-permute-start | bytes 6684680 | tf_op jit(solution)/shard_map/ppermute | solution.py:637
  100.4 7.3 %collective-permute-start.11 = (bf16[512,2048]{1,0:T(8,128)(2,1)}, bf16[512,2048]{1,0:T(8,128)(2,1)}, u32[]{:S(2)}, u32[]{:S(2)}) collective-permute-start(bf16[512,2048]{1,0:T(8,128)(2,1)} %get-tuple-element.101), channel_id=1, source_target_pairs={{0,4},{4,0},{8,12},{12,8},{16,20},{20,16},{24,28},{28,24},{1,5},{5... | collective-permute-start | bytes 6291464 | tf_op jit(solution)/shard_map/ppermute | solution.py:637
  100.4 19.1 %collective-permute-start.13 = (bf16[128,4224]{1,0:T(8,128)(2,1)}, bf16[128,4224]{1,0:T(8,128)(2,1)}, u32[]{:S(2)}, u32[]{:S(2)}) collective-permute-start(bf16[128,4224]{1,0:T(8,128)(2,1)} %collective-permute-done.9.refs_2_.refs_11_), channel_id=1, source_target_pairs={{0,16},{4,12},{8,24},{12,4},{16,0},{20,28},{24,8},{28,20},{1,17},{... | collective-permute-start | bytes 3244040 | tf_op jit(solution)/shard_map/ppermute | solution.py:634
  101.7 19.1 %collective-permute-start.14 = (bf16[128,4224]{1,0:T(8,128)(2,1)}, bf16[128,4224]{1,0:T(8,128)(2,1)}, u32[]{:S(2)}, u32[]{:S(2)}) collective-permute-start(bf16[128,4224]{1,0:T(8,128)(2,1)} %collective-permute-done.3.refs_1_.refs_10_), channel_id=1, source_target_pairs={{0,4},{4,0},{8,12},{12,8},{16,20},{20,16},{24,28},{28,24},{1,5},{5... | collective-permute-start | bytes 3244040 | tf_op jit(solution)/shard_map/ppermute | solution.py:637
  102.3 21.1 %collective-permute-start.15 = (bf16[128,4224]{1,0:T(8,128)(2,1)}, bf16[128,4224]{1,0:T(8,128)(2,1)}, u32[]{:S(2)}, u32[]{:S(2)}) collective-permute-start(bf16[128,4224]{1,0:T(8,128)(2,1)} %collective-permute-done.9.refs_2_.refs_11_), channel_id=1, source_target_pairs={{0,4},{4,0},{8,12},{12,8},{16,20},{20,16},{24,28},{28,24},{1,5},{5... | collective-permute-start | bytes 3244040 | tf_op jit(solution)/shard_map/ppermute | solution.py:637
  107.7 17.0 %collective-permute-start.16 = (bf16[128,4224]{1,0:T(8,128)(2,1)}, bf16[128,4224]{1,0:T(8,128)(2,1)}, u32[]{:S(2)}, u32[]{:S(2)}) collective-permute-start(bf16[128,4224]{1,0:T(8,128)(2,1)} %collective-permute-done.10.refs_3_.refs_12_), channel_id=1, source_target_pairs={{0,4},{4,0},{8,12},{12,8},{16,20},{20,16},{24,28},{28,24},{1,5},{5... | collective-permute-start | bytes 3244040 | tf_op jit(solution)/shard_map/ppermute | solution.py:637
  119.4 6.1 %collective-permute-start.17 = (bf16[128,4224]{1,0:T(8,128)(2,1)}, bf16[128,4224]{1,0:T(8,128)(2,1)}, u32[]{:S(2)}, u32[]{:S(2)}) collective-permute-start(bf16[128,4224]{1,0:T(8,128)(2,1)} %collective-permute-done.13.refs_4_.refs_13_), channel_id=1, source_target_pairs={{0,4},{4,0},{8,12},{12,8},{16,20},{20,16},{24,28},{28,24},{1,5},{5... | collective-permute-start | bytes 3244040 | tf_op jit(solution)/shard_map/ppermute | solution.py:637
  119.6 16.6 %collective-permute-start.19 = (bf16[128,2176]{1,0:T(8,128)(2,1)}, bf16[128,2176]{1,0:T(8,128)(2,1)}, u32[]{:S(2)}, u32[]{:S(2)}) collective-permute-start(bf16[128,2176]{1,0:T(8,128)(2,1)} %get-tuple-element.111), channel_id=1, source_target_pairs={{0,16},{4,12},{8,24},{12,4},{16,0},{20,28},{24,8},{28,20},{1,17},{... | collective-permute-start | bytes 1671176 | tf_op jit(solution)/shard_map/ppermute | solution.py:634
  120.9 15.4 %collective-permute-start.18 = (bf16[128,2048]{1,0:T(8,128)(2,1)}, bf16[128,2048]{1,0:T(8,128)(2,1)}, u32[]{:S(2)}, u32[]{:S(2)}) collective-permute-start(bf16[128,2048]{1,0:T(8,128)(2,1)} %get-tuple-element.110), channel_id=1, source_target_pairs={{0,16},{4,12},{8,24},{12,4},{16,0},{20,28},{24,8},{28,20},{1,17},{... | collective-permute-start | bytes 1572872 | tf_op jit(solution)/shard_map/ppermute | solution.py:634
  123.5 32.4 %collective-permute-start.23 = (bf16[128,2048]{1,0:T(8,128)(2,1)}, bf16[128,2048]{1,0:T(8,128)(2,1)}, u32[]{:S(2)}, u32[]{:S(2)}) collective-permute-start(bf16[128,2048]{1,0:T(8,128)(2,1)} %get-tuple-element.122), channel_id=1, source_target_pairs={{0,16},{4,12},{8,24},{12,4},{16,0},{20,28},{24,8},{28,20},{1,17},{... | collective-permute-start | bytes 1572872 | tf_op jit(solution)/shard_map/ppermute | solution.py:634
  124.7 31.2 %collective-permute-start.24 = (bf16[128,2176]{1,0:T(8,128)(2,1)}, bf16[128,2176]{1,0:T(8,128)(2,1)}, u32[]{:S(2)}, u32[]{:S(2)}) collective-permute-start(bf16[128,2176]{1,0:T(8,128)(2,1)} %get-tuple-element.123), channel_id=1, source_target_pairs={{0,16},{4,12},{8,24},{12,4},{16,0},{20,28},{24,8},{28,20},{1,17},{... | collective-permute-start | bytes 1671176 | tf_op jit(solution)/shard_map/ppermute | solution.py:634
  145.1 19.3 %collective-permute-start.21 = (bf16[2,384,512]{2,1,0:T(8,128)(2,1)}, bf16[2,384,512]{2,1,0:T(8,128)(2,1)S(1)}, u32[]{:S(2)}, u32[]{:S(2)}) collective-permute-start(bf16[2,384,512]{2,1,0:T(8,128)(2,1)} %get-tuple-element.118), channel_id=1, source_target_pairs={{0,1},{1,3},{2,0},{3,2},{4,5},{5,7},{6,4},{7,6},{8,9},{9,11},{10,8... | collective-permute-start | bytes 2359304 | tf_op jit(solution)/shard_map/ppermute | solution.py:819
  152.5 11.8 %collective-permute-start.22 = (bf16[128,2048]{1,0:T(8,128)(2,1)S(1)}, bf16[128,2048]{1,0:T(8,128)(2,1)S(1)}, u32[]{:S(2)}, u32[]{:S(2)}) collective-permute-start(bf16[128,2048]{1,0:T(8,128)(2,1)S(1)} %add_convert_fusion.2), channel_id=1, source_target_pairs={{0,8},{4,20},{8,0},{12,28},{16,24},{20,4},{24,16},{28,12},{1,9},{5... | collective-permute-start | bytes 1572872 | tf_op jit(solution)/shard_map/ppermute | solution.py:631
  155.5 14.2 %collective-permute-start.20 = (bf16[128,2176]{1,0:T(8,128)(2,1)S(1)}, bf16[128,2176]{1,0:T(8,128)(2,1)S(1)}, u32[]{:S(2)}, u32[]{:S(2)}) collective-permute-start(bf16[128,2176]{1,0:T(8,128)(2,1)S(1)} %add_convert_fusion), channel_id=1, source_target_pairs={{0,8},{4,20},{8,0},{12,28},{16,24},{20,4},{24,16},{28,12},{1,9},{5... | collective-permute-start | bytes 1671176 | tf_op jit(solution)/shard_map/ppermute | solution.py:631
  164.3 19.7 %collective-permute-start.25 = (bf16[2,384,512]{2,1,0:T(8,128)(2,1)S(1)}, bf16[2,384,512]{2,1,0:T(8,128)(2,1)S(1)}, u32[]{:S(2)}, u32[]{:S(2)}) collective-permute-start(bf16[2,384,512]{2,1,0:T(8,128)(2,1)S(1)} %copy-done.1), channel_id=1, source_target_pairs={{1,2},{2,1},{5,6},{6,5},{9,10},{10,9},{13,14},{14,13},{17,18},{18,... | collective-permute-start | bytes 2359304 | tf_op jit(solution)/shard_map/ppermute | solution.py:831
  (15 other events, 91.1 us)
Sparse Core Ops, SparseCore 0:
  84.3 61.3 reduce-scatter.1
